TPU v7x, 768 devices: a whole 4x8x12 slice. The times are simulated.
768 devices in a mesh: blk: 48 (over y_lo, z, core), grp: 16 (over x, y_hi).
Axes of the slice: x: 4, y: 8 (y_hi: 4, y_lo: 2; y = y_hi * 2 + y_lo), z: 12, core: 2. Of those that a mesh axis runs over, the one named last changes fastest.
Arguments:
- images: bfloat16 [16, 12288, 1152], P('grp', 'blk'), may hold values from -1 to 1
- texts: bfloat16 [16, 12288, 1152], P('grp', 'blk'), may hold values from -1 to 1
- labels: int32 [16, 48, 256], P('grp', 'blk'), may hold values from 0 to 255, each once within a row
- partners: int32 [2, 48], replicated, may hold values from 0 to 47, as said below
- logit_scale: float32 [], replicated, may hold values from 1 to 3
- logit_bias: float32 [], replicated, may hold values from -3 to -1
Outputs:
- image_grad: float32 [16, 12288, 1152], P('grp', 'blk')
- text_grad: float32 [16, 12288, 1152], P('grp', 'blk')
- loss: float32 [], replicated
Inputs may be any that keep to these rules, and one draw needn't show every extreme that they name: Each block's labels are a permutation of its 256 text rows. partners[r, i] is block i's partner in round r: partners[r, partners[r, i]] == i and partners[r, i] != i; no two rounds pair the same two blocks.
All inputs are finite; a program needn't handle non-finite values.
Results may differ from a plain program's by a relative error of at most 0.00035.
The roundings to bfloat16 on the way count: a program that leaves them out, or rounds other values in their place, can miss the bound.
Values may be sent and summed in bfloat16 or wider, within the bound.
No kernel may reach another device: no remote copies, remote signals or barrier semaphores. Data moves between devices by JAX's collectives and lax.ppermute only.
A program may use at most 32 MiB of HBM per device.

v0:
```python
import functools

import jax
import jax.numpy as jnp
from jax import lax
from jax.sharding import Mesh
from jax.sharding import PartitionSpec as P

BLK = ("blk_0", "blk_1", "blk_2")
BLK_GRP = ("blk_0", "blk_1", "blk_2", "grp_0", "grp_1")
GRP = ("grp_0", "grp_1")


def sent_together(arrays, axis, split_dim, concat_dim, along):
    ends, at = ([], 0)
    for a in arrays[:-1]:
        at += a.shape[along]
        ends.append(at)
    both = jnp.concatenate(arrays, axis=along)
    return tuple(
        jnp.split(
            lax.all_to_all(both, axis, split_axis=split_dim, concat_axis=concat_dim, tiled=True),
            ends,
            axis=along,
        )
    )


def one_axis_at_a_time(x, axes):
    return functools.reduce(lax.psum, axes, x)


def block_weights(image_rows, text_rows, positive, logit_scale, logit_bias):
    logits = (
        logit_scale * jnp.dot(image_rows, text_rows.T, preferred_element_type=jnp.float32)
        + logit_bias
    )
    signed = jnp.where(positive, jnp.float32(1.0), jnp.float32(-1.0))
    loss_sum = jnp.sum(jax.nn.softplus(-signed * logits))
    weight = (-signed * jax.nn.sigmoid(-signed * logits)).astype(jnp.bfloat16)
    return (loss_sum, weight)


def regroup(received, partner_row):
    row_count, width = received.shape
    devices = partner_row.shape[0]
    pieces = received.reshape(row_count, devices, width // devices)
    pieces = jnp.take(pieces, partner_row, axis=1)
    return pieces.reshape(row_count, width)


def body(images, texts, labels, partners, logit_scale, logit_bias):
    own_images = images[0]
    own_texts = texts[0]
    row_count = own_images.shape[0]
    columns = jnp.arange(row_count, dtype=jnp.int32)
    positive = labels[0, 0][:, None] == columns[None, :]
    nothing = jnp.zeros((row_count, row_count), dtype=bool)
    loss_sum, weight = block_weights(own_images, own_texts, positive, logit_scale, logit_bias)
    image_grad = logit_scale * jnp.dot(weight, own_texts, preferred_element_type=jnp.float32)
    text_grad = logit_scale * jnp.dot(weight.T, own_images, preferred_element_type=jnp.float32)
    for round_index in range(partners.shape[0]):
        partner_row = partners[round_index]
        spread_images, spread_texts = sent_together((own_images, own_texts), BLK, 1, 1, 0)
        their_images, their_texts = sent_together(
            (regroup(spread_images, partner_row), regroup(spread_texts, partner_row)), BLK, 1, 1, 0
        )
        round_loss, weight = block_weights(
            own_images, their_texts, nothing, logit_scale, logit_bias
        )
        image_grad = image_grad + logit_scale * jnp.dot(
            weight, their_texts, preferred_element_type=jnp.float32
        )
        mirror_loss, mirror = block_weights(
            their_images, own_texts, nothing, logit_scale, logit_bias
        )
        text_grad = text_grad + logit_scale * jnp.dot(
            mirror.T, their_images, preferred_element_type=jnp.float32
        )
        loss_sum = loss_sum + round_loss
    loss_all = one_axis_at_a_time(loss_sum, BLK_GRP)
    image_count = lax.axis_size(BLK) * lax.axis_size(GRP) * row_count
    loss = loss_all / jnp.float32(image_count)
    return (image_grad[None], text_grad[None], loss)


def solution(mesh):
    split = Mesh(
        mesh.devices.reshape(2, 12, 2, 4, 4), ("blk_0", "blk_1", "blk_2", "grp_0", "grp_1")
    )
    in_specs = (P(GRP, BLK, None), P(GRP, BLK, None), P(GRP, BLK, None), P(), P(), P())
    out_specs = (P(GRP, BLK, None), P(GRP, BLK, None), P())
    return jax.shard_map(body, mesh=split, in_specs=in_specs, out_specs=out_specs, check_vma=False)
```

profile of v0, /device:TPU:6, one launch (start us, length us, event | category | flops | bytes accessed | tf_op | source)
XLA Modules:
  0.0 240.6 jit_solution(11514482315510521492)
XLA Ops:
  0.6 1.4 copy.13
  2.3 1.1 pad_maximum_fusion
  3.4 17.0 %all-to-all-start = ((bf16[512,48,24]{0,2,1:T(8,128)(2,1)}), bf16[512,48,24]{0,2,1:T(8,128)(2,1)S(1)}, u32[]{:S(2)}, u32[]{:S(2)}) async-start(bf16[512,48,24]{0,2,1:T(8,128)(2,1)} %pad_maximum_fusion), calls=%async_computation | async-start | bytes 2359296 | tf_op jit(solution)/shard_map/all_to_all | solution.py:22
  20.4 41.1 %all-to-all-done = bf16[512,48,24]{0,2,1:T(8,128)(2,1)S(1)} async-done(((bf16[512,48,24]{0,2,1:T(8,128)(2,1)}), bf16[512,48,24]{0,2,1:T(8,128)(2,1)S(1)}, u32[]{:S(2)}, u32[]{:S(2)}) %all-to-all-start) | async-done | bytes 1179680 | tf_op jit(solution)/shard_map/all_to_all | solution.py:22
  65.2 1.1 pad_maximum_fusion.2
  66.3 9.3 %all-to-all-start.2 = ((bf16[512,48,24]{0,2,1:T(8,128)(2,1)}), bf16[512,48,24]{0,2,1:T(8,128)(2,1)S(1)}, u32[]{:S(2)}, u32[]{:S(2)}) async-start(bf16[512,48,24]{0,2,1:T(8,128)(2,1)} %pad_maximum_fusion.2), calls=%async_computation.2 | async-start | bytes 2359296 | tf_op jit(solution)/shard_map/all_to_all | solution.py:22
  75.6 1.1 pad_maximum_fusion.1
  76.7 40.0 %all-to-all-done.2 = bf16[512,48,24]{0,2,1:T(8,128)(2,1)S(1)} async-done(((bf16[512,48,24]{0,2,1:T(8,128)(2,1)}), bf16[512,48,24]{0,2,1:T(8,128)(2,1)S(1)}, u32[]{:S(2)}, u32[]{:S(2)}) %all-to-all-start.2) | async-done | bytes 1179680 | tf_op jit(solution)/shard_map/all_to_all | solution.py:22
  116.8 9.4 %all-to-all-start.1 = ((bf16[512,48,24]{0,2,1:T(8,128)(2,1)}), bf16[512,48,24]{0,2,1:T(8,128)(2,1)}, u32[]{:S(2)}, u32[]{:S(2)}) async-start(bf16[512,48,24]{0,2,1:T(8,128)(2,1)} %pad_maximum_fusion.1), calls=%async_computation.1 | async-start | bytes 2359296 | tf_op jit(solution)/shard_map/all_to_all | solution.py:22
  127.5 1.8 fusion.33
  130.7 36.6 %all-to-all-done.1 = bf16[512,48,24]{0,2,1:T(8,128)(2,1)} async-done(((bf16[512,48,24]{0,2,1:T(8,128)(2,1)}), bf16[512,48,24]{0,2,1:T(8,128)(2,1)}, u32[]{:S(2)}, u32[]{:S(2)}) %all-to-all-start.1) | async-done | bytes 1179680 | tf_op jit(solution)/shard_map/all_to_all | solution.py:22
  167.2 1.3 fusion.58
  168.6 1.8 fusion.34
  172.3 5.5 %psum.35 = f32[]{:T(128)} all-reduce(f32[]{:T(128)S(6)} %add.108), channel_id=1, replica_groups=mesh['blk_0'=2,'blk_1'=12,'blk_2'=2,'grp_0'=4,'grp_1'=4] {'blk_0'}, use_global_device_ids=true, to_apply=%region_3.5 | all-reduce | flops 1 | bytes 8 | tf_op jit(solution)/shard_map/psum | solution.py:30
  177.7 26.2 %psum.36 = f32[]{:T(128)} all-reduce(f32[]{:T(128)} %psum.35), channel_id=1, replica_groups=mesh['blk_0'=2,'blk_1'=12,'blk_2'=2,'grp_0'=4,'grp_1'=4] {'blk_1'}, use_global_device_ids=true, to_apply=%region_4.6 | all-reduce | flops 1 | bytes 8 | tf_op jit(solution)/shard_map/psum | solution.py:30
  203.9 3.1 %psum.37 = f32[]{:T(128)} all-reduce(f32[]{:T(128)} %psum.36), channel_id=1, replica_groups=mesh['blk_0'=2,'blk_1'=12,'blk_2'=2,'grp_0'=4,'grp_1'=4] {'blk_2'}, use_global_device_ids=true, to_apply=%region_5.7 | all-reduce | flops 1 | bytes 8 | tf_op jit(solution)/shard_map/psum | solution.py:30
  207.0 2.4 %fusion.28 = f32[256,1152]{1,0:T(8,128)} fusion(bf16[1,256,1152]{2,1,0:T(8,128)(2,1)S(1)} %copy-done.3, f32[256,256]{1,0:T(8,128)} %get-tuple-element.21, s32[256]{0:T(256)S(1)} %bitcast.96), kind=kOutput, calls=%fused_computation.45 | convolution fusion | flops 151519232 | bytes 2032640 | tf_op jit(solution)/shard_map/dot_general | solution.py:61
  209.4 8.1 %psum.38 = f32[]{:T(128)} all-reduce(f32[]{:T(128)} %psum.37), channel_id=1, replica_groups=mesh['blk_0'=2,'blk_1'=12,'blk_2'=2,'grp_0'=4,'grp_1'=4] {'grp_0'}, use_global_device_ids=true, to_apply=%region_6.8 | all-reduce | flops 1 | bytes 8 | tf_op jit(solution)/shard_map/psum | solution.py:30
  217.5 1.3 fusion.25
  218.9 12.6 %psum.39 = f32[]{:T(128)} all-reduce(f32[]{:T(128)} %psum.38), channel_id=1, replica_groups=mesh['blk_0'=2,'blk_1'=12,'blk_2'=2,'grp_0'=4,'grp_1'=4] {'grp_1'}, use_global_device_ids=true, to_apply=%region_7.9 | all-reduce | flops 1 | bytes 8 | tf_op jit(solution)/shard_map/psum | solution.py:30
  231.5 1.6 convolution_add_fusion.3
  233.1 1.4 fusion.3
  235.2 2.3 convolution_add_fusion.1
  237.5 2.0 fusion.2
  (32 shorter events, 5.3 us)
Async XLA Ops:
  0.6 1.4 copy-start
  3.4 17.0 %copy-start.8 = (s32[2,48]{1,0:T(2,128)S(1)}, s32[2,48]{1,0:T(2,128)}, u32[]{:S(2)}) copy-start(s32[2,48]{1,0:T(2,128)} %param.11) | copy-start | bytes 1156
  3.4 58.1 %all-to-all-start = ((bf16[512,48,24]{0,2,1:T(8,128)(2,1)}), bf16[512,48,24]{0,2,1:T(8,128)(2,1)S(1)}, u32[]{:S(2)}, u32[]{:S(2)}) async-start(bf16[512,48,24]{0,2,1:T(8,128)(2,1)} %pad_maximum_fusion), calls=%async_computation | async-start | bytes 2359296 | tf_op jit(solution)/shard_map/all_to_all | solution.py:22
  66.3 9.3 %copy-start.1 = (bf16[256,48,24]{0,2,1:T(8,128)(2,1)S(1)}, bf16[256,48,24]{0,2,1:T(8,128)(2,1)}, u32[]{:S(2)}) copy-start(bf16[256,48,24]{0,2,1:T(8,128)(2,1)} %get-tuple-element.25) | copy-start | bytes 1769476
  66.3 50.5 %all-to-all-start.2 = ((bf16[512,48,24]{0,2,1:T(8,128)(2,1)}), bf16[512,48,24]{0,2,1:T(8,128)(2,1)S(1)}, u32[]{:S(2)}, u32[]{:S(2)}) async-start(bf16[512,48,24]{0,2,1:T(8,128)(2,1)} %pad_maximum_fusion.2), calls=%async_computation.2 | async-start | bytes 2359296 | tf_op jit(solution)/shard_map/all_to_all | solution.py:22
  76.7 50.7 %copy-start.2 = (bf16[1,256,1152]{2,1,0:T(8,128)(2,1)S(1)}, bf16[1,256,1152]{2,1,0:T(8,128)(2,1)}, u32[]{:S(2)}) copy-start(bf16[1,256,1152]{2,1,0:T(8,128)(2,1)} %param.8) | copy-start | bytes 1769476
  76.7 50.7 %copy-start.7 = (s32[1,1,256]{2,1,0:T(1,128)S(1)}, s32[1,1,256]{2,1,0:T(1,128)}, u32[]{:S(2)}) copy-start(s32[1,1,256]{2,1,0:T(1,128)} %param.10) | copy-start | bytes 3076
  116.8 50.5 %all-to-all-start.1 = ((bf16[512,48,24]{0,2,1:T(8,128)(2,1)}), bf16[512,48,24]{0,2,1:T(8,128)(2,1)}, u32[]{:S(2)}, u32[]{:S(2)}) async-start(bf16[512,48,24]{0,2,1:T(8,128)(2,1)} %pad_maximum_fusion.1), calls=%async_computation.1 | async-start | bytes 2359296 | tf_op jit(solution)/shard_map/all_to_all | solution.py:22
  129.9 0.8 copy-start.5
  130.7 37.9 %copy-start.3 = (bf16[1,256,1152]{2,1,0:T(8,128)(2,1)S(1)}, bf16[1,256,1152]{2,1,0:T(8,128)(2,1)}, u32[]{:S(2)}) copy-start(bf16[1,256,1152]{2,1,0:T(8,128)(2,1)} %param.8) | copy-start | bytes 1769476
  168.6 40.9 %copy-start.4 = (bf16[256,48,24]{0,2,1:T(8,128)(2,1)}, bf16[256,48,24]{0,2,1:T(8,128)(2,1)S(1)}, u32[]{:S(2)}) copy-start(bf16[256,48,24]{0,2,1:T(8,128)(2,1)S(1)} %get-tuple-element.11) | copy-start | bytes 1769476
  231.5 1.6 copy-start.6
where the time goes:
time: 243 us; the launch traced here: 241 us
  waiting for transfers between devices  118 us (49%)
  blocking collectives  55.5 us (23%)
  starting transfers between devices  35.7 us (15%)
  matrix products  15 us (6%)
  between operations  5.85 us (2%)
  local copies, waits for them, and re-layouts  5.68 us (2%)
  other arithmetic  5.22 us (2%)
    all_to_all x3, waiting for transfers between devices, sent_together(): lax.all_to_all(both, axis, split_axis=split_dim, concat_axis=concat_dim,...  118 us
    psum x5, blocking collectives, one_axis_at_a_time(): return functools.reduce(lax.psum, axes, x)  55.5 us
    all_to_all x3, starting transfers between devices, sent_together(): lax.all_to_all(both, axis, split_axis=split_dim, concat_axis=concat_dim,...  35.7 us
  transfers between devices with their start and end apart: 3, of which 3 were waited for; matrix products, arithmetic and copies ran while one was open for 2% of the time, Pallas kernels for 0%

commit v1 on v0

v1 whole, which is shorter than its diff:
```python
import functools

import jax
import jax.numpy as jnp
from jax import lax
from jax.experimental import pallas as pl
from jax.experimental.pallas import tpu as pltpu
from jax.sharding import Mesh
from jax.sharding import PartitionSpec as P

BLK = ("blk_0", "blk_1", "blk_2")
BLK_GRP = ("blk_0", "blk_1", "blk_2", "grp_0", "grp_1")
GRP = ("grp_0", "grp_1")

PIECE_ROWS = 16
PIECE_COLS = 384
VMEM = pl.BlockSpec(memory_space=pltpu.VMEM)
SMEM = pl.BlockSpec(memory_space=pltpu.SMEM)


def local_kernel(kernel, out_shape, in_specs, out_specs, scratch=(), flops=0, moved=0, exps=0):
    return pl.pallas_call(
        kernel,
        out_shape=out_shape,
        in_specs=in_specs,
        out_specs=out_specs,
        scratch_shapes=list(scratch),
        compiler_params=pltpu.CompilerParams(vmem_limit_bytes=24 << 20),
        cost_estimate=pl.CostEstimate(flops=flops, bytes_accessed=moved, transcendentals=exps),
    )


def piece_at(index, columns):
    row, col = divmod(index, columns // PIECE_COLS)
    return pl.ds(row * PIECE_ROWS, PIECE_ROWS), pl.ds(col * PIECE_COLS, PIECE_COLS)


def pack_kernel(texts, images, packed):
    for index in range(packed.shape[0]):
        rows, cols = piece_at(index, texts.shape[1])
        packed[index, 0] = texts[rows, cols]
        packed[index, 1] = images[rows, cols]


def regroup_kernel(which, partners, spread, send):
    rounds, blocks = partners.shape
    for block in range(blocks):
        for r in range(rounds):
            send[block, r] = spread[partners[r, block], which]


def unpack(received, whole):
    for index in range(received.shape[0]):
        rows, cols = piece_at(index, whole.shape[2])
        for r in range(received.shape[1]):
            whole[r, rows, cols] = received[index, r]


def dot_nt(a, b):
    return lax.dot_general(a, b, (((1,), (1,)), ((), ())), preferred_element_type=jnp.float32)


def dot_tn(a, b):
    return lax.dot_general(a, b, (((0,), (0,)), ((), ())), preferred_element_type=jnp.float32)


def dot_nn(a, b):
    return jnp.dot(a, b, preferred_element_type=jnp.float32)


def sigmoid_parts(x):
    e = jnp.exp(-jnp.abs(x))
    s = 1.0 / (1.0 + e)
    return e, jnp.where(x >= 0, s, e * s)


def own_kernel(scale, bias, images, texts, labels, loss, image_grad, text_grad):
    x, y = images[...], texts[...]
    logits = scale[0, 0] * dot_nt(x, y) + bias[0, 0]
    match = lax.broadcasted_iota(jnp.int32, logits.shape, 1) == labels[...]
    signed = jnp.where(match, -logits, logits)
    e, s = sigmoid_parts(signed)
    loss[0, 0] = jnp.sum(jnp.maximum(signed, 0.0) + jnp.log1p(e))
    weight = jnp.where(match, -s, s).astype(jnp.bfloat16)
    image_grad[...] = scale[0, 0] * dot_nn(weight, y)
    text_grad[...] = scale[0, 0] * dot_tn(weight, x)


def text_kernel(scale, bias, own_loss, images, received, image_part, loss, image_grad, whole):
    unpack(received, whole)
    x = images[...]
    total = own_loss[0, 0]
    grad = image_part[...]
    for r in range(whole.shape[0]):
        logits = scale[0, 0] * dot_nt(x, whole[r]) + bias[0, 0]
        e, s = sigmoid_parts(logits)
        total += jnp.sum(jnp.maximum(logits, 0.0) + jnp.log1p(e))
        grad += scale[0, 0] * dot_nn(s.astype(jnp.bfloat16), whole[r])
    loss[0, 0] = total
    image_grad[...] = grad


def image_kernel(count, scale, bias, loss_sum, texts, received, text_part, loss, text_grad, whole):
    unpack(received, whole)
    y = texts[...]
    grad = text_part[...]
    for r in range(whole.shape[0]):
        logits = scale[0, 0] * dot_nt(y, whole[r]) + bias[0, 0]
        _, s = sigmoid_parts(logits)
        grad += scale[0, 0] * dot_nn(s.astype(jnp.bfloat16), whole[r])
    text_grad[...] = grad
    loss[0, 0] = loss_sum[0, 0] / count


def body(images, texts, labels, partners, logit_scale, logit_bias):
    x, y = images[0], texts[0]
    rows, width = x.shape
    rounds, blocks = partners.shape
    scale, bias = logit_scale.reshape(1, 1), logit_bias.reshape(1, 1)
    piece = (PIECE_ROWS, PIECE_COLS)
    one = jax.ShapeDtypeStruct((1, 1), jnp.float32)
    grad = jax.ShapeDtypeStruct((rows, width), jnp.float32)
    whole = pltpu.VMEM((rounds, rows, width), x.dtype)
    mac = 2 * rows * rows * width
    nbytes = rows * width * 2
    exchange = functools.partial(
        lax.all_to_all, axis_name=BLK, split_axis=0, concat_axis=0, tiled=True
    )

    packed = local_kernel(
        pack_kernel,
        jax.ShapeDtypeStruct((blocks, 2, *piece), x.dtype),
        [VMEM, VMEM],
        VMEM,
        moved=4 * nbytes,
    )(y, x)
    spread = exchange(packed)

    def regroup(which):
        return local_kernel(
            functools.partial(regroup_kernel, which),
            jax.ShapeDtypeStruct((blocks, rounds, *piece), x.dtype),
            [SMEM, VMEM],
            VMEM,
            moved=4 * nbytes,
        )(partners, spread)

    own_loss, image_part, text_part = local_kernel(
        own_kernel,
        (one, grad, grad),
        [SMEM, SMEM, VMEM, VMEM, VMEM],
        (SMEM, VMEM, VMEM),
        flops=3 * mac,
        moved=6 * nbytes,
        exps=3 * rows * rows,
    )(scale, bias, x, y, labels[0].reshape(rows, 1))

    their_texts = exchange(regroup(0))
    send_images, own_loss, image_part, text_part = lax.optimization_barrier(
        (regroup(1), own_loss, image_part, text_part)
    )
    their_images = exchange(send_images)

    loss_part, image_grad = local_kernel(
        text_kernel,
        (one, grad),
        [SMEM, SMEM, SMEM, VMEM, VMEM, VMEM],
        (SMEM, VMEM),
        [whole],
        flops=2 * rounds * mac,
        moved=7 * nbytes,
        exps=3 * rounds * rows * rows,
    )(scale, bias, own_loss, x, their_texts, image_part)
    loss_sum = functools.reduce(lax.psum, BLK_GRP, loss_part)
    count = lax.axis_size(BLK) * lax.axis_size(GRP) * rows
    loss, text_grad = local_kernel(
        functools.partial(image_kernel, float(count)),
        (one, grad),
        [SMEM, SMEM, SMEM, VMEM, VMEM, VMEM],
        (SMEM, VMEM),
        [whole],
        flops=2 * rounds * mac,
        moved=7 * nbytes,
        exps=2 * rounds * rows * rows,
    )(scale, bias, loss_sum, y, their_images, text_part)
    return image_grad[None], text_grad[None], loss[0, 0]


def solution(mesh):
    split = Mesh(
        mesh.devices.reshape(2, 12, 2, 4, 4), ("blk_0", "blk_1", "blk_2", "grp_0", "grp_1")
    )
    in_specs = (P(GRP, BLK, None), P(GRP, BLK, None), P(GRP, BLK, None), P(), P(), P())
    out_specs = (P(GRP, BLK, None), P(GRP, BLK, None), P())
    return jax.shard_map(body, mesh=split, in_specs=in_specs, out_specs=out_specs, check_vma=False)
```

time: 243 us -> 213 us (0.88)
  waiting for transfers between devices: 118 us -> 33 us
  blocking collectives: 55.5 us -> 135 us
  starting transfers between devices: 35.7 us -> 18.5 us
  matrix products: 15 us -> 0 us
  Pallas kernels: 0 us -> 11.8 us
  other arithmetic: 5.22 us -> 0 us
  between operations: 5.85 us -> 2.01 us
  local copies, waits for them, and re-layouts: 5.68 us -> 8.4 us
    all_to_all x3 -> x2, waiting for transfers between devices: 118 us -> 33 us  [the longest x1 33 us: body(): their_texts = exchange(regroup(0))]
    all_to_all x0 -> x1, blocking collectives: none -> 57.8 us  [body(): spread = exchange(packed)]
    psum x5, blocking collectives: 55.5 us -> 77.3 us  [body(): loss_sum = functools.reduce(lax.psum, BLK_GRP, loss_part)]
    all_to_all x3 -> x2, starting transfers between devices: 35.7 us -> 18.5 us  [the longest x1 9.33 us: body(): their_texts = exchange(regroup(0))]
    dot_general x9 -> x0, matrix products: 15 us -> none  [the longest x2 4.35 us: body(): jnp.dot(mirror.T, their_images, preferred_element_type=jnp.float32)]
    pallas_call x0 -> x6, Pallas kernels: none -> 11.8 us  [the longest x1 3.56 us: body(): local_kernel(text_kernel, (one, grad), [SMEM, SMEM, SMEM, VMEM, VMEM, VME...]
    unnamed x20 -> x22, local copies, waits for them, and re-layouts: 1.65 us -> 7.6 us
    concatenate x3 -> x0, other arithmetic: 3.32 us -> none  [sent_together(): both = jnp.concatenate(arrays, axis=along)]
  transfers between devices with their start and end apart: 3 -> 2, of which waited for: 3 -> 1; matrix products, arithmetic and copies ran while one was open for 2% -> 0% of each run, Pallas kernels for 0% -> 3%
where the time goes in v1:
time: 213 us; the launch traced here: 209 us
  blocking collectives  135 us (63%)
  waiting for transfers between devices  33 us (15%)
  starting transfers between devices  18.5 us (9%)
  Pallas kernels  11.8 us (6%)
  local copies, waits for them, and re-layouts  8.4 us (4%)
    psum x5, blocking collectives, body(): loss_sum = functools.reduce(lax.psum, BLK_GRP, loss_part)  77.3 us
    all_to_all x1, blocking collectives, body(): spread = exchange(packed)  57.8 us
    all_to_all x1, waiting for transfers between devices, body(): their_texts = exchange(regroup(0))  33 us
    all_to_all x1, starting transfers between devices, body(): their_texts = exchange(regroup(0))  9.33 us
    all_to_all x1, starting transfers between devices, body(): their_images = exchange(send_images)  9.2 us
    unnamed x22, local copies, waits for them, and re-layouts  7.6 us
  transfers between devices with their start and end apart: 2, of which 1 were waited for; matrix products, arithmetic and copies ran while one was open for 0% of the time, Pallas kernels for 3%

profile of v1, /device:TPU:6, one launch (start us, length us, event | category | flops | bytes accessed | tf_op | source)
XLA Modules:
  0.0 208.9 jit_solution(15001653704331880591)
XLA Ops:
  0.6 0.0 copy-start
  0.6 1.1 copy-done
  1.7 1.1 copy-done.2
  2.8 0.1 shard_map.85
  2.9 57.8 %all_to_all.15.spread = bf16[48,2,16,384]{3,2,1,0:T(8,128)(2,1)S(1)} all-to-all(bf16[48,2,16,384]{3,2,1,0:T(8,128)(2,1)S(1)} %shard_map.85), channel_id=1, replica_groups=mesh['blk_0'=2,'blk_1'=12,'blk_2'=2,'grp_0'=4,'grp_1'=4] {'blk_0','blk_1..., dimensions={0} | all-to-all | bytes 2359296 | tf_op jit(solution)/shard_map/all_to_all | solution.py:137
  60.7 1.7 shard_map.88
  62.4 9.3 %all-to-all-start.1 = ((bf16[48,2,16,384]{3,2,1,0:T(8,128)(2,1)}), bf16[48,2,16,384]{3,2,1,0:T(8,128)(2,1)S(1)}, u32[]{:S(2)}, u32[]{:S(2)}) async-start(bf16[48,2,16,384]{3,2,1,0:T(8,128)(2,1)} %shard_map.88), calls=%async_computation.1 | async-start | bytes 2359296 | tf_op jit(solution)/shard_map/all_to_all | solution.py:158
  73.0 0.8 copy.9.labels
  73.9 0.9 copy-done.8
  74.8 1.4 shard_map.87
  76.1 1.0 copy-done.4
  77.1 1.0 copy-done.6
  78.1 1.7 shard_map.86
  79.9 33.0 %all-to-all-done.1.received = bf16[48,2,16,384]{3,2,1,0:T(8,128)(2,1)S(1)} async-done(((bf16[48,2,16,384]{3,2,1,0:T(8,128)(2,1)}), bf16[48,2,16,384]{3,2,1,0:T(8,128)(2,1)S(1)}, u32[]{:S(2)}, u32[]{:S(2)}) %all-to-all-start.1) | async-done | bytes 1179680 | tf_op jit(solution)/shard_map/all_to_all | solution.py:158
  112.9 9.2 %all-to-all-start.2 = ((bf16[48,2,16,384]{3,2,1,0:T(8,128)(2,1)}), bf16[48,2,16,384]{3,2,1,0:T(8,128)(2,1)S(1)}, u32[]{:S(2)}, u32[]{:S(2)}) async-start(bf16[48,2,16,384]{3,2,1,0:T(8,128)(2,1)} %shard_map.86), calls=%async_computation.2 | async-start | bytes 2359296 | tf_op jit(solution)/shard_map/all_to_all | solution.py:162
  122.1 1.3 copy-done.7
  123.4 3.6 %shard_map.89 = (f32[1,1]{1,0:T(1,128)}, f32[256,1152]{1,0:T(8,128)}) custom-call(f32[1,1]{1,0:T(1,128)} %bitcast.9.scale, f32[1,1]{1,0:T(1,128)} %bitcast.12.bias, f32[1,1]{1,0:T(1,128)} %get-tuple-element.17.own_loss, bf16[256,1152]{1,0:T(8,128)(2,1)S(1)} %bitcast.16, bf16[48,2,16,384]{3,2,1,0:T(8,128)(2,1)S(1)} %all-to-all-done.1.received, ...), custom_call_target="tpu_custom_call" | custom-call | flops 603979776 | bytes 4128768 | tf_op jit(solution)/shard_map/pallas_call | solution.py:164
  127.0 5.6 %psum.35 = f32[1,1]{1,0:T(1,128)} all-reduce(f32[1,1]{1,0:T(1,128)} %get-tuple-element.20), channel_id=1, replica_groups=mesh['blk_0'=2,'blk_1'=12,'blk_2'=2,'grp_0'=4,'grp_1'=4] {'blk_0'}, use_global_device_ids=true, to_apply=%region_0.0 | all-reduce | flops 1 | bytes 8 | tf_op jit(solution)/shard_map/psum | solution.py:174
  132.6 47.8 %psum.36 = f32[1,1]{1,0:T(1,128)} all-reduce(f32[1,1]{1,0:T(1,128)} %psum.35), channel_id=1, replica_groups=mesh['blk_0'=2,'blk_1'=12,'blk_2'=2,'grp_0'=4,'grp_1'=4] {'blk_1'}, use_global_device_ids=true, to_apply=%region_1.0 | all-reduce | flops 1 | bytes 8 | tf_op jit(solution)/shard_map/psum | solution.py:174
  180.4 3.1 %psum.37 = f32[1,1]{1,0:T(1,128)} all-reduce(f32[1,1]{1,0:T(1,128)} %psum.36), channel_id=1, replica_groups=mesh['blk_0'=2,'blk_1'=12,'blk_2'=2,'grp_0'=4,'grp_1'=4] {'blk_2'}, use_global_device_ids=true, to_apply=%region_2.0 | all-reduce | flops 1 | bytes 8 | tf_op jit(solution)/shard_map/psum | solution.py:174
  183.5 8.1 %psum.38 = f32[1,1]{1,0:T(1,128)} all-reduce(f32[1,1]{1,0:T(1,128)} %psum.37), channel_id=1, replica_groups=mesh['blk_0'=2,'blk_1'=12,'blk_2'=2,'grp_0'=4,'grp_1'=4] {'grp_0'}, use_global_device_ids=true, to_apply=%region_3.0 | all-reduce | flops 1 | bytes 8 | tf_op jit(solution)/shard_map/psum | solution.py:174
  191.6 12.7 %psum.39.loss_sum = f32[1,1]{1,0:T(1,128)} all-reduce(f32[1,1]{1,0:T(1,128)} %psum.38), channel_id=1, replica_groups=mesh['blk_0'=2,'blk_1'=12,'blk_2'=2,'grp_0'=4,'grp_1'=4] {'grp_1'}, use_global_device_ids=true, to_apply=%region_4.0 | all-reduce | flops 1 | bytes 8 | tf_op jit(solution)/shard_map/psum | solution.py:174
  204.2 1.3 copy-done.5
  205.5 3.4 %shard_map.90 = (f32[1,1]{1,0:T(1,128)}, f32[256,1152]{1,0:T(8,128)}) custom-call(f32[1,1]{1,0:T(1,128)} %bitcast.10.scale, f32[1,1]{1,0:T(1,128)} %bitcast.13.bias, f32[1,1]{1,0:T(1,128)} %psum.39.loss_sum, bf16[256,1152]{1,0:T(8,128)(2,1)S(1)} %bitcast.19, bf16[48,2,16,384]{3,2,1,0:T(8,128)(2,1)S(1)} %all-to-all-done.2.received, f32[256,1152]{1,0:T(8,128)S(1)} %copy-done.5), custom_call_target="tpu_custom_call" | custom-call | flops 603979776 | bytes 4128768 | tf_op jit(solution)/shard_map/pallas_call | solution.py:176
  (15 shorter events, 0.0 us)
Async XLA Ops:
  0.6 1.1 copy-start
  1.7 1.1 copy-start.2
  2.9 57.8 %copy-start.9 = (s32[2,48]{1,0:T(2,128)S(1)}, s32[2,48]{1,0:T(2,128)}, u32[]{:S(2)}) copy-start(s32[2,48]{1,0:T(2,128)} %partners.3) | copy-start | bytes 1156
  62.4 10.6 %copy-start.10 = (s32[1,1,256]{2,1,0:T(1,128)S(1)}, s32[1,1,256]{2,1,0:T(1,128)}, u32[]{:S(2)}) copy-start(s32[1,1,256]{2,1,0:T(1,128)} %param.8) | copy-start | bytes 3076
  62.4 11.5 %copy-start.1 = (bf16[1,256,1152]{2,1,0:T(8,128)(2,1)S(1)}, bf16[1,256,1152]{2,1,0:T(8,128)(2,1)}, u32[]{:S(2)}) copy-start(bf16[1,256,1152]{2,1,0:T(8,128)(2,1)} %param.6) | copy-start | bytes 1769476
  62.4 11.5 %copy-start.3 = (bf16[1,256,1152]{2,1,0:T(8,128)(2,1)S(1)}, bf16[1,256,1152]{2,1,0:T(8,128)(2,1)}, u32[]{:S(2)}) copy-start(bf16[1,256,1152]{2,1,0:T(8,128)(2,1)} %param.7) | copy-start | bytes 1769476
  62.4 50.5 %all-to-all-start.1 = ((bf16[48,2,16,384]{3,2,1,0:T(8,128)(2,1)}), bf16[48,2,16,384]{3,2,1,0:T(8,128)(2,1)S(1)}, u32[]{:S(2)}, u32[]{:S(2)}) async-start(bf16[48,2,16,384]{3,2,1,0:T(8,128)(2,1)} %shard_map.88), calls=%async_computation.1 | async-start | bytes 2359296 | tf_op jit(solution)/shard_map/all_to_all | solution.py:158
  73.8 0.9 copy-start.8
  76.1 1.0 copy-start.4
  77.1 1.0 copy-start.6
  112.9 91.3 %all-to-all-start.2 = ((bf16[48,2,16,384]{3,2,1,0:T(8,128)(2,1)}), bf16[48,2,16,384]{3,2,1,0:T(8,128)(2,1)S(1)}, u32[]{:S(2)}, u32[]{:S(2)}) async-start(bf16[48,2,16,384]{3,2,1,0:T(8,128)(2,1)} %shard_map.86), calls=%async_computation.2 | async-start | bytes 2359296 | tf_op jit(solution)/shard_map/all_to_all | solution.py:162
  122.1 1.3 copy-start.7
  204.2 1.3 copy-start.5

commit v2 on v1

v2 whole, which is shorter than its diff:
```python
import functools

import jax
import jax.numpy as jnp
from jax import lax
from jax.experimental import pallas as pl
from jax.experimental.pallas import tpu as pltpu
from jax.sharding import Mesh
from jax.sharding import PartitionSpec as P

BLK = ("blk_0", "blk_1", "blk_2")
GRP = ("grp_0", "grp_1")

ROWS = 256
PIECE_ROWS = 16
PIECE_COLS = 384
VMEM = pl.BlockSpec(memory_space=pltpu.VMEM)
SMEM = pl.BlockSpec(memory_space=pltpu.SMEM)
HBM = pl.BlockSpec(memory_space=pltpu.HBM)


def local_kernel(kernel, out_shape, in_specs, out_specs, scratch=(), vmem=24, flops=0, moved=0, exps=0):
    return pl.pallas_call(
        kernel,
        out_shape=out_shape,
        in_specs=in_specs,
        out_specs=out_specs,
        scratch_shapes=list(scratch),
        compiler_params=pltpu.CompilerParams(vmem_limit_bytes=vmem << 20),
        cost_estimate=pl.CostEstimate(flops=flops, bytes_accessed=moved, transcendentals=exps),
    )


def pack_kernel(texts, images, packed, sems):
    row_groups, _, columns = texts.shape
    copies = []
    for which, rows in enumerate((texts, images)):
        for col in range(columns // PIECE_COLS):
            copies.append(
                pltpu.make_async_copy(
                    rows.at[:, :, pl.ds(col * PIECE_COLS, PIECE_COLS)],
                    packed.at[pl.ds(col * row_groups, row_groups), which],
                    sems.at[len(copies)],
                )
            )
    for copy in copies:
        copy.start()
    for copy in copies:
        copy.wait()


def regroup_kernel(which, partners, spread, send):
    rounds, blocks = partners.shape
    for block in range(blocks):
        for r in range(rounds):
            send[block, r] = spread[partners[r, block], which]


def column_group(received, r, col):
    blocks, _, rows, columns = received.shape
    row_groups = ROWS // rows
    return received[pl.ds(col * row_groups, row_groups), r].reshape(ROWS, columns)


def columns_of(col):
    return pl.ds(col * PIECE_COLS, PIECE_COLS)


def dot_nt(a, b):
    return lax.dot_general(a, b, (((1,), (1,)), ((), ())), preferred_element_type=jnp.float32)


def dot_tn(a, b):
    return lax.dot_general(a, b, (((0,), (0,)), ((), ())), preferred_element_type=jnp.float32)


def dot_nn(a, b):
    return jnp.dot(a, b, preferred_element_type=jnp.float32)


def sigmoid_parts(x):
    e = jnp.exp(-jnp.abs(x))
    s = 1.0 / (1.0 + e)
    return e, jnp.where(x >= 0, s, e * s)


def own_kernel(scale, bias, images, texts, labels, loss, image_grad, text_grad):
    x, y = images[...], texts[...]
    logits = scale[0, 0] * dot_nt(x, y) + bias[0, 0]
    match = lax.broadcasted_iota(jnp.int32, logits.shape, 1) == labels[...]
    signed = jnp.where(match, -logits, logits)
    e, s = sigmoid_parts(signed)
    loss[0, 0] = jnp.sum(jnp.maximum(signed, 0.0) + jnp.log1p(e))
    weight = jnp.where(match, -s, s).astype(jnp.bfloat16)
    image_grad[...] = scale[0, 0] * dot_nn(weight, y)
    text_grad[...] = scale[0, 0] * dot_tn(weight, x)


def partner_logits(scale, bias, own, received, r):
    total = jnp.zeros((own.shape[0], own.shape[0]), jnp.float32)
    for col in range(own.shape[1] // PIECE_COLS):
        total += dot_nt(own[:, columns_of(col)], column_group(received, r, col))
    return scale[0, 0] * total + bias[0, 0]


def add_and_write(scale, weights, received, part_copy, acc, grad, sems):
    part_copy.wait()
    copies = []
    for col in range(acc.shape[1] // PIECE_COLS):
        cols = columns_of(col)
        product = sum(
            dot_nn(weight, column_group(received, r, col)) for r, weight in enumerate(weights)
        )
        acc[:, cols] += scale[0, 0] * product
        copy = pltpu.make_async_copy(acc.at[:, cols], grad.at[:, cols], sems.at[col])
        copy.start()
        copies.append(copy)
    for copy in copies:
        copy.wait()


def text_kernel(scale, bias, own_loss, images, received, part, loss, grad, acc, part_sem, sems):
    part_copy = pltpu.make_async_copy(part, acc, part_sem)
    part_copy.start()
    total, weights = own_loss[0, 0], []
    for r in range(received.shape[1]):
        logits = partner_logits(scale, bias, images, received, r)
        e, s = sigmoid_parts(logits)
        total += jnp.sum(jnp.maximum(logits, 0.0) + jnp.log1p(e))
        weights.append(s.astype(jnp.bfloat16))
    loss[0, 0] = total
    add_and_write(scale, weights, received, part_copy, acc, grad, sems)


def image_kernel(scale, bias, texts, received, part, grad, acc, part_sem, sems):
    part_copy = pltpu.make_async_copy(part, acc, part_sem)
    part_copy.start()
    weights = []
    for r in range(received.shape[1]):
        _, s = sigmoid_parts(partner_logits(scale, bias, texts, received, r))
        weights.append(s.astype(jnp.bfloat16))
    add_and_write(scale, weights, received, part_copy, acc, grad, sems)


def shifted(value, axis, by):
    size = lax.axis_size(axis)
    return lax.ppermute(value, axis, [(i, (i + by) % size) for i in range(size)])


def sum_by_pairs(value, axis):
    size, step = lax.axis_size(axis), 1
    while step < size:
        value += lax.ppermute(value, axis, [(i, i ^ step) for i in range(size)])
        step *= 2
    return value


def sum_of_three(a, b, c):
    least, most = jnp.minimum(a, b), jnp.maximum(a, b)
    middle = jnp.maximum(least, jnp.minimum(most, c))
    return (jnp.minimum(least, c) + jnp.maximum(most, c)) + middle


def body(images, texts, labels, partners, logit_scale, logit_bias):
    x, y = images[0], texts[0]
    rows, width = x.shape
    rounds, blocks = partners.shape
    scale, bias = logit_scale.reshape(1, 1), logit_bias.reshape(1, 1)
    piece = (PIECE_ROWS, PIECE_COLS)
    one = jax.ShapeDtypeStruct((1, 1), jnp.float32)
    grad = jax.ShapeDtypeStruct((rows, width), jnp.float32)
    col_groups = width // PIECE_COLS
    scratch = [
        pltpu.VMEM((rows, width), jnp.float32),
        pltpu.SemaphoreType.DMA,
        pltpu.SemaphoreType.DMA((col_groups,)),
    ]
    mac = 2 * rows * rows * width
    nbytes = rows * width * 2
    exchange = functools.partial(
        lax.all_to_all, axis_name=BLK, split_axis=0, concat_axis=0, tiled=True
    )

    packed = local_kernel(
        pack_kernel,
        jax.ShapeDtypeStruct((blocks, 2, *piece), x.dtype),
        [HBM, HBM],
        HBM,
        [pltpu.SemaphoreType.DMA((2 * col_groups,))],
        vmem=60,
        moved=4 * nbytes,
    )(y.reshape(-1, PIECE_ROWS, width), x.reshape(-1, PIECE_ROWS, width))
    spread = exchange(packed)

    def regroup(which):
        return local_kernel(
            functools.partial(regroup_kernel, which),
            jax.ShapeDtypeStruct((blocks, rounds, *piece), x.dtype),
            [SMEM, VMEM],
            VMEM,
            moved=4 * nbytes,
        )(partners, spread)

    own_loss, image_part, text_part = local_kernel(
        own_kernel,
        (one, grad, grad),
        [SMEM, SMEM, VMEM, VMEM, VMEM],
        (SMEM, VMEM, VMEM),
        flops=3 * mac,
        moved=6 * nbytes,
        exps=3 * rows * rows,
    )(scale, bias, x, y, labels[0].reshape(rows, 1))

    their_texts = exchange(regroup(0))
    send_images, own_loss, image_part, text_part = lax.optimization_barrier(
        (regroup(1), own_loss, image_part, text_part)
    )
    their_images = exchange(send_images)

    loss, image_grad = local_kernel(
        text_kernel,
        (one, grad),
        [SMEM, SMEM, SMEM, VMEM, VMEM, HBM],
        (SMEM, HBM),
        scratch,
        vmem=52,
        flops=2 * rounds * mac,
        moved=7 * nbytes,
        exps=3 * rounds * rows * rows,
    )(scale, bias, own_loss, x, their_texts, image_part)
    for axis in ("blk_2", "blk_0", "grp_0", "grp_1"):
        loss = sum_by_pairs(loss, axis)
    loss = (loss + shifted(loss, "blk_1", 6)) + (
        shifted(loss, "blk_1", 3) + shifted(loss, "blk_1", -3)
    )
    their_images, loss = lax.optimization_barrier((their_images, loss))
    loss = sum_of_three(loss, shifted(loss, "blk_1", 1), shifted(loss, "blk_1", -1))
    loss = loss / jnp.float32(lax.axis_size(BLK) * lax.axis_size(GRP) * rows)
    text_grad = local_kernel(
        image_kernel,
        grad,
        [SMEM, SMEM, VMEM, VMEM, HBM],
        HBM,
        scratch,
        vmem=52,
        flops=2 * rounds * mac,
        moved=7 * nbytes,
        exps=2 * rounds * rows * rows,
    )(scale, bias, y, their_images, text_part)
    return image_grad[None], text_grad[None], loss[0, 0]


def solution(mesh):
    split = Mesh(
        mesh.devices.reshape(2, 12, 2, 4, 4), ("blk_0", "blk_1", "blk_2", "grp_0", "grp_1")
    )
    in_specs = (P(GRP, BLK, None), P(GRP, BLK, None), P(GRP, BLK, None), P(), P(), P())
    out_specs = (P(GRP, BLK, None), P(GRP, BLK, None), P())
    return jax.shard_map(body, mesh=split, in_specs=in_specs, out_specs=out_specs, check_vma=False)
```

time: 213 us -> 245 us (1.15); the launches traced: 209 us -> 244 us
  blocking collectives: 135 us -> 58 us
  starting transfers between devices: 18.5 us -> 80.3 us
  Pallas kernels: 11.8 us -> 48.7 us
  between operations: 2.01 us -> 13 us
  waiting for transfers between devices: 33 us -> 40.5 us
  local copies, waits for them, and re-layouts: 8.4 us -> 3.78 us
    psum x5 -> x0, blocking collectives: 77.3 us -> none  [body(): loss_sum = functools.reduce(lax.psum, BLK_GRP, loss_part)]
    ppermute x0 -> x11, starting transfers between devices: none -> 61.7 us  [the longest x5 32.2 us: shifted(): lax.ppermute(value, axis, [(i, (i + by) % size) for i in range(size)])]
    pallas_call x1, Pallas kernels: 0.1 us -> 36.9 us  [body(): local_kernel(pack_kernel, jax.ShapeDtypeStruct((blocks, 2, *piece), x.dty...]
    ppermute x0 -> x11, waiting for transfers between devices: none -> 7.44 us  [the longest x6 6.86 us: sum_by_pairs(): value += lax.ppermute(value, axis, [(i, i ^ step) for i in range(size)])]
    unnamed x22 -> x14, local copies, waits for them, and re-layouts: 7.6 us -> 2.98 us
  transfers between devices with their start and end apart: 2 -> 13, of which waited for: 1 -> 9; matrix products, arithmetic and copies ran while one was open for 0% -> 0% of each run, Pallas kernels for 3% -> 4%
where the time goes in v2:
time: 245 us; the launch traced here: 244 us
  starting transfers between devices  80.3 us (33%)
  blocking collectives  58 us (24%)
  Pallas kernels  48.7 us (20%)
  waiting for transfers between devices  40.5 us (17%)
  between operations  13 us (5%)
  local copies, waits for them, and re-layouts  3.78 us (2%)
    all_to_all x1, blocking collectives, body(): spread = exchange(packed)  58 us
    pallas_call x1, Pallas kernels, body(): local_kernel(pack_kernel, jax.ShapeDtypeStruct((blocks, 2, *piece), x.dty...  36.9 us
    all_to_all x1, waiting for transfers between devices, body(): their_texts = exchange(regroup(0))  33 us
    ppermute x5, starting transfers between devices, shifted(): lax.ppermute(value, axis, [(i, (i + by) % size) for i in range(size)])  32.2 us
    ppermute x6, starting transfers between devices, sum_by_pairs(): value += lax.ppermute(value, axis, [(i, i ^ step) for i in range(size)])  29.5 us
    all_to_all x1, starting transfers between devices, body(): their_texts = exchange(regroup(0))  9.33 us
    all_to_all x1, starting transfers between devices, body(): their_images = exchange(send_images)  9.2 us
    ppermute x6, waiting for transfers between devices, sum_by_pairs(): value += lax.ppermute(value, axis, [(i, i ^ step) for i in range(size)])  6.86 us
  transfers between devices with their start and end apart: 13, of which 9 were waited for; matrix products, arithmetic and copies ran while one was open for 0% of the time, Pallas kernels for 4%

profile of v2, /device:TPU:6, one launch (start us, length us, event | category | flops | bytes accessed | tf_op | source)
XLA Modules:
  0.0 244.2 jit_solution(16435044988239164467)
XLA Ops:
  0.6 36.9 %shard_map.85 = bf16[48,2,16,384]{3,2,1,0:T(8,128)(2,1)} custom-call(bf16[16,16,1152]{2,1,0:T(8,128)(2,1)} %bitcast.16, bf16[16,16,1152]{2,1,0:T(8,128)(2,1)} %bitcast.19), custom_call_target="tpu_custom_call" | custom-call | bytes 2359296 | tf_op jit(solution)/shard_map/pallas_call | solution.py:184
  37.5 58.0 %all_to_all.15.spread = bf16[48,2,16,384]{3,2,1,0:T(8,128)(2,1)S(1)} all-to-all(bf16[48,2,16,384]{3,2,1,0:T(8,128)(2,1)} %shard_map.85), channel_id=1, replica_groups=mesh['blk_0'=2,'blk_1'=12,'blk_2'=2,'grp_0'=4,'grp_1'=4] {'blk_0','blk_1..., dimensions={0} | all-to-all | bytes 2359296 | tf_op jit(solution)/shard_map/all_to_all | solution.py:193
  95.6 1.7 shard_map.88
  97.3 9.3 %all-to-all-start.1 = ((bf16[48,2,16,384]{3,2,1,0:T(8,128)(2,1)}), bf16[48,2,16,384]{3,2,1,0:T(8,128)(2,1)S(1)}, u32[]{:S(2)}, u32[]{:S(2)}) async-start(bf16[48,2,16,384]{3,2,1,0:T(8,128)(2,1)} %shard_map.88), calls=%async_computation.1 | async-start | bytes 2359296 | tf_op jit(solution)/shard_map/all_to_all | solution.py:214
  109.6 1.4 shard_map.87
  113.1 1.7 shard_map.86
  114.8 33.0 %all-to-all-done.1.received = bf16[48,2,16,384]{3,2,1,0:T(8,128)(2,1)S(1)} async-done(((bf16[48,2,16,384]{3,2,1,0:T(8,128)(2,1)}), bf16[48,2,16,384]{3,2,1,0:T(8,128)(2,1)S(1)}, u32[]{:S(2)}, u32[]{:S(2)}) %all-to-all-start.1) | async-done | bytes 1179680 | tf_op jit(solution)/shard_map/all_to_all | solution.py:214
  147.8 9.2 %all-to-all-start.2 = ((bf16[48,2,16,384]{3,2,1,0:T(8,128)(2,1)}), bf16[48,2,16,384]{3,2,1,0:T(8,128)(2,1)S(1)}, u32[]{:S(2)}, u32[]{:S(2)}) async-start(bf16[48,2,16,384]{3,2,1,0:T(8,128)(2,1)} %shard_map.86), calls=%async_computation.2 | async-start | bytes 2359296 | tf_op jit(solution)/shard_map/all_to_all | solution.py:218
  157.0 4.1 %shard_map.89 = (f32[1,1]{1,0:T(1,128)}, f32[256,1152]{1,0:T(8,128)}) custom-call(f32[1,1]{1,0:T(1,128)} %bitcast.11.scale, f32[1,1]{1,0:T(1,128)} %bitcast.14.bias, f32[1,1]{1,0:T(1,128)} %get-tuple-element.17.own_loss, bf16[256,1152]{1,0:T(8,128)(2,1)S(1)} %bitcast.21, bf16[48,2,16,384]{3,2,1,0:T(8,128)(2,1)S(1)} %all-to-all-done.1.received, ...), custom_call_target="tpu_custom_call" | custom-call | flops 603979776 | bytes 4128768 | tf_op jit(solution)/shard_map/pallas_call | solution.py:220
  161.1 2.1 collective-permute-start
  165.6 4.9 %collective-permute-start.1 = (f32[1,1]{1,0:T(1,128)}, f32[1,1]{1,0:T(1,128)}, u32[]{:S(2)}, u32[]{:S(2)}) collective-permute-start(f32[1,1]{1,0:T(1,128)} %add.33), channel_id=1, source_target_pairs={{0,384},{384,0},{1,385},{385,1},{2,386},{386,2},{3,387},{387,3},{4... | collective-permute-start | bytes 20 | tf_op jit(solution)/shard_map/ppermute | solution.py:153
  171.6 4.0 %collective-permute-start.2 = (f32[1,1]{1,0:T(1,128)}, f32[1,1]{1,0:T(1,128)}, u32[]{:S(2)}, u32[]{:S(2)}) collective-permute-start(f32[1,1]{1,0:T(1,128)} %add.34), channel_id=1, source_target_pairs={{0,4},{4,0},{8,12},{12,8},{1,5},{5,1},{9,13},{13,9},{2,6},{6,2},{1... | collective-permute-start | bytes 20 | tf_op jit(solution)/shard_map/ppermute | solution.py:153
  175.6 1.4 collective-permute-done.2
  177.7 4.6 %collective-permute-start.3 = (f32[1,1]{1,0:T(1,128)}, f32[1,1]{1,0:T(1,128)}, u32[]{:S(2)}, u32[]{:S(2)}) collective-permute-start(f32[1,1]{1,0:T(1,128)} %add.35), channel_id=1, source_target_pairs={{0,8},{4,12},{8,0},{12,4},{1,9},{5,13},{9,1},{13,5},{2,10},{6,14},... | collective-permute-start | bytes 20 | tf_op jit(solution)/shard_map/ppermute | solution.py:153
  182.3 2.3 collective-permute-done.3
  185.3 5.8 %collective-permute-start.4 = (f32[1,1]{1,0:T(1,128)}, f32[1,1]{1,0:T(1,128)}, u32[]{:S(2)}, u32[]{:S(2)}) collective-permute-start(f32[1,1]{1,0:T(1,128)} %add.36), channel_id=1, source_target_pairs={{0,1},{1,0},{2,3},{3,2},{4,5},{5,4},{6,7},{7,6},{8,9},{9,8},{10,11... | collective-permute-start | bytes 20 | tf_op jit(solution)/shard_map/ppermute | solution.py:153
  192.2 8.1 %collective-permute-start.5 = (f32[1,1]{1,0:T(1,128)}, f32[1,1]{1,0:T(1,128)}, u32[]{:S(2)}, u32[]{:S(2)}) collective-permute-start(f32[1,1]{1,0:T(1,128)} %add.37), channel_id=1, source_target_pairs={{0,2},{1,3},{2,0},{3,1},{4,6},{5,7},{6,4},{7,5},{8,10},{9,11},{10,... | collective-permute-start | bytes 20 | tf_op jit(solution)/shard_map/ppermute | solution.py:153
  200.4 1.2 collective-permute-done.5
  202.2 7.9 %collective-permute-start.8 = (f32[1,1]{1,0:T(1,128)}, f32[1,1]{1,0:T(1,128)}, u32[]{:S(2)}, u32[]{:S(2)}) collective-permute-start(f32[1,1]{1,0:T(1,128)} %add.38), channel_id=1, source_target_pairs={{0,288},{32,320},{64,352},{96,0},{128,32},{160,64},{192,96},{224,1... | collective-permute-start | bytes 20 | tf_op jit(solution)/shard_map/ppermute | solution.py:147
  210.1 3.2 %collective-permute-start.7 = (f32[1,1]{1,0:T(1,128)}, f32[1,1]{1,0:T(1,128)}, u32[]{:S(2)}, u32[]{:S(2)}) collective-permute-start(f32[1,1]{1,0:T(1,128)} %add.38), channel_id=1, source_target_pairs={{0,96},{32,128},{64,160},{96,192},{128,224},{160,256},{192,288},{2... | collective-permute-start | bytes 20 | tf_op jit(solution)/shard_map/ppermute | solution.py:147
  213.3 11.5 %collective-permute-start.6 = (f32[1,1]{1,0:T(1,128)}, f32[1,1]{1,0:T(1,128)}, u32[]{:S(2)}, u32[]{:S(2)}) collective-permute-start(f32[1,1]{1,0:T(1,128)} %add.38), channel_id=1, source_target_pairs={{0,192},{32,224},{64,256},{96,288},{128,320},{160,352},{192,0},{22... | collective-permute-start | bytes 20 | tf_op jit(solution)/shard_map/ppermute | solution.py:147
  226.9 6.4 %collective-permute-start.10 = (f32[1,1]{1,0:T(1,128)}, f32[1,1]{1,0:T(1,128)}, u32[]{:S(2)}, u32[]{:S(2)}) collective-permute-start(f32[1,1]{1,0:T(1,128)} %add.41), channel_id=1, source_target_pairs={{0,352},{32,0},{64,32},{96,64},{128,96},{160,128},{192,160},{224,1... | collective-permute-start | bytes 20 | tf_op jit(solution)/shard_map/ppermute | solution.py:147
  233.4 3.2 %collective-permute-start.9 = (f32[1,1]{1,0:T(1,128)}, f32[1,1]{1,0:T(1,128)}, u32[]{:S(2)}, u32[]{:S(2)}) collective-permute-start(f32[1,1]{1,0:T(1,128)} %add.41), channel_id=1, source_target_pairs={{0,32},{32,64},{64,96},{96,128},{128,160},{160,192},{192,224},{224... | collective-permute-start | bytes 20 | tf_op jit(solution)/shard_map/ppermute | solution.py:147
  236.6 3.0 %shard_map.90 = f32[256,1152]{1,0:T(8,128)} custom-call(f32[1,1]{1,0:T(1,128)} %bitcast.12.scale, f32[1,1]{1,0:T(1,128)} %bitcast.15.bias, bf16[256,1152]{1,0:T(8,128)(2,1)S(1)} %bitcast.18, bf16[48,2,16,384]{3,2,1,0:T(8,128)(2,1)S(1)} %all-to-all-done.2.received, f32[256,1152]{1,0:T(8,128)} %copy-done.2), custom_call_target="tpu_custom_call" | custom-call | flops 603979776 | bytes 4128768 | tf_op jit(solution)/shard_map/pallas_call | solution.py:239
  (24 shorter events, 6.4 us)
Async XLA Ops:
  37.5 58.0 %copy-start.5 = (s32[2,48]{1,0:T(2,128)S(1)}, s32[2,48]{1,0:T(2,128)}, u32[]{:S(2)}) copy-start(s32[2,48]{1,0:T(2,128)} %partners.3) | copy-start | bytes 1156
  97.3 10.6 %copy-start.6 = (s32[1,1,256]{2,1,0:T(1,128)S(1)}, s32[1,1,256]{2,1,0:T(1,128)}, u32[]{:S(2)}) copy-start(s32[1,1,256]{2,1,0:T(1,128)} %param.8) | copy-start | bytes 3076
  97.3 11.5 %copy-start = (bf16[1,256,1152]{2,1,0:T(8,128)(2,1)S(1)}, bf16[1,256,1152]{2,1,0:T(8,128)(2,1)}, u32[]{:S(2)}) copy-start(bf16[1,256,1152]{2,1,0:T(8,128)(2,1)} %param.7) | copy-start | bytes 1769476
  97.3 11.5 %copy-start.1 = (bf16[1,256,1152]{2,1,0:T(8,128)(2,1)S(1)}, bf16[1,256,1152]{2,1,0:T(8,128)(2,1)}, u32[]{:S(2)}) copy-start(bf16[1,256,1152]{2,1,0:T(8,128)(2,1)} %param.6) | copy-start | bytes 1769476
  97.3 50.5 %all-to-all-start.1 = ((bf16[48,2,16,384]{3,2,1,0:T(8,128)(2,1)}), bf16[48,2,16,384]{3,2,1,0:T(8,128)(2,1)S(1)}, u32[]{:S(2)}, u32[]{:S(2)}) async-start(bf16[48,2,16,384]{3,2,1,0:T(8,128)(2,1)} %shard_map.88), calls=%async_computation.1 | async-start | bytes 2359296 | tf_op jit(solution)/shard_map/all_to_all | solution.py:214
  108.7 0.9 copy-start.4
  111.0 1.0 copy-start.2
  112.0 1.0 copy-start.3
  147.8 79.2 %all-to-all-start.2 = ((bf16[48,2,16,384]{3,2,1,0:T(8,128)(2,1)}), bf16[48,2,16,384]{3,2,1,0:T(8,128)(2,1)S(1)}, u32[]{:S(2)}, u32[]{:S(2)}) async-start(bf16[48,2,16,384]{3,2,1,0:T(8,128)(2,1)} %shard_map.86), calls=%async_computation.2 | async-start | bytes 2359296 | tf_op jit(solution)/shard_map/all_to_all | solution.py:218
  161.1 3.1 %collective-permute-start = (f32[1,1]{1,0:T(1,128)}, f32[1,1]{1,0:T(1,128)}, u32[]{:S(2)}, u32[]{:S(2)}) collective-permute-start(f32[1,1]{1,0:T(1,128)} %get-tuple-element.21), channel_id=1, source_target_pairs={{0,16},{16,0},{1,17},{17,1},{2,18},{18,2},{3,19},{19,3},{4,20},{20... | collective-permute-start | bytes 20 | tf_op jit(solution)/shard_map/ppermute | solution.py:153
  165.6 5.4 %collective-permute-start.1 = (f32[1,1]{1,0:T(1,128)}, f32[1,1]{1,0:T(1,128)}, u32[]{:S(2)}, u32[]{:S(2)}) collective-permute-start(f32[1,1]{1,0:T(1,128)} %add.33), channel_id=1, source_target_pairs={{0,384},{384,0},{1,385},{385,1},{2,386},{386,2},{3,387},{387,3},{4... | collective-permute-start | bytes 20 | tf_op jit(solution)/shard_map/ppermute | solution.py:153
  171.6 5.4 %collective-permute-start.2 = (f32[1,1]{1,0:T(1,128)}, f32[1,1]{1,0:T(1,128)}, u32[]{:S(2)}, u32[]{:S(2)}) collective-permute-start(f32[1,1]{1,0:T(1,128)} %add.34), channel_id=1, source_target_pairs={{0,4},{4,0},{8,12},{12,8},{1,5},{5,1},{9,13},{13,9},{2,6},{6,2},{1... | collective-permute-start | bytes 20 | tf_op jit(solution)/shard_map/ppermute | solution.py:153
  177.7 6.9 %collective-permute-start.3 = (f32[1,1]{1,0:T(1,128)}, f32[1,1]{1,0:T(1,128)}, u32[]{:S(2)}, u32[]{:S(2)}) collective-permute-start(f32[1,1]{1,0:T(1,128)} %add.35), channel_id=1, source_target_pairs={{0,8},{4,12},{8,0},{12,4},{1,9},{5,13},{9,1},{13,5},{2,10},{6,14},... | collective-permute-start | bytes 20 | tf_op jit(solution)/shard_map/ppermute | solution.py:153
  185.3 6.3 %collective-permute-start.4 = (f32[1,1]{1,0:T(1,128)}, f32[1,1]{1,0:T(1,128)}, u32[]{:S(2)}, u32[]{:S(2)}) collective-permute-start(f32[1,1]{1,0:T(1,128)} %add.36), channel_id=1, source_target_pairs={{0,1},{1,0},{2,3},{3,2},{4,5},{5,4},{6,7},{7,6},{8,9},{9,8},{10,11... | collective-permute-start | bytes 20 | tf_op jit(solution)/shard_map/ppermute | solution.py:153
  192.2 9.3 %collective-permute-start.5 = (f32[1,1]{1,0:T(1,128)}, f32[1,1]{1,0:T(1,128)}, u32[]{:S(2)}, u32[]{:S(2)}) collective-permute-start(f32[1,1]{1,0:T(1,128)} %add.37), channel_id=1, source_target_pairs={{0,2},{1,3},{2,0},{3,1},{4,6},{5,7},{6,4},{7,5},{8,10},{9,11},{10,... | collective-permute-start | bytes 20 | tf_op jit(solution)/shard_map/ppermute | solution.py:153
  202.2 23.5 %collective-permute-start.8 = (f32[1,1]{1,0:T(1,128)}, f32[1,1]{1,0:T(1,128)}, u32[]{:S(2)}, u32[]{:S(2)}) collective-permute-start(f32[1,1]{1,0:T(1,128)} %add.38), channel_id=1, source_target_pairs={{0,288},{32,320},{64,352},{96,0},{128,32},{160,64},{192,96},{224,1... | collective-permute-start | bytes 20 | tf_op jit(solution)/shard_map/ppermute | solution.py:147
  210.1 15.6 %collective-permute-start.7 = (f32[1,1]{1,0:T(1,128)}, f32[1,1]{1,0:T(1,128)}, u32[]{:S(2)}, u32[]{:S(2)}) collective-permute-start(f32[1,1]{1,0:T(1,128)} %add.38), channel_id=1, source_target_pairs={{0,96},{32,128},{64,160},{96,192},{128,224},{160,256},{192,288},{2... | collective-permute-start | bytes 20 | tf_op jit(solution)/shard_map/ppermute | solution.py:147
  213.3 11.7 %collective-permute-start.6 = (f32[1,1]{1,0:T(1,128)}, f32[1,1]{1,0:T(1,128)}, u32[]{:S(2)}, u32[]{:S(2)}) collective-permute-start(f32[1,1]{1,0:T(1,128)} %add.38), channel_id=1, source_target_pairs={{0,192},{32,224},{64,256},{96,288},{128,320},{160,352},{192,0},{22... | collective-permute-start | bytes 20 | tf_op jit(solution)/shard_map/ppermute | solution.py:147
  226.9 14.4 %collective-permute-start.10 = (f32[1,1]{1,0:T(1,128)}, f32[1,1]{1,0:T(1,128)}, u32[]{:S(2)}, u32[]{:S(2)}) collective-permute-start(f32[1,1]{1,0:T(1,128)} %add.41), channel_id=1, source_target_pairs={{0,352},{32,0},{64,32},{96,64},{128,96},{160,128},{192,160},{224,1... | collective-permute-start | bytes 20 | tf_op jit(solution)/shard_map/ppermute | solution.py:147
  233.4 6.6 %collective-permute-start.9 = (f32[1,1]{1,0:T(1,128)}, f32[1,1]{1,0:T(1,128)}, u32[]{:S(2)}, u32[]{:S(2)}) collective-permute-start(f32[1,1]{1,0:T(1,128)} %add.41), channel_id=1, source_target_pairs={{0,32},{32,64},{64,96},{96,128},{128,160},{160,192},{192,224},{224... | collective-permute-start | bytes 20 | tf_op jit(solution)/shard_map/ppermute | solution.py:147

commit v3 on v2

--- a/solution.py
+++ b/solution.py
@@ -31,22 +31,23 @@
     )
 
 
-def pack_kernel(texts, images, packed, sems):
-    row_groups, _, columns = texts.shape
-    copies = []
-    for which, rows in enumerate((texts, images)):
-        for col in range(columns // PIECE_COLS):
-            copies.append(
-                pltpu.make_async_copy(
-                    rows.at[:, :, pl.ds(col * PIECE_COLS, PIECE_COLS)],
-                    packed.at[pl.ds(col * row_groups, row_groups), which],
-                    sems.at[len(copies)],
-                )
-            )
+def columns_of(col):
+    return pl.ds(col * PIECE_COLS, PIECE_COLS)
+
+
+def pack_kernel(texts, images, packed, rows, sems):
+    copies = [
+        pltpu.make_async_copy(block, rows.at[which], sems.at[which])
+        for which, block in enumerate((texts, images))
+    ]
     for copy in copies:
         copy.start()
-    for copy in copies:
+    row_groups = ROWS // PIECE_ROWS
+    for which, copy in enumerate(copies):
         copy.wait()
+        for index in range(packed.shape[0]):
+            col, row = divmod(index, row_groups)
+            packed[index, which] = rows[which, pl.ds(row * PIECE_ROWS, PIECE_ROWS), columns_of(col)]
 
 
 def regroup_kernel(which, partners, spread, send):
@@ -60,10 +61,6 @@
     blocks, _, rows, columns = received.shape
     row_groups = ROWS // rows
     return received[pl.ds(col * row_groups, row_groups), r].reshape(ROWS, columns)
-
-
-def columns_of(col):
-    return pl.ds(col * PIECE_COLS, PIECE_COLS)
 
 
 def dot_nt(a, b):
@@ -119,16 +116,20 @@
         copy.wait()
 
 
-def text_kernel(scale, bias, own_loss, images, received, part, loss, grad, acc, part_sem, sems):
-    part_copy = pltpu.make_async_copy(part, acc, part_sem)
-    part_copy.start()
-    total, weights = own_loss[0, 0], []
+def loss_kernel(scale, bias, own_loss, images, received, loss, weights):
+    total = own_loss[0, 0]
     for r in range(received.shape[1]):
         logits = partner_logits(scale, bias, images, received, r)
         e, s = sigmoid_parts(logits)
         total += jnp.sum(jnp.maximum(logits, 0.0) + jnp.log1p(e))
-        weights.append(s.astype(jnp.bfloat16))
+        weights[r] = s.astype(jnp.bfloat16)
     loss[0, 0] = total
+
+
+def text_kernel(scale, weights, received, part, grad, acc, part_sem, sems):
+    part_copy = pltpu.make_async_copy(part, acc, part_sem)
+    part_copy.start()
+    weights = [weights[r] for r in range(received.shape[1])]
     add_and_write(scale, weights, received, part_copy, acc, grad, sems)
 
 
@@ -140,25 +141,6 @@
         _, s = sigmoid_parts(partner_logits(scale, bias, texts, received, r))
         weights.append(s.astype(jnp.bfloat16))
     add_and_write(scale, weights, received, part_copy, acc, grad, sems)
-
-
-def shifted(value, axis, by):
-    size = lax.axis_size(axis)
-    return lax.ppermute(value, axis, [(i, (i + by) % size) for i in range(size)])
-
-
-def sum_by_pairs(value, axis):
-    size, step = lax.axis_size(axis), 1
-    while step < size:
-        value += lax.ppermute(value, axis, [(i, i ^ step) for i in range(size)])
-        step *= 2
-    return value
-
-
-def sum_of_three(a, b, c):
-    least, most = jnp.minimum(a, b), jnp.maximum(a, b)
-    middle = jnp.maximum(least, jnp.minimum(most, c))
-    return (jnp.minimum(least, c) + jnp.maximum(most, c)) + middle
 
 
 def body(images, texts, labels, partners, logit_scale, logit_bias):
@@ -185,11 +167,11 @@
         pack_kernel,
         jax.ShapeDtypeStruct((blocks, 2, *piece), x.dtype),
         [HBM, HBM],
-        HBM,
-        [pltpu.SemaphoreType.DMA((2 * col_groups,))],
-        vmem=60,
+        VMEM,
+        [pltpu.VMEM((2, rows, width), x.dtype), pltpu.SemaphoreType.DMA((2,))],
+        vmem=56,
         moved=4 * nbytes,
-    )(y.reshape(-1, PIECE_ROWS, width), x.reshape(-1, PIECE_ROWS, width))
+    )(y, x)
     spread = exchange(packed)
 
     def regroup(which):
@@ -217,24 +199,32 @@
     )
     their_images = exchange(send_images)
 
-    loss, image_grad = local_kernel(
+    loss, weights = local_kernel(
+        loss_kernel,
+        (one, jax.ShapeDtypeStruct((rounds, rows, rows), x.dtype)),
+        [SMEM, SMEM, SMEM, VMEM, VMEM],
+        (SMEM, VMEM),
+        flops=rounds * mac,
+        moved=3 * nbytes,
+        exps=3 * rounds * rows * rows,
+    )(scale, bias, own_loss, x, their_texts)
+    image_grad = local_kernel(
         text_kernel,
-        (one, grad),
-        [SMEM, SMEM, SMEM, VMEM, VMEM, HBM],
-        (SMEM, HBM),
+        grad,
+        [SMEM, VMEM, VMEM, HBM],
+        HBM,
         scratch,
         vmem=52,
-        flops=2 * rounds * mac,
-        moved=7 * nbytes,
-        exps=3 * rounds * rows * rows,
-    )(scale, bias, own_loss, x, their_texts, image_part)
+        flops=rounds * mac,
+        moved=6 * nbytes,
+    )(scale, weights, their_texts, image_part)
     for axis in ("blk_2", "blk_0", "grp_0", "grp_1"):
-        loss = sum_by_pairs(loss, axis)
-    loss = (loss + shifted(loss, "blk_1", 6)) + (
-        shifted(loss, "blk_1", 3) + shifted(loss, "blk_1", -3)
-    )
+        loss = lax.psum(loss, axis)
+    z = lax.axis_size("blk_1")
+    loss = jnp.broadcast_to(loss.reshape(1, 1, 1), (z, 1, 128))
     their_images, loss = lax.optimization_barrier((their_images, loss))
-    loss = sum_of_three(loss, shifted(loss, "blk_1", 1), shifted(loss, "blk_1", -1))
+    loss = lax.all_to_all(loss, "blk_1", split_axis=0, concat_axis=0, tiled=True)
+    loss = jnp.sum(loss[:, :, :1], axis=0)
     loss = loss / jnp.float32(lax.axis_size(BLK) * lax.axis_size(GRP) * rows)
     text_grad = local_kernel(
         image_kernel,

time: 245 us -> 187 us (0.76)
  starting transfers between devices: 80.3 us -> 27.1 us
  Pallas kernels: 48.7 us -> 14.8 us
  blocking collectives: 58 us -> 87.4 us
  between operations: 13 us -> 3.82 us
  waiting for transfers between devices: 40.5 us -> 46.4 us
    ppermute x11 -> x0, starting transfers between devices: 61.7 us -> none  [the longest x5 32.2 us: shifted(): lax.ppermute(value, axis, [(i, (i + by) % size) for i in range(size)])]
    pallas_call x1, Pallas kernels: 36.9 us -> 2.32 us  [body(): local_kernel(pack_kernel, jax.ShapeDtypeStruct((blocks, 2, *piece), x.dty...]
    psum x0 -> x4, blocking collectives: none -> 29.4 us  [body(): loss = lax.psum(loss, axis)]
    all_to_all x1, waiting for transfers between devices: 0.01 us -> 8.94 us  [body(): their_images = exchange(send_images)]
    all_to_all x0 -> x1, starting transfers between devices: none -> 8.53 us  [body(): lax.all_to_all(loss, 'blk_1', split_axis=0, concat_axis=0, tiled=True)]
    ppermute x11 -> x0, waiting for transfers between devices: 7.44 us -> none  [the longest x6 6.86 us: sum_by_pairs(): value += lax.ppermute(value, axis, [(i, i ^ step) for i in range(size)])]
    all_to_all x0 -> x1, waiting for transfers between devices: none -> 4.47 us  [body(): lax.all_to_all(loss, 'blk_1', split_axis=0, concat_axis=0, tiled=True)]
  transfers between devices with their start and end apart: 13 -> 3, of which waited for: 9 -> 3; matrix products, arithmetic and copies ran while one was open for 0% -> 0% of each run, Pallas kernels for 4% -> 6%
where the time goes in v3:
time: 187 us; the launch traced here: 186 us
  blocking collectives  87.4 us (47%)
  waiting for transfers between devices  46.4 us (25%)
  starting transfers between devices  27.1 us (14%)
  Pallas kernels  14.8 us (8%)
  local copies, waits for them, and re-layouts  5.73 us (3%)
  between operations  3.82 us (2%)
    all_to_all x1, blocking collectives, body(): spread = exchange(packed)  58 us
    all_to_all x1, waiting for transfers between devices, body(): their_texts = exchange(regroup(0))  33 us
    psum x4, blocking collectives, body(): loss = lax.psum(loss, axis)  29.4 us
    all_to_all x1, starting transfers between devices, body(): their_texts = exchange(regroup(0))  9.33 us
    all_to_all x1, starting transfers between devices, body(): their_images = exchange(send_images)  9.2 us
    all_to_all x1, waiting for transfers between devices, body(): their_images = exchange(send_images)  8.94 us
    all_to_all x1, starting transfers between devices, body(): lax.all_to_all(loss, 'blk_1', split_axis=0, concat_axis=0, tiled=True)  8.53 us
    all_to_all x1, waiting for transfers between devices, body(): lax.all_to_all(loss, 'blk_1', split_axis=0, concat_axis=0, tiled=True)  4.47 us
  transfers between devices with their start and end apart: 3, of which 3 were waited for; matrix products, arithmetic and copies ran while one was open for 0% of the time, Pallas kernels for 6%

profile of v3, /device:TPU:6, one launch (start us, length us, event | category | flops | bytes accessed | tf_op | source)
XLA Modules:
  0.0 185.9 jit_solution(7151469340921835602)
XLA Ops:
  0.6 2.3 %shard_map.85 = bf16[48,2,16,384]{3,2,1,0:T(8,128)(2,1)} custom-call(bf16[256,1152]{1,0:T(8,128)(2,1)} %bitcast.15, bf16[256,1152]{1,0:T(8,128)(2,1)} %bitcast.18), custom_call_target="tpu_custom_call" | custom-call | bytes 2359296 | tf_op jit(solution)/shard_map/pallas_call | solution.py:166
  3.0 58.0 %all_to_all.20.spread = bf16[48,2,16,384]{3,2,1,0:T(8,128)(2,1)S(1)} all-to-all(bf16[48,2,16,384]{3,2,1,0:T(8,128)(2,1)} %shard_map.85), channel_id=1, replica_groups=mesh['blk_0'=2,'blk_1'=12,'blk_2'=2,'grp_0'=4,'grp_1'=4] {'blk_0','blk_1..., dimensions={0} | all-to-all | bytes 2359296 | tf_op jit(solution)/shard_map/all_to_all | solution.py:175
  61.0 1.7 shard_map.88
  62.7 9.3 %all-to-all-start.1 = ((bf16[48,2,16,384]{3,2,1,0:T(8,128)(2,1)}), bf16[48,2,16,384]{3,2,1,0:T(8,128)(2,1)S(1)}, u32[]{:S(2)}, u32[]{:S(2)}) async-start(bf16[48,2,16,384]{3,2,1,0:T(8,128)(2,1)} %shard_map.88), calls=%async_computation.1 | async-start | bytes 2359296 | tf_op jit(solution)/shard_map/all_to_all | solution.py:196
  73.3 0.8 copy.11.labels
  74.2 0.9 copy-done.6
  75.1 1.4 shard_map.87
  76.4 1.0 copy-done.2
  77.5 1.0 copy-done.3
  78.5 1.7 shard_map.86
  80.2 33.0 %all-to-all-done.1.received = bf16[48,2,16,384]{3,2,1,0:T(8,128)(2,1)S(1)} async-done(((bf16[48,2,16,384]{3,2,1,0:T(8,128)(2,1)}), bf16[48,2,16,384]{3,2,1,0:T(8,128)(2,1)S(1)}, u32[]{:S(2)}, u32[]{:S(2)}) %all-to-all-start.1) | async-done | bytes 1179680 | tf_op jit(solution)/shard_map/all_to_all | solution.py:196
  113.2 9.2 %all-to-all-start.2 = ((bf16[48,2,16,384]{3,2,1,0:T(8,128)(2,1)}), bf16[48,2,16,384]{3,2,1,0:T(8,128)(2,1)S(1)}, u32[]{:S(2)}, u32[]{:S(2)}) async-start(bf16[48,2,16,384]{3,2,1,0:T(8,128)(2,1)} %shard_map.86), calls=%async_computation.2 | async-start | bytes 2359296 | tf_op jit(solution)/shard_map/all_to_all | solution.py:200
  122.4 2.1 %shard_map.89 = (f32[1,1]{1,0:T(1,128)}, bf16[2,256,256]{2,1,0:T(8,128)(2,1)S(1)}) custom-call(f32[1,1]{1,0:T(1,128)} %bitcast.9.scale, f32[1,1]{1,0:T(1,128)} %bitcast.13.bias, f32[1,1]{1,0:T(1,128)} %get-tuple-element.17.own_loss, bf16[256,1152]{1,0:T(8,128)(2,1)S(1)} %bitcast.20, bf16[48,2,16,384]{3,2,1,0:T(8,128)(2,1)S(1)} %all-to-all-done.1.received), custom_call_target="tpu_custom_call" | custom-call | flops 301989888 | bytes 1769472 | tf_op jit(solution)/shard_map/pallas_call | solution.py:202
  124.6 0.7 copy-done.4
  125.3 3.1 %psum.28 = f32[1,1]{1,0:T(1,128)} all-reduce(f32[1,1]{1,0:T(1,128)} %get-tuple-element.21), channel_id=1, replica_groups=mesh['blk_0'=2,'blk_1'=12,'blk_2'=2,'grp_0'=4,'grp_1'=4] {'blk_2'}, use_global_device_ids=true, to_apply=%region_0.0 | all-reduce | flops 1 | bytes 8 | tf_op jit(solution)/shard_map/psum | solution.py:222
  128.3 5.6 %psum.29 = f32[1,1]{1,0:T(1,128)} all-reduce(f32[1,1]{1,0:T(1,128)} %psum.28), channel_id=1, replica_groups=mesh['blk_0'=2,'blk_1'=12,'blk_2'=2,'grp_0'=4,'grp_1'=4] {'blk_0'}, use_global_device_ids=true, to_apply=%region_1.0 | all-reduce | flops 1 | bytes 8 | tf_op jit(solution)/shard_map/psum | solution.py:222
  133.9 8.1 %psum.30 = f32[1,1]{1,0:T(1,128)} all-reduce(f32[1,1]{1,0:T(1,128)} %psum.29), channel_id=1, replica_groups=mesh['blk_0'=2,'blk_1'=12,'blk_2'=2,'grp_0'=4,'grp_1'=4] {'grp_0'}, use_global_device_ids=true, to_apply=%region_2.0 | all-reduce | flops 1 | bytes 8 | tf_op jit(solution)/shard_map/psum | solution.py:222
  142.0 12.6 %psum.31 = f32[]{:T(128)} all-reduce(f32[]{:T(128)} %bitcast.6), channel_id=1, replica_groups=mesh['blk_0'=2,'blk_1'=12,'blk_2'=2,'grp_0'=4,'grp_1'=4] {'grp_1'}, use_global_device_ids=true, to_apply=%region_3.0 | all-reduce | flops 1 | bytes 8 | tf_op jit(solution)/shard_map/psum | solution.py:222
  154.6 8.9 %all-to-all-done.2.received = bf16[48,2,16,384]{3,2,1,0:T(8,128)(2,1)S(1)} async-done(((bf16[48,2,16,384]{3,2,1,0:T(8,128)(2,1)}), bf16[48,2,16,384]{3,2,1,0:T(8,128)(2,1)S(1)}, u32[]{:S(2)}, u32[]{:S(2)}) %all-to-all-start.2) | async-done | bytes 1179680 | tf_op jit(solution)/shard_map/all_to_all | solution.py:200
  163.6 1.2 broadcast_in_dim.15
  164.8 8.5 %all-to-all-start.3 = ((f32[12,1,128]{2,1,0:T(1,128)}), f32[12,1,128]{2,1,0:T(1,128)S(1)}, u32[]{:S(2)}, u32[]{:S(2)}) async-start(f32[12,1,128]{2,1,0:T(1,128)} %broadcast_in_dim.15), calls=%async_computation.3 | async-start | bytes 12288 | tf_op jit(solution)/shard_map/all_to_all | solution.py:226
  173.4 3.0 %shard_map.91 = f32[256,1152]{1,0:T(8,128)} custom-call(f32[1,1]{1,0:T(1,128)} %bitcast.11.scale, f32[1,1]{1,0:T(1,128)} %bitcast.14.bias, bf16[256,1152]{1,0:T(8,128)(2,1)S(1)} %bitcast.17, bf16[48,2,16,384]{3,2,1,0:T(8,128)(2,1)S(1)} %all-to-all-done.2.received, f32[256,1152]{1,0:T(8,128)} %copy-done.2), custom_call_target="tpu_custom_call" | custom-call | flops 603979776 | bytes 4128768 | tf_op jit(solution)/shard_map/pallas_call | solution.py:229
  176.4 2.6 %shard_map.90 = f32[256,1152]{1,0:T(8,128)} custom-call(f32[1,1]{1,0:T(1,128)} %bitcast.10.scale, bf16[2,256,256]{2,1,0:T(8,128)(2,1)S(1)} %copy-done.5, bf16[48,2,16,384]{3,2,1,0:T(8,128)(2,1)S(1)} %all-to-all-done.1.received, f32[256,1152]{1,0:T(8,128)} %copy-done.3), custom_call_target="tpu_custom_call" | custom-call | flops 301989888 | bytes 3538944 | tf_op jit(solution)/shard_map/pallas_call | solution.py:211
  179.0 4.5 %all-to-all-done.3 = f32[12,1,128]{2,1,0:T(1,128)S(1)} async-done(((f32[12,1,128]{2,1,0:T(1,128)}), f32[12,1,128]{2,1,0:T(1,128)S(1)}, u32[]{:S(2)}, u32[]{:S(2)}) %all-to-all-start.3) | async-done | bytes 6176 | tf_op jit(solution)/shard_map/all_to_all | solution.py:226
  (15 shorter events, 0.6 us)
Async XLA Ops:
  3.0 58.0 %copy-start.7 = (s32[2,48]{1,0:T(2,128)S(1)}, s32[2,48]{1,0:T(2,128)}, u32[]{:S(2)}) copy-start(s32[2,48]{1,0:T(2,128)} %partners.3) | copy-start | bytes 1156
  62.7 10.6 %copy-start.8 = (s32[1,1,256]{2,1,0:T(1,128)S(1)}, s32[1,1,256]{2,1,0:T(1,128)}, u32[]{:S(2)}) copy-start(s32[1,1,256]{2,1,0:T(1,128)} %param.8) | copy-start | bytes 3076
  62.7 11.5 %copy-start = (bf16[1,256,1152]{2,1,0:T(8,128)(2,1)S(1)}, bf16[1,256,1152]{2,1,0:T(8,128)(2,1)}, u32[]{:S(2)}) copy-start(bf16[1,256,1152]{2,1,0:T(8,128)(2,1)} %param.7) | copy-start | bytes 1769476
  62.7 11.5 %copy-start.1 = (bf16[1,256,1152]{2,1,0:T(8,128)(2,1)S(1)}, bf16[1,256,1152]{2,1,0:T(8,128)(2,1)}, u32[]{:S(2)}) copy-start(bf16[1,256,1152]{2,1,0:T(8,128)(2,1)} %param.6) | copy-start | bytes 1769476
  62.7 50.5 %all-to-all-start.1 = ((bf16[48,2,16,384]{3,2,1,0:T(8,128)(2,1)}), bf16[48,2,16,384]{3,2,1,0:T(8,128)(2,1)S(1)}, u32[]{:S(2)}, u32[]{:S(2)}) async-start(bf16[48,2,16,384]{3,2,1,0:T(8,128)(2,1)} %shard_map.88), calls=%async_computation.1 | async-start | bytes 2359296 | tf_op jit(solution)/shard_map/all_to_all | solution.py:196
  74.2 0.9 copy-start.6
  76.4 1.1 copy-start.2
  77.5 1.0 copy-start.3
  113.2 50.4 %all-to-all-start.2 = ((bf16[48,2,16,384]{3,2,1,0:T(8,128)(2,1)}), bf16[48,2,16,384]{3,2,1,0:T(8,128)(2,1)S(1)}, u32[]{:S(2)}, u32[]{:S(2)}) async-start(bf16[48,2,16,384]{3,2,1,0:T(8,128)(2,1)} %shard_map.86), calls=%async_computation.2 | async-start | bytes 2359296 | tf_op jit(solution)/shard_map/all_to_all | solution.py:200
  124.5 0.7 copy-start.4
  164.8 18.7 %all-to-all-start.3 = ((f32[12,1,128]{2,1,0:T(1,128)}), f32[12,1,128]{2,1,0:T(1,128)S(1)}, u32[]{:S(2)}, u32[]{:S(2)}) async-start(f32[12,1,128]{2,1,0:T(1,128)} %broadcast_in_dim.15), calls=%async_computation.3 | async-start | bytes 12288 | tf_op jit(solution)/shard_map/all_to_all | solution.py:226
  173.3 3.0 %copy-start.5 = (bf16[2,256,256]{2,1,0:T(8,128)(2,1)S(1)}, bf16[2,256,256]{2,1,0:T(8,128)(2,1)}, u32[]{:S(2)}) copy-start(bf16[2,256,256]{2,1,0:T(8,128)(2,1)} %copy-done.4) | copy-start | bytes 786436

commit v4 on v3

--- a/solution.py
+++ b/solution.py
@@ -35,19 +35,29 @@
     return pl.ds(col * PIECE_COLS, PIECE_COLS)
 
 
-def pack_kernel(texts, images, packed, rows, sems):
+def pack_kernel(texts, images, packed, rows, filled, in_sems, out_sems):
     copies = [
-        pltpu.make_async_copy(block, rows.at[which], sems.at[which])
+        pltpu.make_async_copy(block, rows.at[which], in_sems.at[which])
         for which, block in enumerate((texts, images))
     ]
     for copy in copies:
         copy.start()
+    for copy in copies:
+        copy.wait()
     row_groups = ROWS // PIECE_ROWS
-    for which, copy in enumerate(copies):
+    sent = []
+    for col in range(packed.shape[0] // row_groups):
+        for row in range(row_groups):
+            for which in range(len(copies)):
+                filled[col * row_groups + row, which] = rows[
+                    which, pl.ds(row * PIECE_ROWS, PIECE_ROWS), columns_of(col)
+                ]
+        part = pl.ds(col * row_groups, row_groups)
+        copy = pltpu.make_async_copy(filled.at[part], packed.at[part], out_sems.at[col])
+        copy.start()
+        sent.append(copy)
+    for copy in sent:
         copy.wait()
-        for index in range(packed.shape[0]):
-            col, row = divmod(index, row_groups)
-            packed[index, which] = rows[which, pl.ds(row * PIECE_ROWS, PIECE_ROWS), columns_of(col)]
 
 
 def regroup_kernel(which, partners, spread, send):
@@ -116,29 +126,20 @@
         copy.wait()
 
 
-def loss_kernel(scale, bias, own_loss, images, received, loss, weights):
-    total = own_loss[0, 0]
+def loss_kernel(scale, bias, own_loss, images, received, loss):
+    terms = jnp.zeros((ROWS, ROWS), jnp.float32)
     for r in range(received.shape[1]):
         logits = partner_logits(scale, bias, images, received, r)
-        e, s = sigmoid_parts(logits)
-        total += jnp.sum(jnp.maximum(logits, 0.0) + jnp.log1p(e))
-        weights[r] = s.astype(jnp.bfloat16)
-    loss[0, 0] = total
-
-
-def text_kernel(scale, weights, received, part, grad, acc, part_sem, sems):
-    part_copy = pltpu.make_async_copy(part, acc, part_sem)
-    part_copy.start()
-    weights = [weights[r] for r in range(received.shape[1])]
-    add_and_write(scale, weights, received, part_copy, acc, grad, sems)
-
-
-def image_kernel(scale, bias, texts, received, part, grad, acc, part_sem, sems):
+        terms += jnp.maximum(logits, 0.0) + jnp.log1p(jnp.exp(-jnp.abs(logits)))
+    loss[...] = jnp.full(loss.shape, own_loss[0, 0] + jnp.sum(terms), jnp.float32)
+
+
+def grad_kernel(scale, bias, own, received, part, grad, acc, part_sem, sems):
     part_copy = pltpu.make_async_copy(part, acc, part_sem)
     part_copy.start()
     weights = []
     for r in range(received.shape[1]):
-        _, s = sigmoid_parts(partner_logits(scale, bias, texts, received, r))
+        _, s = sigmoid_parts(partner_logits(scale, bias, own, received, r))
         weights.append(s.astype(jnp.bfloat16))
     add_and_write(scale, weights, received, part_copy, acc, grad, sems)
 
@@ -163,12 +164,18 @@
         lax.all_to_all, axis_name=BLK, split_axis=0, concat_axis=0, tiled=True
     )
 
+    pieces = jax.ShapeDtypeStruct((blocks, 2, *piece), x.dtype)
     packed = local_kernel(
         pack_kernel,
-        jax.ShapeDtypeStruct((blocks, 2, *piece), x.dtype),
+        pieces,
         [HBM, HBM],
-        VMEM,
-        [pltpu.VMEM((2, rows, width), x.dtype), pltpu.SemaphoreType.DMA((2,))],
+        HBM,
+        [
+            pltpu.VMEM((2, rows, width), x.dtype),
+            pltpu.VMEM(pieces.shape, x.dtype),
+            pltpu.SemaphoreType.DMA((2,)),
+            pltpu.SemaphoreType.DMA((col_groups,)),
+        ],
         vmem=56,
         moved=4 * nbytes,
     )(y, x)
@@ -177,7 +184,7 @@
     def regroup(which):
         return local_kernel(
             functools.partial(regroup_kernel, which),
-            jax.ShapeDtypeStruct((blocks, rounds, *piece), x.dtype),
+            pieces,
             [SMEM, VMEM],
             VMEM,
             moved=4 * nbytes,
@@ -194,50 +201,43 @@
     )(scale, bias, x, y, labels[0].reshape(rows, 1))
 
     their_texts = exchange(regroup(0))
-    send_images, own_loss, image_part, text_part = lax.optimization_barrier(
-        (regroup(1), own_loss, image_part, text_part)
-    )
-    their_images = exchange(send_images)
-
-    loss, weights = local_kernel(
+    z = lax.axis_size("blk_1")
+    loss = local_kernel(
         loss_kernel,
-        (one, jax.ShapeDtypeStruct((rounds, rows, rows), x.dtype)),
+        jax.ShapeDtypeStruct((z, 1, 128), jnp.float32),
         [SMEM, SMEM, SMEM, VMEM, VMEM],
-        (SMEM, VMEM),
+        VMEM,
         flops=rounds * mac,
         moved=3 * nbytes,
-        exps=3 * rounds * rows * rows,
+        exps=2 * rounds * rows * rows,
     )(scale, bias, own_loss, x, their_texts)
-    image_grad = local_kernel(
-        text_kernel,
-        grad,
-        [SMEM, VMEM, VMEM, HBM],
-        HBM,
-        scratch,
-        vmem=52,
-        flops=rounds * mac,
-        moved=6 * nbytes,
-    )(scale, weights, their_texts, image_part)
+    loss = lax.all_to_all(loss, "blk_1", split_axis=0, concat_axis=0, tiled=True)
+    send_images, loss, image_part, text_part = lax.optimization_barrier(
+        (regroup(1), loss, image_part, text_part)
+    )
+    their_images = exchange(send_images)
+
+    def gradient(own, theirs, part):
+        return local_kernel(
+            grad_kernel,
+            grad,
+            [SMEM, SMEM, VMEM, VMEM, HBM],
+            HBM,
+            scratch,
+            vmem=52,
+            flops=2 * rounds * mac,
+            moved=7 * nbytes,
+            exps=2 * rounds * rows * rows,
+        )(scale, bias, own, theirs, part)
+
+    image_grad = gradient(x, their_texts, image_part)
+    loss = jnp.sum(loss[:, 0, 0])
     for axis in ("blk_2", "blk_0", "grp_0", "grp_1"):
         loss = lax.psum(loss, axis)
-    z = lax.axis_size("blk_1")
-    loss = jnp.broadcast_to(loss.reshape(1, 1, 1), (z, 1, 128))
-    their_images, loss = lax.optimization_barrier((their_images, loss))
-    loss = lax.all_to_all(loss, "blk_1", split_axis=0, concat_axis=0, tiled=True)
-    loss = jnp.sum(loss[:, :, :1], axis=0)
     loss = loss / jnp.float32(lax.axis_size(BLK) * lax.axis_size(GRP) * rows)
-    text_grad = local_kernel(
-        image_kernel,
-        grad,
-        [SMEM, SMEM, VMEM, VMEM, HBM],
-        HBM,
-        scratch,
-        vmem=52,
-        flops=2 * rounds * mac,
-        moved=7 * nbytes,
-        exps=2 * rounds * rows * rows,
-    )(scale, bias, y, their_images, text_part)
-    return image_grad[None], text_grad[None], loss[0, 0]
+    their_images, loss, image_grad = lax.optimization_barrier((their_images, loss, image_grad))
+    text_grad = gradient(y, their_images, text_part)
+    return image_grad[None], text_grad[None], loss
 
 
 def solution(mesh):

time: 187 us -> 187 us (level); the launches traced: 186 us -> 184 us
  starting transfers between devices: 27.1 us -> 22.4 us
  waiting for transfers between devices: 46.4 us -> 50.2 us
    all_to_all x1, starting transfers between devices: 9.2 us -> 4.58 us  [body(): their_images = exchange(send_images)]
    all_to_all x1, waiting for transfers between devices: 4.47 us -> 8.28 us  [body(): lax.all_to_all(loss, 'blk_1', split_axis=0, concat_axis=0, tiled=True)]
  transfers between devices with their start and end apart: 3 -> 3, of which waited for: 3 -> 3; matrix products, arithmetic and copies ran while one was open for 0% -> 1% of each run, Pallas kernels for 6% -> 3%
where the time goes in v4:
time: 187 us; the launch traced here: 184 us
  blocking collectives  87.7 us (47%)
  waiting for transfers between devices  50.2 us (27%)
  starting transfers between devices  22.4 us (12%)
  Pallas kernels  13.2 us (7%)
  local copies, waits for them, and re-layouts  5.8 us (3%)
  between operations  3.82 us (2%)
    all_to_all x1, blocking collectives, body(): spread = exchange(packed)  58 us
    all_to_all x1, waiting for transfers between devices, body(): their_texts = exchange(regroup(0))  34.7 us
    psum x4, blocking collectives, body(): loss = lax.psum(loss, axis)  29.7 us
    all_to_all x1, starting transfers between devices, body(): their_texts = exchange(regroup(0))  9.33 us
    all_to_all x1, starting transfers between devices, body(): lax.all_to_all(loss, 'blk_1', split_axis=0, concat_axis=0, tiled=True)  8.53 us
    all_to_all x1, waiting for transfers between devices, body(): lax.all_to_all(loss, 'blk_1', split_axis=0, concat_axis=0, tiled=True)  8.28 us
    all_to_all x1, waiting for transfers between devices, body(): their_images = exchange(send_images)  7.18 us
    pallas_call x2, Pallas kernels, gradient(): local_kernel(grad_kernel, grad, [SMEM, SMEM, VMEM, VMEM, HBM], HBM, scrat...  5.97 us
  transfers between devices with their start and end apart: 3, of which 3 were waited for; matrix products, arithmetic and copies ran while one was open for 1% of the time, Pallas kernels for 3%

profile of v4, /device:TPU:6, one launch (start us, length us, event | category | flops | bytes accessed | tf_op | source)
XLA Modules:
  0.0 183.8 jit_solution(2141794774417976077)
XLA Ops:
  0.6 2.3 %shard_map.85 = bf16[48,2,16,384]{3,2,1,0:T(8,128)(2,1)} custom-call(bf16[256,1152]{1,0:T(8,128)(2,1)} %bitcast.19, bf16[256,1152]{1,0:T(8,128)(2,1)} %bitcast.15), custom_call_target="tpu_custom_call" | custom-call | bytes 2359296 | tf_op jit(solution)/shard_map/pallas_call | solution.py:168
  3.0 58.0 %all_to_all.20.spread = bf16[48,2,16,384]{3,2,1,0:T(8,128)(2,1)S(1)} all-to-all(bf16[48,2,16,384]{3,2,1,0:T(8,128)(2,1)} %shard_map.85), channel_id=1, replica_groups=mesh['blk_0'=2,'blk_1'=12,'blk_2'=2,'grp_0'=4,'grp_1'=4] {'blk_0','blk_1..., dimensions={0} | all-to-all | bytes 2359296 | tf_op jit(solution)/shard_map/all_to_all | solution.py:182
  61.0 0.7 shard_map.88
  61.7 1.0 copy-done.2
  62.7 9.3 %all-to-all-start.1 = ((bf16[48,2,16,384]{3,2,1,0:T(8,128)(2,1)}), bf16[48,2,16,384]{3,2,1,0:T(8,128)(2,1)S(1)}, u32[]{:S(2)}, u32[]{:S(2)}) async-start(bf16[48,2,16,384]{3,2,1,0:T(8,128)(2,1)} %copy-done.2), calls=%async_computation.1 | async-start | bytes 2359296 | tf_op jit(solution)/shard_map/all_to_all | solution.py:203
  73.4 0.8 copy.9.labels
  74.2 0.9 copy-done.6
  75.1 1.4 shard_map.87
  76.4 1.0 copy-done.4
  77.4 1.1 copy-done.5
  78.5 34.7 %all-to-all-done.1.received = bf16[48,2,16,384]{3,2,1,0:T(8,128)(2,1)S(1)} async-done(((bf16[48,2,16,384]{3,2,1,0:T(8,128)(2,1)}), bf16[48,2,16,384]{3,2,1,0:T(8,128)(2,1)S(1)}, u32[]{:S(2)}, u32[]{:S(2)}) %all-to-all-start.1) | async-done | bytes 1179680 | tf_op jit(solution)/shard_map/all_to_all | solution.py:203
  113.2 2.2 %shard_map.89 = f32[12,1,128]{2,1,0:T(1,128)} custom-call(f32[1,1]{1,0:T(1,128)} %bitcast.8.scale, f32[1,1]{1,0:T(1,128)} %bitcast.12.bias, f32[1,1]{1,0:T(1,128)} %get-tuple-element.13.own_loss, bf16[256,1152]{1,0:T(8,128)(2,1)S(1)} %bitcast.17, bf16[48,2,16,384]{3,2,1,0:T(8,128)(2,1)S(1)} %all-to-all-done.1.received), custom_call_target="tpu_custom_call" | custom-call | flops 301989888 | bytes 1769472 | tf_op jit(solution)/shard_map/pallas_call | solution.py:205
  115.4 8.5 %all-to-all-start.2 = ((f32[12,1,128]{2,1,0:T(1,128)}), f32[12,1,128]{2,1,0:T(1,128)S(1)}, u32[]{:S(2)}, u32[]{:S(2)}) async-start(f32[12,1,128]{2,1,0:T(1,128)} %shard_map.89), calls=%async_computation.2 | async-start | bytes 12288 | tf_op jit(solution)/shard_map/all_to_all | solution.py:214
  124.0 0.7 shard_map.86
  124.7 1.0 copy-done.1
  125.7 8.3 %all-to-all-done.2 = f32[12,1,128]{2,1,0:T(1,128)S(1)} async-done(((f32[12,1,128]{2,1,0:T(1,128)}), f32[12,1,128]{2,1,0:T(1,128)S(1)}, u32[]{:S(2)}, u32[]{:S(2)}) %all-to-all-start.2) | async-done | bytes 6176 | tf_op jit(solution)/shard_map/all_to_all | solution.py:214
  133.9 4.6 %all-to-all-start.3 = ((bf16[48,2,16,384]{3,2,1,0:T(8,128)(2,1)}), bf16[48,2,16,384]{3,2,1,0:T(8,128)(2,1)S(1)}, u32[]{:S(2)}, u32[]{:S(2)}) async-start(bf16[48,2,16,384]{3,2,1,0:T(8,128)(2,1)} %copy-done.1), calls=%async_computation.3 | async-start | bytes 2359296 | tf_op jit(solution)/shard_map/all_to_all | solution.py:218
  139.1 3.1 %psum.28 = f32[]{:T(128)} all-reduce(f32[]{:T(128)} %slice_reduce_fusion), channel_id=1, replica_groups=mesh['blk_0'=2,'blk_1'=12,'blk_2'=2,'grp_0'=4,'grp_1'=4] {'blk_2'}, use_global_device_ids=true, to_apply=%region_1.0 | all-reduce | flops 1 | bytes 8 | tf_op jit(solution)/shard_map/psum | solution.py:236
  142.2 5.9 %psum.29 = f32[]{:T(128)} all-reduce(f32[]{:T(128)} %psum.28), channel_id=1, replica_groups=mesh['blk_0'=2,'blk_1'=12,'blk_2'=2,'grp_0'=4,'grp_1'=4] {'blk_0'}, use_global_device_ids=true, to_apply=%region_2.0 | all-reduce | flops 1 | bytes 8 | tf_op jit(solution)/shard_map/psum | solution.py:236
  148.2 8.1 %psum.30 = f32[]{:T(128)} all-reduce(f32[]{:T(128)} %psum.29), channel_id=1, replica_groups=mesh['blk_0'=2,'blk_1'=12,'blk_2'=2,'grp_0'=4,'grp_1'=4] {'grp_0'}, use_global_device_ids=true, to_apply=%region_3.0 | all-reduce | flops 1 | bytes 8 | tf_op jit(solution)/shard_map/psum | solution.py:236
  156.3 12.6 %psum.31 = f32[]{:T(128)} all-reduce(f32[]{:T(128)} %psum.30), channel_id=1, replica_groups=mesh['blk_0'=2,'blk_1'=12,'blk_2'=2,'grp_0'=4,'grp_1'=4] {'grp_1'}, use_global_device_ids=true, to_apply=%region_4.0 | all-reduce | flops 1 | bytes 8 | tf_op jit(solution)/shard_map/psum | solution.py:236
  169.5 3.0 %shard_map.90 = f32[256,1152]{1,0:T(8,128)} custom-call(f32[1,1]{1,0:T(1,128)} %bitcast.9.scale, f32[1,1]{1,0:T(1,128)} %bitcast.13.bias, bf16[256,1152]{1,0:T(8,128)(2,1)S(1)} %bitcast.18, bf16[48,2,16,384]{3,2,1,0:T(8,128)(2,1)S(1)} %all-to-all-done.1.received, f32[256,1152]{1,0:T(8,128)} %copy-done.5), custom_call_target="tpu_custom_call" | custom-call | flops 603979776 | bytes 4128768 | tf_op jit(solution)/shard_map/pallas_call | solution.py:221
  172.5 7.2 %all-to-all-done.3.received = bf16[48,2,16,384]{3,2,1,0:T(8,128)(2,1)S(1)} async-done(((bf16[48,2,16,384]{3,2,1,0:T(8,128)(2,1)}), bf16[48,2,16,384]{3,2,1,0:T(8,128)(2,1)S(1)}, u32[]{:S(2)}, u32[]{:S(2)}) %all-to-all-start.3) | async-done | bytes 1179680 | tf_op jit(solution)/shard_map/all_to_all | solution.py:218
  179.7 3.0 %shard_map.91 = f32[256,1152]{1,0:T(8,128)} custom-call(f32[1,1]{1,0:T(1,128)} %bitcast.10.scale, f32[1,1]{1,0:T(1,128)} %bitcast.14.bias, bf16[256,1152]{1,0:T(8,128)(2,1)S(1)} %bitcast.21, bf16[48,2,16,384]{3,2,1,0:T(8,128)(2,1)S(1)} %all-to-all-done.3.received, f32[256,1152]{1,0:T(8,128)} %copy-done.4), custom_call_target="tpu_custom_call" | custom-call | flops 603979776 | bytes 4128768 | tf_op jit(solution)/shard_map/pallas_call | solution.py:221
  (14 shorter events, 0.6 us)
Async XLA Ops:
  3.0 58.0 %copy-start.7 = (s32[2,48]{1,0:T(2,128)S(1)}, s32[2,48]{1,0:T(2,128)}, u32[]{:S(2)}) copy-start(s32[2,48]{1,0:T(2,128)} %partners.3) | copy-start | bytes 1156
  61.7 1.0 copy-start.2
  62.7 10.6 %copy-start.8 = (s32[1,1,256]{2,1,0:T(1,128)S(1)}, s32[1,1,256]{2,1,0:T(1,128)}, u32[]{:S(2)}) copy-start(s32[1,1,256]{2,1,0:T(1,128)} %param.8) | copy-start | bytes 3076
  62.7 11.5 %copy-start = (bf16[1,256,1152]{2,1,0:T(8,128)(2,1)S(1)}, bf16[1,256,1152]{2,1,0:T(8,128)(2,1)}, u32[]{:S(2)}) copy-start(bf16[1,256,1152]{2,1,0:T(8,128)(2,1)} %param.6) | copy-start | bytes 1769476
  62.7 11.5 %copy-start.3 = (bf16[1,256,1152]{2,1,0:T(8,128)(2,1)S(1)}, bf16[1,256,1152]{2,1,0:T(8,128)(2,1)}, u32[]{:S(2)}) copy-start(bf16[1,256,1152]{2,1,0:T(8,128)(2,1)} %param.7) | copy-start | bytes 1769476
  62.7 50.5 %all-to-all-start.1 = ((bf16[48,2,16,384]{3,2,1,0:T(8,128)(2,1)}), bf16[48,2,16,384]{3,2,1,0:T(8,128)(2,1)S(1)}, u32[]{:S(2)}, u32[]{:S(2)}) async-start(bf16[48,2,16,384]{3,2,1,0:T(8,128)(2,1)} %copy-done.2), calls=%async_computation.1 | async-start | bytes 2359296 | tf_op jit(solution)/shard_map/all_to_all | solution.py:203
  74.2 0.9 copy-start.6
  76.4 1.0 copy-start.4
  77.4 1.1 copy-start.5
  115.4 18.5 %all-to-all-start.2 = ((f32[12,1,128]{2,1,0:T(1,128)}), f32[12,1,128]{2,1,0:T(1,128)S(1)}, u32[]{:S(2)}, u32[]{:S(2)}) async-start(f32[12,1,128]{2,1,0:T(1,128)} %shard_map.89), calls=%async_computation.2 | async-start | bytes 12288 | tf_op jit(solution)/shard_map/all_to_all | solution.py:214
  124.6 1.0 copy-start.1
  133.9 45.8 %all-to-all-start.3 = ((bf16[48,2,16,384]{3,2,1,0:T(8,128)(2,1)}), bf16[48,2,16,384]{3,2,1,0:T(8,128)(2,1)S(1)}, u32[]{:S(2)}, u32[]{:S(2)}) async-start(bf16[48,2,16,384]{3,2,1,0:T(8,128)(2,1)} %copy-done.1), calls=%async_computation.3 | async-start | bytes 2359296 | tf_op jit(solution)/shard_map/all_to_all | solution.py:218

commit v5 on v4

--- a/solution.py
+++ b/solution.py
@@ -131,7 +131,7 @@
     for r in range(received.shape[1]):
         logits = partner_logits(scale, bias, images, received, r)
         terms += jnp.maximum(logits, 0.0) + jnp.log1p(jnp.exp(-jnp.abs(logits)))
-    loss[...] = jnp.full(loss.shape, own_loss[0, 0] + jnp.sum(terms), jnp.float32)
+    loss[0, 0] = own_loss[0, 0] + jnp.sum(terms)
 
 
 def grad_kernel(scale, bias, own, received, part, grad, acc, part_sem, sems):
@@ -142,6 +142,30 @@
         _, s = sigmoid_parts(partner_logits(scale, bias, own, received, r))
         weights.append(s.astype(jnp.bfloat16))
     add_and_write(scale, weights, received, part_copy, acc, grad, sems)
+
+
+def last_kernel(count, a, b, c, *refs):
+    operands, loss, rest = refs[:5], refs[5], refs[6:]
+    x, y, z = a[0, 0], b[0, 0], c[0, 0]
+    least, most = jnp.minimum(x, y), jnp.maximum(x, y)
+    middle = jnp.maximum(least, jnp.minimum(most, z))
+    loss[0, 0] = ((jnp.minimum(least, z) + jnp.maximum(most, z)) + middle) / count
+    grad_kernel(*operands, *rest)
+
+
+def shifted(value, by):
+    size = lax.axis_size("blk_1")
+    return lax.ppermute(value, "blk_1", [(i, (i + by) % size) for i in range(size)])
+
+
+def shifted_beside(value, by):
+    size, across = lax.axis_size("blk_1"), lax.axis_size("grp_0")
+    pairs = [
+        (i * across + j, (i + by) % size * across + (j + 1) % across)
+        for i in range(size)
+        for j in range(across)
+    ]
+    return lax.ppermute(value, ("blk_1", "grp_0"), pairs)
 
 
 def body(images, texts, labels, partners, logit_scale, logit_bias):
@@ -200,44 +224,45 @@
         exps=3 * rows * rows,
     )(scale, bias, x, y, labels[0].reshape(rows, 1))
 
-    their_texts = exchange(regroup(0))
-    z = lax.axis_size("blk_1")
+    their_texts, send_images, own_loss, image_part, text_part = lax.optimization_barrier(
+        (exchange(regroup(0)), regroup(1), own_loss, image_part, text_part)
+    )
     loss = local_kernel(
         loss_kernel,
-        jax.ShapeDtypeStruct((z, 1, 128), jnp.float32),
+        one,
         [SMEM, SMEM, SMEM, VMEM, VMEM],
-        VMEM,
+        SMEM,
         flops=rounds * mac,
         moved=3 * nbytes,
         exps=2 * rounds * rows * rows,
     )(scale, bias, own_loss, x, their_texts)
-    loss = lax.all_to_all(loss, "blk_1", split_axis=0, concat_axis=0, tiled=True)
-    send_images, loss, image_part, text_part = lax.optimization_barrier(
-        (regroup(1), loss, image_part, text_part)
-    )
+    loss = (loss + shifted(loss, 6)) + (shifted(loss, 3) + shifted(loss, -3))
+    send_images, loss = lax.optimization_barrier((send_images, loss))
     their_images = exchange(send_images)
-
-    def gradient(own, theirs, part):
+    for axis in ("grp_0", "grp_1", "blk_0", "blk_2"):
+        loss = lax.psum(loss, axis)
+    losses = (loss, shifted_beside(loss, 1), shifted_beside(loss, -1))
+
+    def gradient(kernel, more, outs, own, theirs, part):
         return local_kernel(
-            grad_kernel,
-            grad,
-            [SMEM, SMEM, VMEM, VMEM, HBM],
-            HBM,
+            kernel,
+            (*outs, grad),
+            [SMEM] * (len(more) + 2) + [VMEM, VMEM, HBM],
+            (*[SMEM] * len(outs), HBM),
             scratch,
             vmem=52,
             flops=2 * rounds * mac,
             moved=7 * nbytes,
             exps=2 * rounds * rows * rows,
-        )(scale, bias, own, theirs, part)
-
-    image_grad = gradient(x, their_texts, image_part)
-    loss = jnp.sum(loss[:, 0, 0])
-    for axis in ("blk_2", "blk_0", "grp_0", "grp_1"):
-        loss = lax.psum(loss, axis)
-    loss = loss / jnp.float32(lax.axis_size(BLK) * lax.axis_size(GRP) * rows)
-    their_images, loss, image_grad = lax.optimization_barrier((their_images, loss, image_grad))
-    text_grad = gradient(y, their_images, text_part)
-    return image_grad[None], text_grad[None], loss
+        )(*more, scale, bias, own, theirs, part)
+
+    [image_grad] = gradient(grad_kernel, (), (), x, their_texts, image_part)
+    their_images, image_grad = lax.optimization_barrier((their_images, image_grad))
+    count = lax.axis_size(BLK) * lax.axis_size(GRP) * rows
+    loss, text_grad = gradient(
+        functools.partial(last_kernel, float(count)), losses, (one,), y, their_images, text_part
+    )
+    return image_grad[None], text_grad[None], loss[0, 0]
 
 
 def solution(mesh):

time: 187 us -> 202 us (1.080)
  starting transfers between devices: 22.4 us -> 44.2 us
  waiting for transfers between devices: 50.2 us -> 43.4 us
  Pallas kernels: 13.2 us -> 16.4 us
    ppermute x0 -> x5, starting transfers between devices: none -> 27.7 us  [the longest x3 18 us: shifted(): lax.ppermute(value, 'blk_1', [(i, (i + by) % size) for i in range(size)])]
    ppermute x0 -> x5, waiting for transfers between devices: none -> 10.4 us  [the longest x2 5.61 us: shifted_beside(): return lax.ppermute(value, ('blk_1', 'grp_0'), pairs)]
    all_to_all x2 -> x1, waiting for transfers between devices: 43 us -> 33 us  [body(): exchange(regroup(0))]
    all_to_all x2 -> x1, starting transfers between devices: 17.9 us -> 9.33 us  [body(): exchange(regroup(0))]
    all_to_all x1, waiting for transfers between devices: 7.18 us -> 0.01 us  [body(): their_images = exchange(send_images)]
    all_to_all x1, starting transfers between devices: 4.58 us -> 7.12 us  [body(): their_images = exchange(send_images)]
    pallas_call x3, Pallas kernels: 8.17 us -> 10.4 us  [the longest x2 8.25 us: gradient(): local_kernel(kernel, (*outs, grad), [SMEM] * (len(more) + 2) + [VMEM, VME...]
    unnamed x18 -> x16, local copies, waits for them, and re-layouts: 4.99 us -> 3.98 us
  transfers between devices with their start and end apart: 3 -> 7, of which waited for: 3 -> 3; matrix products, arithmetic and copies ran while one was open for 1% -> 0% of each run, Pallas kernels for 3% -> 3%
where the time goes in v5:
time: 202 us; the launch traced here: 201 us
  blocking collectives  87.4 us (43%)
  starting transfers between devices  44.2 us (22%)
  waiting for transfers between devices  43.4 us (21%)
  Pallas kernels  16.4 us (8%)
  local copies, waits for them, and re-layouts  4.78 us (2%)
  between operations  4.62 us (2%)
    all_to_all x1, blocking collectives, body(): spread = exchange(packed)  58 us
    all_to_all x1, waiting for transfers between devices, body(): exchange(regroup(0))  33 us
    psum x4, blocking collectives, body(): loss = lax.psum(loss, axis)  29.3 us
    ppermute x3, starting transfers between devices, shifted(): lax.ppermute(value, 'blk_1', [(i, (i + by) % size) for i in range(size)])  18 us
    ppermute x2, starting transfers between devices, shifted_beside(): return lax.ppermute(value, ('blk_1', 'grp_0'), pairs)  9.71 us
    all_to_all x1, starting transfers between devices, body(): exchange(regroup(0))  9.33 us
    pallas_call x2, Pallas kernels, gradient(): local_kernel(kernel, (*outs, grad), [SMEM] * (len(more) + 2) + [VMEM, VME...  8.25 us
    all_to_all x1, starting transfers between devices, body(): their_images = exchange(send_images)  7.12 us
  transfers between devices with their start and end apart: 7, of which 3 were waited for; matrix products, arithmetic and copies ran while one was open for 0% of the time, Pallas kernels for 3%

profile of v5, /device:TPU:6, one launch (start us, length us, event | category | flops | bytes accessed | tf_op | source)
XLA Modules:
  0.0 200.8 jit_solution(352342406561111686)
XLA Ops:
  0.6 2.3 %shard_map.85 = bf16[48,2,16,384]{3,2,1,0:T(8,128)(2,1)} custom-call(bf16[256,1152]{1,0:T(8,128)(2,1)} %bitcast.20, bf16[256,1152]{1,0:T(8,128)(2,1)} %bitcast.16), custom_call_target="tpu_custom_call" | custom-call | bytes 2359296 | tf_op jit(solution)/shard_map/pallas_call | solution.py:192
  3.0 58.0 %all_to_all.15.spread = bf16[48,2,16,384]{3,2,1,0:T(8,128)(2,1)S(1)} all-to-all(bf16[48,2,16,384]{3,2,1,0:T(8,128)(2,1)} %shard_map.85), channel_id=1, replica_groups=mesh['blk_0'=2,'blk_1'=12,'blk_2'=2,'grp_0'=4,'grp_1'=4] {'blk_0','blk_1..., dimensions={0} | all-to-all | bytes 2359296 | tf_op jit(solution)/shard_map/all_to_all | solution.py:206
  61.7 1.0 copy-done.1
  62.7 9.3 %all-to-all-start.1 = ((bf16[48,2,16,384]{3,2,1,0:T(8,128)(2,1)}), bf16[48,2,16,384]{3,2,1,0:T(8,128)(2,1)S(1)}, u32[]{:S(2)}, u32[]{:S(2)}) async-start(bf16[48,2,16,384]{3,2,1,0:T(8,128)(2,1)} %copy-done.1), calls=%async_computation.1 | async-start | bytes 2359296 | tf_op jit(solution)/shard_map/all_to_all | solution.py:228
  75.1 1.4 shard_map.88
  76.4 1.0 copy-done.3
  77.5 1.0 copy-done.4
  78.5 1.7 shard_map.87
  80.2 33.0 %all-to-all-done.1.received = bf16[48,2,16,384]{3,2,1,0:T(8,128)(2,1)S(1)} async-done(((bf16[48,2,16,384]{3,2,1,0:T(8,128)(2,1)}), bf16[48,2,16,384]{3,2,1,0:T(8,128)(2,1)S(1)}, u32[]{:S(2)}, u32[]{:S(2)}) %all-to-all-start.1) | async-done | bytes 1179680 | tf_op jit(solution)/shard_map/all_to_all | solution.py:228
  113.2 2.1 %shard_map.89 = f32[1,1]{1,0:T(1,128)} custom-call(f32[1,1]{1,0:T(1,128)} %bitcast.9.scale, f32[1,1]{1,0:T(1,128)} %bitcast.13.bias, f32[1,1]{1,0:T(1,128)} %get-tuple-element.21.own_loss, bf16[256,1152]{1,0:T(8,128)(2,1)S(1)} %bitcast.18, bf16[48,2,16,384]{3,2,1,0:T(8,128)(2,1)S(1)} %all-to-all-done.1.received), custom_call_target="tpu_custom_call" | custom-call | flops 301989888 | bytes 1769472 | tf_op jit(solution)/shard_map/pallas_call | solution.py:230
  115.3 9.0 %collective-permute-start.2 = (f32[1,1]{1,0:T(1,128)}, f32[1,1]{1,0:T(1,128)}, u32[]{:S(2)}, u32[]{:S(2)}) collective-permute-start(f32[1,1]{1,0:T(1,128)} %shard_map.89), channel_id=1, source_target_pairs={{0,288},{32,320},{64,352},{96,0},{128,32},{160,64},{192,96},{224,1... | collective-permute-start | bytes 20 | tf_op jit(solution)/shard_map/ppermute | solution.py:158
  124.4 1.9 collective-permute-start.1
  126.3 7.0 %collective-permute-start = (f32[1,1]{1,0:T(1,128)}, f32[1,1]{1,0:T(1,128)}, u32[]{:S(2)}, u32[]{:S(2)}) collective-permute-start(f32[1,1]{1,0:T(1,128)} %shard_map.89), channel_id=1, source_target_pairs={{0,192},{32,224},{64,256},{96,288},{128,320},{160,352},{192,0},{22... | collective-permute-start | bytes 20 | tf_op jit(solution)/shard_map/ppermute | solution.py:158
  133.3 4.8 %collective-permute-done = f32[1,1]{1,0:T(1,128)} collective-permute-done((f32[1,1]{1,0:T(1,128)}, f32[1,1]{1,0:T(1,128)}, u32[]{:S(2)}, u32[]{:S(2)}) %collective-permute-start) | collective-permute-done | bytes 36 | tf_op jit(solution)/shard_map/ppermute | solution.py:158
  140.7 7.1 %all-to-all-start.2 = ((bf16[48,2,16,384]{3,2,1,0:T(8,128)(2,1)}), bf16[48,2,16,384]{3,2,1,0:T(8,128)(2,1)S(1)}, u32[]{:S(2)}, u32[]{:S(2)}) async-start(bf16[48,2,16,384]{3,2,1,0:T(8,128)(2,1)} %shard_map.87), calls=%async_computation.2 | async-start | bytes 2359296 | tf_op jit(solution)/shard_map/all_to_all | solution.py:241
  147.8 8.0 %psum.28 = f32[1,1]{1,0:T(1,128)} all-reduce(f32[1,1]{1,0:T(1,128)S(6)} %add.19), channel_id=1, replica_groups=mesh['blk_0'=2,'blk_1'=12,'blk_2'=2,'grp_0'=4,'grp_1'=4] {'grp_0'}, use_global_device_ids=true, to_apply=%region_0.0 | all-reduce | flops 1 | bytes 8 | tf_op jit(solution)/shard_map/psum | solution.py:243
  155.8 12.6 %psum.29 = f32[1,1]{1,0:T(1,128)} all-reduce(f32[1,1]{1,0:T(1,128)} %psum.28), channel_id=1, replica_groups=mesh['blk_0'=2,'blk_1'=12,'blk_2'=2,'grp_0'=4,'grp_1'=4] {'grp_1'}, use_global_device_ids=true, to_apply=%region_1.0 | all-reduce | flops 1 | bytes 8 | tf_op jit(solution)/shard_map/psum | solution.py:243
  168.4 5.6 %psum.30 = f32[1,1]{1,0:T(1,128)} all-reduce(f32[1,1]{1,0:T(1,128)} %psum.29), channel_id=1, replica_groups=mesh['blk_0'=2,'blk_1'=12,'blk_2'=2,'grp_0'=4,'grp_1'=4] {'blk_0'}, use_global_device_ids=true, to_apply=%region_2.0 | all-reduce | flops 1 | bytes 8 | tf_op jit(solution)/shard_map/psum | solution.py:243
  174.0 3.0 %shard_map.90 = f32[256,1152]{1,0:T(8,128)} custom-call(f32[1,1]{1,0:T(1,128)} %bitcast.10.scale, f32[1,1]{1,0:T(1,128)} %bitcast.14.bias, bf16[256,1152]{1,0:T(8,128)(2,1)S(1)} %bitcast.19, bf16[48,2,16,384]{3,2,1,0:T(8,128)(2,1)S(1)} %all-to-all-done.1.received, f32[256,1152]{1,0:T(8,128)} %copy-done.3), custom_call_target="tpu_custom_call" | custom-call | flops 603979776 | bytes 4128768 | tf_op jit(solution)/shard_map/pallas_call | solution.py:247
  177.0 3.2 %psum.31.a = f32[1,1]{1,0:T(1,128)} all-reduce(f32[1,1]{1,0:T(1,128)} %psum.30), channel_id=1, replica_groups=mesh['blk_0'=2,'blk_1'=12,'blk_2'=2,'grp_0'=4,'grp_1'=4] {'blk_2'}, use_global_device_ids=true, to_apply=%region_3.0 | all-reduce | flops 1 | bytes 8 | tf_op jit(solution)/shard_map/psum | solution.py:243
  180.2 7.8 %collective-permute-start.4 = (f32[1,1]{1,0:T(1,128)}, f32[1,1]{1,0:T(1,128)}, u32[]{:S(2)}, u32[]{:S(2)}) collective-permute-start(f32[1,1]{1,0:T(1,128)} %psum.31.a), channel_id=1, source_target_pairs={{0,356},{4,360},{8,364},{12,352},{32,4},{36,8},{40,12},{44,0},{64,... | collective-permute-start | bytes 20 | tf_op jit(solution)/shard_map/ppermute | solution.py:168
  187.9 1.9 collective-permute-start.3
  189.9 5.6 %collective-permute-done.3.b = f32[1,1]{1,0:T(1,128)} collective-permute-done((f32[1,1]{1,0:T(1,128)}, f32[1,1]{1,0:T(1,128)}, u32[]{:S(2)}, u32[]{:S(2)}) %collective-permute-start.3) | collective-permute-done | bytes 36 | tf_op jit(solution)/shard_map/ppermute | solution.py:168
  195.5 5.3 %shard_map.91 = (f32[1,1]{1,0:T(1,128)}, f32[256,1152]{1,0:T(8,128)}) custom-call(f32[1,1]{1,0:T(1,128)} %psum.31.a, f32[1,1]{1,0:T(1,128)} %collective-permute-done.3.b, f32[1,1]{1,0:T(1,128)} %collective-permute-done.4.c, f32[1,1]{1,0:T(1,128)} %bitcast.11.refs_0_, f32[1,1]{1,0:T(1,128)} %bitcast.15.refs_1_, bf16[256,1152]{1,0:T(8,128)(2,1)S(1)} %bitcast.22, ...), custom_call_target="tpu_custom_call" | custom-call | flops 603979776 | bytes 4128768 | tf_op jit(solution)/shard_map/pallas_call | solution.py:247
  (19 shorter events, 2.4 us)
Async XLA Ops:
  3.0 58.0 %copy-start.6 = (s32[2,48]{1,0:T(2,128)S(1)}, s32[2,48]{1,0:T(2,128)}, u32[]{:S(2)}) copy-start(s32[2,48]{1,0:T(2,128)} %partners.3) | copy-start | bytes 1156
  61.7 1.0 copy-start.1
  62.7 10.6 %copy-start.7 = (s32[1,1,256]{2,1,0:T(1,128)S(1)}, s32[1,1,256]{2,1,0:T(1,128)}, u32[]{:S(2)}) copy-start(s32[1,1,256]{2,1,0:T(1,128)} %param.8) | copy-start | bytes 3076
  62.7 11.5 %copy-start = (bf16[1,256,1152]{2,1,0:T(8,128)(2,1)S(1)}, bf16[1,256,1152]{2,1,0:T(8,128)(2,1)}, u32[]{:S(2)}) copy-start(bf16[1,256,1152]{2,1,0:T(8,128)(2,1)} %param.6) | copy-start | bytes 1769476
  62.7 11.5 %copy-start.2 = (bf16[1,256,1152]{2,1,0:T(8,128)(2,1)S(1)}, bf16[1,256,1152]{2,1,0:T(8,128)(2,1)}, u32[]{:S(2)}) copy-start(bf16[1,256,1152]{2,1,0:T(8,128)(2,1)} %param.7) | copy-start | bytes 1769476
  62.7 50.5 %all-to-all-start.1 = ((bf16[48,2,16,384]{3,2,1,0:T(8,128)(2,1)}), bf16[48,2,16,384]{3,2,1,0:T(8,128)(2,1)S(1)}, u32[]{:S(2)}, u32[]{:S(2)}) async-start(bf16[48,2,16,384]{3,2,1,0:T(8,128)(2,1)} %copy-done.1), calls=%async_computation.1 | async-start | bytes 2359296 | tf_op jit(solution)/shard_map/all_to_all | solution.py:228
  74.2 0.9 copy-start.5
  76.4 1.0 copy-start.3
  77.5 1.0 copy-start.4
  115.3 24.1 %collective-permute-start.2 = (f32[1,1]{1,0:T(1,128)}, f32[1,1]{1,0:T(1,128)}, u32[]{:S(2)}, u32[]{:S(2)}) collective-permute-start(f32[1,1]{1,0:T(1,128)} %shard_map.89), channel_id=1, source_target_pairs={{0,288},{32,320},{64,352},{96,0},{128,32},{160,64},{192,96},{224,1... | collective-permute-start | bytes 20 | tf_op jit(solution)/shard_map/ppermute | solution.py:158
  124.4 15.1 %collective-permute-start.1 = (f32[1,1]{1,0:T(1,128)}, f32[1,1]{1,0:T(1,128)}, u32[]{:S(2)}, u32[]{:S(2)}) collective-permute-start(f32[1,1]{1,0:T(1,128)} %shard_map.89), channel_id=1, source_target_pairs={{0,96},{32,128},{64,160},{96,192},{128,224},{160,256},{192,288},{2... | collective-permute-start | bytes 20 | tf_op jit(solution)/shard_map/ppermute | solution.py:158
  126.3 11.8 %collective-permute-start = (f32[1,1]{1,0:T(1,128)}, f32[1,1]{1,0:T(1,128)}, u32[]{:S(2)}, u32[]{:S(2)}) collective-permute-start(f32[1,1]{1,0:T(1,128)} %shard_map.89), channel_id=1, source_target_pairs={{0,192},{32,224},{64,256},{96,288},{128,320},{160,352},{192,0},{22... | collective-permute-start | bytes 20 | tf_op jit(solution)/shard_map/ppermute | solution.py:158
  140.7 49.2 %all-to-all-start.2 = ((bf16[48,2,16,384]{3,2,1,0:T(8,128)(2,1)}), bf16[48,2,16,384]{3,2,1,0:T(8,128)(2,1)S(1)}, u32[]{:S(2)}, u32[]{:S(2)}) async-start(bf16[48,2,16,384]{3,2,1,0:T(8,128)(2,1)} %shard_map.87), calls=%async_computation.2 | async-start | bytes 2359296 | tf_op jit(solution)/shard_map/all_to_all | solution.py:241
  180.2 9.7 %collective-permute-start.4 = (f32[1,1]{1,0:T(1,128)}, f32[1,1]{1,0:T(1,128)}, u32[]{:S(2)}, u32[]{:S(2)}) collective-permute-start(f32[1,1]{1,0:T(1,128)} %psum.31.a), channel_id=1, source_target_pairs={{0,356},{4,360},{8,364},{12,352},{32,4},{36,8},{40,12},{44,0},{64,... | collective-permute-start | bytes 20 | tf_op jit(solution)/shard_map/ppermute | solution.py:168
  187.9 7.6 %collective-permute-start.3 = (f32[1,1]{1,0:T(1,128)}, f32[1,1]{1,0:T(1,128)}, u32[]{:S(2)}, u32[]{:S(2)}) collective-permute-start(f32[1,1]{1,0:T(1,128)} %psum.31.a), channel_id=1, source_target_pairs={{0,36},{4,40},{8,44},{12,32},{32,68},{36,72},{40,76},{44,64},{64,1... | collective-permute-start | bytes 20 | tf_op jit(solution)/shard_map/ppermute | solution.py:168

commit v6 on v4

--- a/solution.py
+++ b/solution.py
@@ -42,22 +42,23 @@
     ]
     for copy in copies:
         copy.start()
-    for copy in copies:
-        copy.wait()
     row_groups = ROWS // PIECE_ROWS
     sent = []
-    for col in range(packed.shape[0] // row_groups):
-        for row in range(row_groups):
-            for which in range(len(copies)):
+    for which, copy in enumerate(copies):
+        copy.wait()
+        for col in range(packed.shape[0] // row_groups):
+            for row in range(row_groups):
                 filled[col * row_groups + row, which] = rows[
                     which, pl.ds(row * PIECE_ROWS, PIECE_ROWS), columns_of(col)
                 ]
-        part = pl.ds(col * row_groups, row_groups)
-        copy = pltpu.make_async_copy(filled.at[part], packed.at[part], out_sems.at[col])
-        copy.start()
-        sent.append(copy)
-    for copy in sent:
-        copy.wait()
+            part = pl.ds(col * row_groups, row_groups)
+            out = pltpu.make_async_copy(
+                filled.at[part, which], packed.at[part, which], out_sems.at[len(sent)]
+            )
+            out.start()
+            sent.append(out)
+    for out in sent:
+        out.wait()
 
 
 def regroup_kernel(which, partners, spread, send):
@@ -91,34 +92,59 @@
     return e, jnp.where(x >= 0, s, e * s)
 
 
-def own_kernel(scale, bias, images, texts, labels, loss, image_grad, text_grad):
+def own_kernel(numbers, images, texts, labels, loss, image_grad, text_grad):
+    scale, bias = numbers_of(numbers, ROWS)
     x, y = images[...], texts[...]
-    logits = scale[0, 0] * dot_nt(x, y) + bias[0, 0]
+    logits = scale * dot_nt(x, y) + bias
     match = lax.broadcasted_iota(jnp.int32, logits.shape, 1) == labels[...]
     signed = jnp.where(match, -logits, logits)
     e, s = sigmoid_parts(signed)
-    loss[0, 0] = jnp.sum(jnp.maximum(signed, 0.0) + jnp.log1p(e))
+    total = jnp.sum(jnp.maximum(signed, 0.0) + jnp.log1p(e))
+    loss[...] = jnp.full(loss.shape, total, jnp.float32)
     weight = jnp.where(match, -s, s).astype(jnp.bfloat16)
-    image_grad[...] = scale[0, 0] * dot_nn(weight, y)
-    text_grad[...] = scale[0, 0] * dot_tn(weight, x)
-
-
-def partner_logits(scale, bias, own, received, r):
-    total = jnp.zeros((own.shape[0], own.shape[0]), jnp.float32)
+    scale, _ = numbers_of(numbers, x.shape[1])
+    image_grad[...] = scale * dot_nn(weight, y)
+    text_grad[...] = scale * dot_tn(weight, x)
+
+
+def numbers_of(numbers, columns):
+    return numbers[0:1, :columns], numbers[1:2, :columns]
+
+
+def partner_logits(numbers, own, received, r):
+    scale, bias = numbers_of(numbers, ROWS)
+    total = jnp.zeros((ROWS, ROWS), jnp.float32)
     for col in range(own.shape[1] // PIECE_COLS):
         total += dot_nt(own[:, columns_of(col)], column_group(received, r, col))
-    return scale[0, 0] * total + bias[0, 0]
-
-
-def add_and_write(scale, weights, received, part_copy, acc, grad, sems):
+    return scale * total + bias
+
+
+def loss_kernel(numbers, own_loss, images, received, loss):
+    terms = jnp.zeros((ROWS, ROWS), jnp.float32)
+    for r in range(received.shape[1]):
+        logits = partner_logits(numbers, images, received, r)
+        terms += jnp.maximum(logits, 0.0) + jnp.log1p(jnp.exp(-jnp.abs(logits)))
+    row = own_loss[...] + jnp.sum(terms)
+    for place in range(loss.shape[0]):
+        loss[place] = row
+
+
+def grad_kernel(numbers, own, received, part, grad, acc, part_sem, sems):
+    part_copy = pltpu.make_async_copy(part, acc, part_sem)
+    part_copy.start()
+    weights = []
+    for r in range(received.shape[1]):
+        _, s = sigmoid_parts(partner_logits(numbers, own, received, r))
+        weights.append(s.astype(jnp.bfloat16))
     part_copy.wait()
+    scale, _ = numbers_of(numbers, PIECE_COLS)
     copies = []
     for col in range(acc.shape[1] // PIECE_COLS):
         cols = columns_of(col)
         product = sum(
             dot_nn(weight, column_group(received, r, col)) for r, weight in enumerate(weights)
         )
-        acc[:, cols] += scale[0, 0] * product
+        acc[:, cols] += scale * product
         copy = pltpu.make_async_copy(acc.at[:, cols], grad.at[:, cols], sems.at[col])
         copy.start()
         copies.append(copy)
@@ -126,31 +152,13 @@
         copy.wait()
 
 
-def loss_kernel(scale, bias, own_loss, images, received, loss):
-    terms = jnp.zeros((ROWS, ROWS), jnp.float32)
-    for r in range(received.shape[1]):
-        logits = partner_logits(scale, bias, images, received, r)
-        terms += jnp.maximum(logits, 0.0) + jnp.log1p(jnp.exp(-jnp.abs(logits)))
-    loss[...] = jnp.full(loss.shape, own_loss[0, 0] + jnp.sum(terms), jnp.float32)
-
-
-def grad_kernel(scale, bias, own, received, part, grad, acc, part_sem, sems):
-    part_copy = pltpu.make_async_copy(part, acc, part_sem)
-    part_copy.start()
-    weights = []
-    for r in range(received.shape[1]):
-        _, s = sigmoid_parts(partner_logits(scale, bias, own, received, r))
-        weights.append(s.astype(jnp.bfloat16))
-    add_and_write(scale, weights, received, part_copy, acc, grad, sems)
-
-
 def body(images, texts, labels, partners, logit_scale, logit_bias):
     x, y = images[0], texts[0]
     rows, width = x.shape
     rounds, blocks = partners.shape
-    scale, bias = logit_scale.reshape(1, 1), logit_bias.reshape(1, 1)
+    numbers = jnp.broadcast_to(jnp.stack([logit_scale, logit_bias])[:, None], (2, width))
     piece = (PIECE_ROWS, PIECE_COLS)
-    one = jax.ShapeDtypeStruct((1, 1), jnp.float32)
+    row = jax.ShapeDtypeStruct((1, 128), jnp.float32)
     grad = jax.ShapeDtypeStruct((rows, width), jnp.float32)
     col_groups = width // PIECE_COLS
     scratch = [
@@ -174,12 +182,11 @@
             pltpu.VMEM((2, rows, width), x.dtype),
             pltpu.VMEM(pieces.shape, x.dtype),
             pltpu.SemaphoreType.DMA((2,)),
-            pltpu.SemaphoreType.DMA((col_groups,)),
+            pltpu.SemaphoreType.DMA((2 * col_groups,)),
         ],
         vmem=56,
         moved=4 * nbytes,
     )(y, x)
-    spread = exchange(packed)
 
     def regroup(which):
         return local_kernel(
@@ -192,43 +199,44 @@
 
     own_loss, image_part, text_part = local_kernel(
         own_kernel,
-        (one, grad, grad),
-        [SMEM, SMEM, VMEM, VMEM, VMEM],
-        (SMEM, VMEM, VMEM),
+        (row, grad, grad),
+        [VMEM, VMEM, VMEM, VMEM],
+        (VMEM, VMEM, VMEM),
         flops=3 * mac,
         moved=6 * nbytes,
         exps=3 * rows * rows,
-    )(scale, bias, x, y, labels[0].reshape(rows, 1))
-
+    )(numbers, x, y, labels[0].reshape(rows, 1))
+
+    spread, own_loss, image_part, text_part = lax.optimization_barrier(
+        (exchange(packed), own_loss, image_part, text_part)
+    )
     their_texts = exchange(regroup(0))
     z = lax.axis_size("blk_1")
     loss = local_kernel(
         loss_kernel,
         jax.ShapeDtypeStruct((z, 1, 128), jnp.float32),
-        [SMEM, SMEM, SMEM, VMEM, VMEM],
+        [VMEM, VMEM, VMEM, VMEM],
         VMEM,
         flops=rounds * mac,
         moved=3 * nbytes,
         exps=2 * rounds * rows * rows,
-    )(scale, bias, own_loss, x, their_texts)
+    )(numbers, own_loss, x, their_texts)
     loss = lax.all_to_all(loss, "blk_1", split_axis=0, concat_axis=0, tiled=True)
-    send_images, loss, image_part, text_part = lax.optimization_barrier(
-        (regroup(1), loss, image_part, text_part)
-    )
+    send_images, loss = lax.optimization_barrier((regroup(1), loss))
     their_images = exchange(send_images)
 
     def gradient(own, theirs, part):
         return local_kernel(
             grad_kernel,
             grad,
-            [SMEM, SMEM, VMEM, VMEM, HBM],
+            [VMEM, VMEM, VMEM, HBM],
             HBM,
             scratch,
             vmem=52,
             flops=2 * rounds * mac,
             moved=7 * nbytes,
             exps=2 * rounds * rows * rows,
-        )(scale, bias, own, theirs, part)
+        )(numbers, own, theirs, part)
 
     image_grad = gradient(x, their_texts, image_part)
     loss = jnp.sum(loss[:, 0, 0])

time: 187 us -> 184 us (0.984)
  blocking collectives: 87.7 us -> 79.6 us
  starting transfers between devices: 22.4 us -> 30.1 us
  Pallas kernels: 13.2 us -> 11.1 us
    all_to_all x1, blocking collectives: 58 us -> 50.2 us  [body(): their_texts = exchange(regroup(0))]
    all_to_all x1, starting transfers between devices: 9.33 us -> 17 us  [body(): exchange(packed)]
    unnamed x18 -> x22, local copies, waits for them, and re-layouts: 4.99 us -> 4.58 us
where the time goes in v6:
time: 184 us; the launch traced here: 181 us
  blocking collectives  79.6 us (43%)
  waiting for transfers between devices  50 us (27%)
  starting transfers between devices  30.1 us (16%)
  Pallas kernels  11.1 us (6%)
  local copies, waits for them, and re-layouts  5.45 us (3%)
  between operations  3.87 us (2%)
    all_to_all x1, blocking collectives, body(): their_texts = exchange(regroup(0))  50.2 us
    all_to_all x1, waiting for transfers between devices, body(): exchange(packed)  34.6 us
    psum x4, blocking collectives, body(): loss = lax.psum(loss, axis)  29.4 us
    all_to_all x1, starting transfers between devices, body(): exchange(packed)  17 us
    all_to_all x1, starting transfers between devices, body(): lax.all_to_all(loss, 'blk_1', split_axis=0, concat_axis=0, tiled=True)  8.54 us
    all_to_all x1, waiting for transfers between devices, body(): lax.all_to_all(loss, 'blk_1', split_axis=0, concat_axis=0, tiled=True)  8.22 us
    all_to_all x1, waiting for transfers between devices, body(): their_images = exchange(send_images)  7.15 us
    pallas_call x2, Pallas kernels, gradient(): local_kernel(grad_kernel, grad, [VMEM, VMEM, VMEM, HBM], HBM, scratch, vm...  5.29 us
  transfers between devices with their start and end apart: 3, of which 3 were waited for; matrix products, arithmetic and copies ran while one was open for 1% of the time, Pallas kernels for 3%

profile of v6, /device:TPU:6, one launch (start us, length us, event | category | flops | bytes accessed | tf_op | source)
XLA Modules:
  0.0 181.4 jit_solution(17234324870596302918)
XLA Ops:
  0.6 2.2 %shard_map.85 = bf16[48,2,16,384]{3,2,1,0:T(8,128)(2,1)} custom-call(bf16[256,1152]{1,0:T(8,128)(2,1)} %bitcast.13, bf16[256,1152]{1,0:T(8,128)(2,1)} %bitcast.9), custom_call_target="tpu_custom_call" | custom-call | bytes 2359296 | tf_op jit(solution)/shard_map/pallas_call | solution.py:176
  2.8 17.0 %all-to-all-start = ((bf16[48,2,16,384]{3,2,1,0:T(8,128)(2,1)}), bf16[48,2,16,384]{3,2,1,0:T(8,128)(2,1)S(1)}, u32[]{:S(2)}, u32[]{:S(2)}) async-start(bf16[48,2,16,384]{3,2,1,0:T(8,128)(2,1)} %shard_map.85), calls=%async_computation | async-start | bytes 2359296 | tf_op jit(solution)/shard_map/all_to_all | solution.py:211
  21.1 0.8 copy.9.labels
  22.1 0.9 copy-done.5
  23.0 1.3 shard_map.86
  24.3 1.0 copy-done.3
  25.3 1.0 copy-done.4
  26.3 34.6 %all-to-all-done.spread = bf16[48,2,16,384]{3,2,1,0:T(8,128)(2,1)S(1)} async-done(((bf16[48,2,16,384]{3,2,1,0:T(8,128)(2,1)}), bf16[48,2,16,384]{3,2,1,0:T(8,128)(2,1)S(1)}, u32[]{:S(2)}, u32[]{:S(2)}) %all-to-all-start) | async-done | bytes 1179680 | tf_op jit(solution)/shard_map/all_to_all | solution.py:211
  61.0 0.7 shard_map.88
  61.7 50.2 %all_to_all.20.received = bf16[48,2,16,384]{3,2,1,0:T(8,128)(2,1)S(1)} all-to-all(bf16[48,2,16,384]{3,2,1,0:T(8,128)(2,1)S(1)} %shard_map.88), channel_id=1, replica_groups=mesh['blk_0'=2,'blk_1'=12,'blk_2'=2,'grp_0'=4,'grp_1'=4] {'blk_0','blk_1..., dimensions={0} | all-to-all | bytes 2359296 | tf_op jit(solution)/shard_map/all_to_all | solution.py:213
  111.9 1.0 shard_map.89
  113.4 8.5 %all-to-all-start.2 = ((f32[12,1,128]{2,1,0:T(1,128)}), f32[12,1,128]{2,1,0:T(1,128)}, u32[]{:S(2)}, u32[]{:S(2)}) async-start(f32[12,1,128]{2,1,0:T(1,128)} %copy-done.6), calls=%async_computation.2 | async-start | bytes 12288 | tf_op jit(solution)/shard_map/all_to_all | solution.py:224
  122.0 0.7 shard_map.87
  122.7 1.0 copy-done.1
  123.7 8.2 %all-to-all-done.2 = f32[12,1,128]{2,1,0:T(1,128)} async-done(((f32[12,1,128]{2,1,0:T(1,128)}), f32[12,1,128]{2,1,0:T(1,128)}, u32[]{:S(2)}, u32[]{:S(2)}) %all-to-all-start.2) | async-done | bytes 6176 | tf_op jit(solution)/shard_map/all_to_all | solution.py:224
  131.9 4.6 %all-to-all-start.3 = ((bf16[48,2,16,384]{3,2,1,0:T(8,128)(2,1)}), bf16[48,2,16,384]{3,2,1,0:T(8,128)(2,1)S(1)}, u32[]{:S(2)}, u32[]{:S(2)}) async-start(bf16[48,2,16,384]{3,2,1,0:T(8,128)(2,1)} %copy-done.1), calls=%async_computation.3 | async-start | bytes 2359296 | tf_op jit(solution)/shard_map/all_to_all | solution.py:226
  136.5 1.3 slice_reduce_fusion
  137.8 3.1 %psum.28 = f32[]{:T(128)} all-reduce(f32[]{:T(128)} %slice_reduce_fusion), channel_id=1, replica_groups=mesh['blk_0'=2,'blk_1'=12,'blk_2'=2,'grp_0'=4,'grp_1'=4] {'blk_2'}, use_global_device_ids=true, to_apply=%region_1.0 | all-reduce | flops 1 | bytes 8 | tf_op jit(solution)/shard_map/psum | solution.py:244
  140.9 5.6 %psum.29 = f32[]{:T(128)} all-reduce(f32[]{:T(128)} %psum.28), channel_id=1, replica_groups=mesh['blk_0'=2,'blk_1'=12,'blk_2'=2,'grp_0'=4,'grp_1'=4] {'blk_0'}, use_global_device_ids=true, to_apply=%region_2.0 | all-reduce | flops 1 | bytes 8 | tf_op jit(solution)/shard_map/psum | solution.py:244
  146.5 8.1 %psum.30 = f32[]{:T(128)} all-reduce(f32[]{:T(128)} %psum.29), channel_id=1, replica_groups=mesh['blk_0'=2,'blk_1'=12,'blk_2'=2,'grp_0'=4,'grp_1'=4] {'grp_0'}, use_global_device_ids=true, to_apply=%region_3.0 | all-reduce | flops 1 | bytes 8 | tf_op jit(solution)/shard_map/psum | solution.py:244
  154.5 2.6 %shard_map.90 = f32[256,1152]{1,0:T(8,128)} custom-call(f32[2,1152]{1,0:T(2,128)S(1)} %broadcast_in_dim.12.numbers, bf16[256,1152]{1,0:T(8,128)(2,1)S(1)} %bitcast.12, bf16[48,2,16,384]{3,2,1,0:T(8,128)(2,1)S(1)} %all_to_all.20.received, f32[256,1152]{1,0:T(8,128)} %copy-done.4), custom_call_target="tpu_custom_call" | custom-call | flops 603979776 | bytes 4128768 | tf_op jit(solution)/shard_map/pallas_call | solution.py:229
  157.2 12.7 %psum.31 = f32[]{:T(128)} all-reduce(f32[]{:T(128)} %psum.30), channel_id=1, replica_groups=mesh['blk_0'=2,'blk_1'=12,'blk_2'=2,'grp_0'=4,'grp_1'=4] {'grp_1'}, use_global_device_ids=true, to_apply=%region_4.0 | all-reduce | flops 1 | bytes 8 | tf_op jit(solution)/shard_map/psum | solution.py:244
  170.5 7.2 %all-to-all-done.3.received = bf16[48,2,16,384]{3,2,1,0:T(8,128)(2,1)S(1)} async-done(((bf16[48,2,16,384]{3,2,1,0:T(8,128)(2,1)}), bf16[48,2,16,384]{3,2,1,0:T(8,128)(2,1)S(1)}, u32[]{:S(2)}, u32[]{:S(2)}) %all-to-all-start.3) | async-done | bytes 1179680 | tf_op jit(solution)/shard_map/all_to_all | solution.py:226
  177.7 2.6 %shard_map.91 = f32[256,1152]{1,0:T(8,128)} custom-call(f32[2,1152]{1,0:T(2,128)S(1)} %broadcast_in_dim.12.numbers, bf16[256,1152]{1,0:T(8,128)(2,1)S(1)} %bitcast.15, bf16[48,2,16,384]{3,2,1,0:T(8,128)(2,1)S(1)} %all-to-all-done.3.received, f32[256,1152]{1,0:T(8,128)} %copy-done.3), custom_call_target="tpu_custom_call" | custom-call | flops 603979776 | bytes 4128768 | tf_op jit(solution)/shard_map/pallas_call | solution.py:229
  (20 shorter events, 0.8 us)
Async XLA Ops:
  2.8 18.4 %copy-start.10 = (s32[1,1,256]{2,1,0:T(1,128)S(1)}, s32[1,1,256]{2,1,0:T(1,128)}, u32[]{:S(2)}) copy-start(s32[1,1,256]{2,1,0:T(1,128)} %param.8) | copy-start | bytes 3076
  2.8 19.3 %copy-start = (bf16[1,256,1152]{2,1,0:T(8,128)(2,1)S(1)}, bf16[1,256,1152]{2,1,0:T(8,128)(2,1)}, u32[]{:S(2)}) copy-start(bf16[1,256,1152]{2,1,0:T(8,128)(2,1)} %param.6) | copy-start | bytes 1769476
  2.8 19.3 %copy-start.2 = (bf16[1,256,1152]{2,1,0:T(8,128)(2,1)S(1)}, bf16[1,256,1152]{2,1,0:T(8,128)(2,1)}, u32[]{:S(2)}) copy-start(bf16[1,256,1152]{2,1,0:T(8,128)(2,1)} %param.7) | copy-start | bytes 1769476
  2.8 58.2 %all-to-all-start = ((bf16[48,2,16,384]{3,2,1,0:T(8,128)(2,1)}), bf16[48,2,16,384]{3,2,1,0:T(8,128)(2,1)S(1)}, u32[]{:S(2)}, u32[]{:S(2)}) async-start(bf16[48,2,16,384]{3,2,1,0:T(8,128)(2,1)} %shard_map.85), calls=%async_computation | async-start | bytes 2359296 | tf_op jit(solution)/shard_map/all_to_all | solution.py:211
  19.8 41.2 %copy-start.7 = (s32[2,48]{1,0:T(2,128)S(1)}, s32[2,48]{1,0:T(2,128)}, u32[]{:S(2)}) copy-start(s32[2,48]{1,0:T(2,128)} %partners.3) | copy-start | bytes 1156
  22.1 0.9 copy-start.5
  24.3 1.0 copy-start.3
  25.3 1.0 copy-start.4
  26.3 34.6 %copy-start.8 = (f32[1,128]{1,0:T(1,128)}, f32[1,128]{1,0:T(1,128)S(1)}, u32[]{:S(2)}) copy-start(f32[1,128]{1,0:T(1,128)S(1)} %get-tuple-element.19.own_loss) | copy-start | bytes 1540
  61.7 50.2 %copy-start.9 = (f32[1,128]{1,0:T(1,128)S(1)}, f32[1,128]{1,0:T(1,128)}, u32[]{:S(2)}) copy-start(f32[1,128]{1,0:T(1,128)} %copy-done.8) | copy-start | bytes 1540
  112.8 0.6 copy-start.6
  113.4 18.5 %all-to-all-start.2 = ((f32[12,1,128]{2,1,0:T(1,128)}), f32[12,1,128]{2,1,0:T(1,128)}, u32[]{:S(2)}, u32[]{:S(2)}) async-start(f32[12,1,128]{2,1,0:T(1,128)} %copy-done.6), calls=%async_computation.2 | async-start | bytes 12288 | tf_op jit(solution)/shard_map/all_to_all | solution.py:224
  122.7 1.0 copy-start.1
  131.9 45.7 %all-to-all-start.3 = ((bf16[48,2,16,384]{3,2,1,0:T(8,128)(2,1)}), bf16[48,2,16,384]{3,2,1,0:T(8,128)(2,1)S(1)}, u32[]{:S(2)}, u32[]{:S(2)}) async-start(bf16[48,2,16,384]{3,2,1,0:T(8,128)(2,1)} %copy-done.1), calls=%async_computation.3 | async-start | bytes 2359296 | tf_op jit(solution)/shard_map/all_to_all | solution.py:226

commit v7 on v6

--- a/solution.py
+++ b/solution.py
@@ -35,37 +35,38 @@
     return pl.ds(col * PIECE_COLS, PIECE_COLS)
 
 
-def pack_kernel(texts, images, packed, rows, filled, in_sems, out_sems):
-    copies = [
-        pltpu.make_async_copy(block, rows.at[which], in_sems.at[which])
-        for which, block in enumerate((texts, images))
-    ]
-    for copy in copies:
-        copy.start()
-    row_groups = ROWS // PIECE_ROWS
+def pack_kernel(texts, images, packed, filled, in_sems, out_sems):
+    row_groups, _, columns = texts.shape
+    groups = []
+    for col in range(columns // PIECE_COLS):
+        part = pl.ds(col * row_groups, row_groups)
+        coming = [
+            pltpu.make_async_copy(
+                rows.at[:, :, columns_of(col)], filled.at[part, which], in_sems.at[col, which]
+            )
+            for which, rows in enumerate((texts, images))
+        ]
+        for copy in coming:
+            copy.start()
+        groups.append((part, coming))
     sent = []
-    for which, copy in enumerate(copies):
-        copy.wait()
-        for col in range(packed.shape[0] // row_groups):
-            for row in range(row_groups):
-                filled[col * row_groups + row, which] = rows[
-                    which, pl.ds(row * PIECE_ROWS, PIECE_ROWS), columns_of(col)
-                ]
-            part = pl.ds(col * row_groups, row_groups)
-            out = pltpu.make_async_copy(
-                filled.at[part, which], packed.at[part, which], out_sems.at[len(sent)]
-            )
-            out.start()
-            sent.append(out)
+    for col, (part, coming) in enumerate(groups):
+        for copy in coming:
+            copy.wait()
+        out = pltpu.make_async_copy(filled.at[part], packed.at[part], out_sems.at[col])
+        out.start()
+        sent.append(out)
     for out in sent:
         out.wait()
 
 
-def regroup_kernel(which, partners, spread, send):
+def regroup_kernel(partners, spread, *sends):
     rounds, blocks = partners.shape
     for block in range(blocks):
         for r in range(rounds):
-            send[block, r] = spread[partners[r, block], which]
+            source = partners[r, block]
+            for which, send in enumerate(sends):
+                send[block, r] = spread[source, which]
 
 
 def column_group(received, r, col):
@@ -179,23 +180,13 @@
         [HBM, HBM],
         HBM,
         [
-            pltpu.VMEM((2, rows, width), x.dtype),
             pltpu.VMEM(pieces.shape, x.dtype),
-            pltpu.SemaphoreType.DMA((2,)),
-            pltpu.SemaphoreType.DMA((2 * col_groups,)),
+            pltpu.SemaphoreType.DMA((col_groups, 2)),
+            pltpu.SemaphoreType.DMA((col_groups,)),
         ],
         vmem=56,
         moved=4 * nbytes,
-    )(y, x)
-
-    def regroup(which):
-        return local_kernel(
-            functools.partial(regroup_kernel, which),
-            pieces,
-            [SMEM, VMEM],
-            VMEM,
-            moved=4 * nbytes,
-        )(partners, spread)
+    )(y.reshape(-1, PIECE_ROWS, width), x.reshape(-1, PIECE_ROWS, width))
 
     own_loss, image_part, text_part = local_kernel(
         own_kernel,
@@ -210,7 +201,14 @@
     spread, own_loss, image_part, text_part = lax.optimization_barrier(
         (exchange(packed), own_loss, image_part, text_part)
     )
-    their_texts = exchange(regroup(0))
+    send_texts, send_images = local_kernel(
+        regroup_kernel,
+        (pieces, pieces),
+        [SMEM, VMEM],
+        (VMEM, VMEM),
+        moved=6 * nbytes,
+    )(partners, spread)
+    their_texts = exchange(send_texts)
     z = lax.axis_size("blk_1")
     loss = local_kernel(
         loss_kernel,
@@ -222,7 +220,7 @@
         exps=2 * rounds * rows * rows,
     )(numbers, own_loss, x, their_texts)
     loss = lax.all_to_all(loss, "blk_1", split_axis=0, concat_axis=0, tiled=True)
-    send_images, loss = lax.optimization_barrier((regroup(1), loss))
+    send_images, loss, their_texts = lax.optimization_barrier((send_images, loss, their_texts))
     their_images = exchange(send_images)
 
     def gradient(own, theirs, part):

time: 184 us -> 184 us (level)
  blocking collectives: 79.6 us -> 98 us
  starting transfers between devices: 30.1 us -> 21.6 us
  waiting for transfers between devices: 50 us -> 42.3 us
  local copies, waits for them, and re-layouts: 5.45 us -> 3.33 us
    all_to_all x1 -> x2, blocking collectives: 50.2 us -> 68.7 us  [the longest x1 50.3 us: body(): their_texts = exchange(send_texts)]
    all_to_all x1 -> x0, starting transfers between devices: 8.54 us -> none  [body(): lax.all_to_all(loss, 'blk_1', split_axis=0, concat_axis=0, tiled=True)]
    all_to_all x1 -> x0, waiting for transfers between devices: 8.22 us -> none  [body(): lax.all_to_all(loss, 'blk_1', split_axis=0, concat_axis=0, tiled=True)]
    unnamed x22 -> x20, local copies, waits for them, and re-layouts: 4.58 us -> 2.45 us
  transfers between devices with their start and end apart: 3 -> 2, of which waited for: 3 -> 2; matrix products, arithmetic and copies ran while one was open for 1% -> 1% of each run, Pallas kernels for 3% -> 2%
where the time goes in v7:
time: 184 us; the launch traced here: 181 us
  blocking collectives  98 us (53%)
  waiting for transfers between devices  42.3 us (23%)
  starting transfers between devices  21.6 us (12%)
  Pallas kernels  10.5 us (6%)
  between operations  3.85 us (2%)
  local copies, waits for them, and re-layouts  3.33 us (2%)
    all_to_all x1, blocking collectives, body(): their_texts = exchange(send_texts)  50.3 us
    all_to_all x1, waiting for transfers between devices, body(): exchange(packed)  35.2 us
    psum x4, blocking collectives, body(): loss = lax.psum(loss, axis)  29.4 us
    all_to_all x1, blocking collectives, body(): lax.all_to_all(loss, 'blk_1', split_axis=0, concat_axis=0, tiled=True)  18.4 us
    all_to_all x1, starting transfers between devices, body(): exchange(packed)  17 us
    all_to_all x1, waiting for transfers between devices, body(): their_images = exchange(send_images)  7.18 us
    pallas_call x2, Pallas kernels, gradient(): local_kernel(grad_kernel, grad, [VMEM, VMEM, VMEM, HBM], HBM, scratch, vm...  5.29 us
    all_to_all x1, starting transfers between devices, body(): their_images = exchange(send_images)  4.58 us
  transfers between devices with their start and end apart: 2, of which 2 were waited for; matrix products, arithmetic and copies ran while one was open for 1% of the time, Pallas kernels for 2%

profile of v7, /device:TPU:6, one launch (start us, length us, event | category | flops | bytes accessed | tf_op | source)
XLA Modules:
  0.0 181.0 jit_solution(1764613854704966006)
XLA Ops:
  0.6 2.2 %shard_map.85 = bf16[48,2,16,384]{3,2,1,0:T(8,128)(2,1)} custom-call(bf16[16,16,1152]{2,1,0:T(8,128)(2,1)} %bitcast.15, bf16[16,16,1152]{2,1,0:T(8,128)(2,1)} %bitcast.11), custom_call_target="tpu_custom_call" | custom-call | bytes 2359296 | tf_op jit(solution)/shard_map/pallas_call | solution.py:177
  2.8 0.0 copy-start.9
  2.9 17.0 %all-to-all-start = ((bf16[48,2,16,384]{3,2,1,0:T(8,128)(2,1)}), bf16[48,2,16,384]{3,2,1,0:T(8,128)(2,1)S(1)}, u32[]{:S(2)}, u32[]{:S(2)}) async-start(bf16[48,2,16,384]{3,2,1,0:T(8,128)(2,1)} %shard_map.85), calls=%async_computation | async-start | bytes 2359296 | tf_op jit(solution)/shard_map/all_to_all | solution.py:202
  21.2 0.8 copy.9.labels
  22.0 0.1 pad_maximum_fusion
  22.1 0.1 broadcast_in_dim.12.numbers
  22.1 0.9 copy-done.5
  23.0 1.3 shard_map.86
  24.3 1.0 copy-done.2
  25.3 0.5 copy-done.7
  25.9 35.2 %all-to-all-done.spread = bf16[48,2,16,384]{3,2,1,0:T(8,128)(2,1)S(1)} async-done(((bf16[48,2,16,384]{3,2,1,0:T(8,128)(2,1)}), bf16[48,2,16,384]{3,2,1,0:T(8,128)(2,1)S(1)}, u32[]{:S(2)}, u32[]{:S(2)}) %all-to-all-start) | async-done | bytes 1179680 | tf_op jit(solution)/shard_map/all_to_all | solution.py:202
  61.0 0.8 shard_map.87
  61.8 50.3 %all_to_all.20.received = bf16[48,2,16,384]{3,2,1,0:T(8,128)(2,1)S(1)} all-to-all(bf16[48,2,16,384]{3,2,1,0:T(8,128)(2,1)S(1)} %get-tuple-element.24), channel_id=1, replica_groups=mesh['blk_0'=2,'blk_1'=12,'blk_2'=2,'grp_0'=4,'grp_1'=4] {'blk_0','blk_1..., dimensions={0} | all-to-all | bytes 2359296 | tf_op jit(solution)/shard_map/all_to_all | solution.py:211
  112.1 1.0 shard_map.88
  113.1 18.4 %all_to_all.21 = f32[12,1,128]{2,1,0:T(1,128)} all-to-all(f32[12,1,128]{2,1,0:T(1,128)S(1)} %shard_map.88), channel_id=1, replica_groups=mesh['blk_0'=2,'blk_1'=12,'blk_2'=2,'grp_0'=4,'grp_1'=4] {'blk_1'}, dimensions={0} | all-to-all | bytes 12288 | tf_op jit(solution)/shard_map/all_to_all | solution.py:222
  131.5 4.6 %all-to-all-start.3 = ((bf16[48,2,16,384]{3,2,1,0:T(8,128)(2,1)}), bf16[48,2,16,384]{3,2,1,0:T(8,128)(2,1)S(1)}, u32[]{:S(2)}, u32[]{:S(2)}) async-start(bf16[48,2,16,384]{3,2,1,0:T(8,128)(2,1)} %copy-done.4), calls=%async_computation.3 | async-start | bytes 2359296 | tf_op jit(solution)/shard_map/all_to_all | solution.py:224
  136.1 1.3 slice_reduce_fusion
  137.4 3.1 %psum.28 = f32[]{:T(128)} all-reduce(f32[]{:T(128)} %slice_reduce_fusion), channel_id=1, replica_groups=mesh['blk_0'=2,'blk_1'=12,'blk_2'=2,'grp_0'=4,'grp_1'=4] {'blk_2'}, use_global_device_ids=true, to_apply=%region_1.0 | all-reduce | flops 1 | bytes 8 | tf_op jit(solution)/shard_map/psum | solution.py:242
  140.5 5.6 %psum.29 = f32[]{:T(128)} all-reduce(f32[]{:T(128)} %psum.28), channel_id=1, replica_groups=mesh['blk_0'=2,'blk_1'=12,'blk_2'=2,'grp_0'=4,'grp_1'=4] {'blk_0'}, use_global_device_ids=true, to_apply=%region_2.0 | all-reduce | flops 1 | bytes 8 | tf_op jit(solution)/shard_map/psum | solution.py:242
  146.0 8.1 %psum.30 = f32[]{:T(128)} all-reduce(f32[]{:T(128)} %psum.29), channel_id=1, replica_groups=mesh['blk_0'=2,'blk_1'=12,'blk_2'=2,'grp_0'=4,'grp_1'=4] {'grp_0'}, use_global_device_ids=true, to_apply=%region_3.0 | all-reduce | flops 1 | bytes 8 | tf_op jit(solution)/shard_map/psum | solution.py:242
  154.1 12.6 %psum.31 = f32[]{:T(128)} all-reduce(f32[]{:T(128)} %psum.30), channel_id=1, replica_groups=mesh['blk_0'=2,'blk_1'=12,'blk_2'=2,'grp_0'=4,'grp_1'=4] {'grp_1'}, use_global_device_ids=true, to_apply=%region_4.0 | all-reduce | flops 1 | bytes 8 | tf_op jit(solution)/shard_map/psum | solution.py:242
  167.4 2.6 %shard_map.89 = f32[256,1152]{1,0:T(8,128)} custom-call(f32[2,1152]{1,0:T(2,128)S(1)} %broadcast_in_dim.12.numbers, bf16[256,1152]{1,0:T(8,128)(2,1)S(1)} %bitcast.14, bf16[48,2,16,384]{3,2,1,0:T(8,128)(2,1)S(1)} %all_to_all.20.received, f32[256,1152]{1,0:T(8,128)} %copy-done.3), custom_call_target="tpu_custom_call" | custom-call | flops 603979776 | bytes 4128768 | tf_op jit(solution)/shard_map/pallas_call | solution.py:227
  170.0 7.2 %all-to-all-done.3.received = bf16[48,2,16,384]{3,2,1,0:T(8,128)(2,1)S(1)} async-done(((bf16[48,2,16,384]{3,2,1,0:T(8,128)(2,1)}), bf16[48,2,16,384]{3,2,1,0:T(8,128)(2,1)S(1)}, u32[]{:S(2)}, u32[]{:S(2)}) %all-to-all-start.3) | async-done | bytes 1179680 | tf_op jit(solution)/shard_map/all_to_all | solution.py:224
  177.2 2.6 %shard_map.90 = f32[256,1152]{1,0:T(8,128)} custom-call(f32[2,1152]{1,0:T(2,128)S(1)} %broadcast_in_dim.12.numbers, bf16[256,1152]{1,0:T(8,128)(2,1)S(1)} %bitcast.17, bf16[48,2,16,384]{3,2,1,0:T(8,128)(2,1)S(1)} %all-to-all-done.3.received, f32[256,1152]{1,0:T(8,128)} %copy-done.2), custom_call_target="tpu_custom_call" | custom-call | flops 603979776 | bytes 4128768 | tf_op jit(solution)/shard_map/pallas_call | solution.py:227
  (16 shorter events, 0.0 us)
Async XLA Ops:
  2.8 18.4 %copy-start.9 = (s32[1,1,256]{2,1,0:T(1,128)S(1)}, s32[1,1,256]{2,1,0:T(1,128)}, u32[]{:S(2)}) copy-start(s32[1,1,256]{2,1,0:T(1,128)} %param.8) | copy-start | bytes 3076
  2.8 19.3 %copy-start = (bf16[1,256,1152]{2,1,0:T(8,128)(2,1)S(1)}, bf16[1,256,1152]{2,1,0:T(8,128)(2,1)}, u32[]{:S(2)}) copy-start(bf16[1,256,1152]{2,1,0:T(8,128)(2,1)} %param.6) | copy-start | bytes 1769476
  2.8 19.3 %copy-start.1 = (bf16[1,256,1152]{2,1,0:T(8,128)(2,1)S(1)}, bf16[1,256,1152]{2,1,0:T(8,128)(2,1)}, u32[]{:S(2)}) copy-start(bf16[1,256,1152]{2,1,0:T(8,128)(2,1)} %param.7) | copy-start | bytes 1769476
  2.9 58.2 %all-to-all-start = ((bf16[48,2,16,384]{3,2,1,0:T(8,128)(2,1)}), bf16[48,2,16,384]{3,2,1,0:T(8,128)(2,1)S(1)}, u32[]{:S(2)}, u32[]{:S(2)}) async-start(bf16[48,2,16,384]{3,2,1,0:T(8,128)(2,1)} %shard_map.85), calls=%async_computation | async-start | bytes 2359296 | tf_op jit(solution)/shard_map/all_to_all | solution.py:202
  19.9 41.2 %copy-start.6 = (s32[2,48]{1,0:T(2,128)S(1)}, s32[2,48]{1,0:T(2,128)}, u32[]{:S(2)}) copy-start(s32[2,48]{1,0:T(2,128)} %partners.1) | copy-start | bytes 1156
  22.1 0.9 copy-start.5
  24.3 1.0 copy-start.2
  25.3 0.5 copy-start.7
  25.8 86.3 %copy-start.3 = (f32[256,1152]{1,0:T(8,128)}, f32[256,1152]{1,0:T(8,128)S(1)}, u32[]{:S(2)}) copy-start(f32[256,1152]{1,0:T(8,128)S(1)} %get-tuple-element.28.part) | copy-start | bytes 3538948
  61.8 50.3 %copy-start.4 = (bf16[48,2,16,384]{3,2,1,0:T(8,128)(2,1)}, bf16[48,2,16,384]{3,2,1,0:T(8,128)(2,1)S(1)}, u32[]{:S(2)}) copy-start(bf16[48,2,16,384]{3,2,1,0:T(8,128)(2,1)S(1)} %get-tuple-element.25) | copy-start | bytes 3538948
  61.8 50.3 %copy-start.8 = (f32[1,128]{1,0:T(1,128)S(1)}, f32[1,128]{1,0:T(1,128)}, u32[]{:S(2)}) copy-start(f32[1,128]{1,0:T(1,128)} %copy-done.7) | copy-start | bytes 1540
  131.5 45.7 %all-to-all-start.3 = ((bf16[48,2,16,384]{3,2,1,0:T(8,128)(2,1)}), bf16[48,2,16,384]{3,2,1,0:T(8,128)(2,1)S(1)}, u32[]{:S(2)}, u32[]{:S(2)}) async-start(bf16[48,2,16,384]{3,2,1,0:T(8,128)(2,1)} %copy-done.4), calls=%async_computation.3 | async-start | bytes 2359296 | tf_op jit(solution)/shard_map/all_to_all | solution.py:224

commit v8 on v7

--- a/solution.py
+++ b/solution.py
@@ -219,8 +219,6 @@
         moved=3 * nbytes,
         exps=2 * rounds * rows * rows,
     )(numbers, own_loss, x, their_texts)
-    loss = lax.all_to_all(loss, "blk_1", split_axis=0, concat_axis=0, tiled=True)
-    send_images, loss, their_texts = lax.optimization_barrier((send_images, loss, their_texts))
     their_images = exchange(send_images)
 
     def gradient(own, theirs, part):
@@ -237,12 +235,13 @@
         )(numbers, own, theirs, part)
 
     image_grad = gradient(x, their_texts, image_part)
-    loss = jnp.sum(loss[:, 0, 0])
     for axis in ("blk_2", "blk_0", "grp_0", "grp_1"):
         loss = lax.psum(loss, axis)
+    their_images, loss, image_grad = lax.optimization_barrier((their_images, loss, image_grad))
+    loss = lax.all_to_all(loss, "blk_1", split_axis=0, concat_axis=0, tiled=True)
+    text_grad = gradient(y, their_images, text_part)
+    loss = jnp.sum(loss[:, 0, 0])
     loss = loss / jnp.float32(lax.axis_size(BLK) * lax.axis_size(GRP) * rows)
-    their_images, loss, image_grad = lax.optimization_barrier((their_images, loss, image_grad))
-    text_grad = gradient(y, their_images, text_part)
     return image_grad[None], text_grad[None], loss
 
 

time: 184 us -> 184 us (level); the launches traced: 181 us -> 183 us
  blocking collectives: 98 us -> 80.4 us
  starting transfers between devices: 21.6 us -> 34.9 us
  waiting for transfers between devices: 42.3 us -> 49.2 us
    all_to_all x1 -> x0, blocking collectives: 18.4 us -> none  [body(): lax.all_to_all(loss, 'blk_1', split_axis=0, concat_axis=0, tiled=True)]
    all_to_all x0 -> x1, starting transfers between devices: none -> 8.53 us  [body(): lax.all_to_all(loss, 'blk_1', split_axis=0, concat_axis=0, tiled=True)]
    all_to_all x0 -> x1, waiting for transfers between devices: none -> 7.39 us  [body(): lax.all_to_all(loss, 'blk_1', split_axis=0, concat_axis=0, tiled=True)]
    all_to_all x1, starting transfers between devices: 4.58 us -> 9.34 us  [body(): their_images = exchange(send_images)]
  transfers between devices with their start and end apart: 2 -> 3, of which waited for: 2 -> 3; matrix products, arithmetic and copies ran while one was open for 1% -> 1% of each run, Pallas kernels for 2% -> 4%
where the time goes in v8:
time: 184 us; the launch traced here: 183 us
  blocking collectives  80.4 us (44%)
  waiting for transfers between devices  49.2 us (27%)
  starting transfers between devices  34.9 us (19%)
  Pallas kernels  10.5 us (6%)
  local copies, waits for them, and re-layouts  3.93 us (2%)
  between operations  3.86 us (2%)
    all_to_all x1, blocking collectives, body(): their_texts = exchange(send_texts)  50.2 us
    all_to_all x1, waiting for transfers between devices, body(): exchange(packed)  35.2 us
    psum x4, blocking collectives, body(): loss = lax.psum(loss, axis)  30.2 us
    all_to_all x1, starting transfers between devices, body(): exchange(packed)  17 us
    all_to_all x1, starting transfers between devices, body(): their_images = exchange(send_images)  9.34 us
    all_to_all x1, starting transfers between devices, body(): lax.all_to_all(loss, 'blk_1', split_axis=0, concat_axis=0, tiled=True)  8.53 us
    all_to_all x1, waiting for transfers between devices, body(): lax.all_to_all(loss, 'blk_1', split_axis=0, concat_axis=0, tiled=True)  7.39 us
    all_to_all x1, waiting for transfers between devices, body(): their_images = exchange(send_images)  6.69 us
  transfers between devices with their start and end apart: 3, of which 3 were waited for; matrix products, arithmetic and copies ran while one was open for 1% of the time, Pallas kernels for 4%

profile of v8, /device:TPU:6, one launch (start us, length us, event | category | flops | bytes accessed | tf_op | source)
XLA Modules:
  0.0 183.5 jit_solution(2827541303926154195)
XLA Ops:
  0.6 2.2 %shard_map.85 = bf16[48,2,16,384]{3,2,1,0:T(8,128)(2,1)} custom-call(bf16[16,16,1152]{2,1,0:T(8,128)(2,1)} %bitcast.15, bf16[16,16,1152]{2,1,0:T(8,128)(2,1)} %bitcast.11), custom_call_target="tpu_custom_call" | custom-call | bytes 2359296 | tf_op jit(solution)/shard_map/pallas_call | solution.py:177
  2.9 17.0 %all-to-all-start = ((bf16[48,2,16,384]{3,2,1,0:T(8,128)(2,1)}), bf16[48,2,16,384]{3,2,1,0:T(8,128)(2,1)S(1)}, u32[]{:S(2)}, u32[]{:S(2)}) async-start(bf16[48,2,16,384]{3,2,1,0:T(8,128)(2,1)} %shard_map.85), calls=%async_computation | async-start | bytes 2359296 | tf_op jit(solution)/shard_map/all_to_all | solution.py:202
  21.2 0.8 copy.9.labels
  22.1 0.1 broadcast_in_dim.12.numbers
  22.1 0.9 copy-done.5
  23.0 1.3 shard_map.86
  24.3 1.0 copy-done.2
  25.4 0.5 copy-done.8
  25.9 35.2 %all-to-all-done.spread = bf16[48,2,16,384]{3,2,1,0:T(8,128)(2,1)S(1)} async-done(((bf16[48,2,16,384]{3,2,1,0:T(8,128)(2,1)}), bf16[48,2,16,384]{3,2,1,0:T(8,128)(2,1)S(1)}, u32[]{:S(2)}, u32[]{:S(2)}) %all-to-all-start) | async-done | bytes 1179680 | tf_op jit(solution)/shard_map/all_to_all | solution.py:202
  61.0 0.8 shard_map.87
  61.8 50.2 %all_to_all.20.received = bf16[48,2,16,384]{3,2,1,0:T(8,128)(2,1)S(1)} all-to-all(bf16[48,2,16,384]{3,2,1,0:T(8,128)(2,1)S(1)} %get-tuple-element.21), channel_id=1, replica_groups=mesh['blk_0'=2,'blk_1'=12,'blk_2'=2,'grp_0'=4,'grp_1'=4] {'blk_0','blk_1..., dimensions={0} | all-to-all | bytes 2359296 | tf_op jit(solution)/shard_map/all_to_all | solution.py:211
  112.0 9.3 %all-to-all-start.1 = ((bf16[48,2,16,384]{3,2,1,0:T(8,128)(2,1)}), bf16[48,2,16,384]{3,2,1,0:T(8,128)(2,1)S(1)}, u32[]{:S(2)}, u32[]{:S(2)}) async-start(bf16[48,2,16,384]{3,2,1,0:T(8,128)(2,1)} %copy-done.4), calls=%async_computation.1 | async-start | bytes 2359296 | tf_op jit(solution)/shard_map/all_to_all | solution.py:222
  121.3 1.0 shard_map.88
  122.3 0.6 copy-done.6
  122.9 3.2 %psum.28 = f32[12,1,128]{2,1,0:T(1,128)} all-reduce(f32[12,1,128]{2,1,0:T(1,128)} %copy-done.6), channel_id=1, replica_groups=mesh['blk_0'=2,'blk_1'=12,'blk_2'=2,'grp_0'=4,'grp_1'=4] {'blk_2'}, use_global_device_ids=true, to_apply=%region_0.0 | all-reduce | flops 1536 | bytes 12288 | tf_op jit(solution)/shard_map/psum | solution.py:239
  126.1 5.8 %psum.29 = f32[12,1,128]{2,1,0:T(1,128)} all-reduce(f32[12,1,128]{2,1,0:T(1,128)} %psum.28), channel_id=1, replica_groups=mesh['blk_0'=2,'blk_1'=12,'blk_2'=2,'grp_0'=4,'grp_1'=4] {'blk_0'}, use_global_device_ids=true, to_apply=%region_1.0 | all-reduce | flops 1536 | bytes 12288 | tf_op jit(solution)/shard_map/psum | solution.py:239
  131.9 8.3 %psum.30 = f32[12,1,128]{2,1,0:T(1,128)} all-reduce(f32[12,1,128]{2,1,0:T(1,128)} %psum.29), channel_id=1, replica_groups=mesh['blk_0'=2,'blk_1'=12,'blk_2'=2,'grp_0'=4,'grp_1'=4] {'grp_0'}, use_global_device_ids=true, to_apply=%region_2.0 | all-reduce | flops 1536 | bytes 12288 | tf_op jit(solution)/shard_map/psum | solution.py:239
  140.1 13.0 %psum.31 = f32[12,1,128]{2,1,0:T(1,128)} all-reduce(f32[12,1,128]{2,1,0:T(1,128)} %psum.30), channel_id=1, replica_groups=mesh['blk_0'=2,'blk_1'=12,'blk_2'=2,'grp_0'=4,'grp_1'=4] {'grp_1'}, use_global_device_ids=true, to_apply=%region_3.0 | all-reduce | flops 1536 | bytes 12288 | tf_op jit(solution)/shard_map/psum | solution.py:239
  153.2 2.6 %shard_map.89 = f32[256,1152]{1,0:T(8,128)} custom-call(f32[2,1152]{1,0:T(2,128)S(1)} %broadcast_in_dim.12.numbers, bf16[256,1152]{1,0:T(8,128)(2,1)S(1)} %bitcast.14, bf16[48,2,16,384]{3,2,1,0:T(8,128)(2,1)S(1)} %all_to_all.20.received, f32[256,1152]{1,0:T(8,128)} %copy-done.3), custom_call_target="tpu_custom_call" | custom-call | flops 603979776 | bytes 4128768 | tf_op jit(solution)/shard_map/pallas_call | solution.py:225
  155.8 6.7 %all-to-all-done.1.received = bf16[48,2,16,384]{3,2,1,0:T(8,128)(2,1)S(1)} async-done(((bf16[48,2,16,384]{3,2,1,0:T(8,128)(2,1)}), bf16[48,2,16,384]{3,2,1,0:T(8,128)(2,1)S(1)}, u32[]{:S(2)}, u32[]{:S(2)}) %all-to-all-start.1) | async-done | bytes 1179680 | tf_op jit(solution)/shard_map/all_to_all | solution.py:222
  162.5 8.5 %all-to-all-start.3 = ((f32[12,1,128]{2,1,0:T(1,128)}), f32[12,1,128]{2,1,0:T(1,128)S(1)}, u32[]{:S(2)}, u32[]{:S(2)}) async-start(f32[12,1,128]{2,1,0:T(1,128)} %psum.31), calls=%async_computation.3 | async-start | bytes 12288 | tf_op jit(solution)/shard_map/all_to_all | solution.py:241
  171.0 2.6 %shard_map.90 = f32[256,1152]{1,0:T(8,128)} custom-call(f32[2,1152]{1,0:T(2,128)S(1)} %broadcast_in_dim.12.numbers, bf16[256,1152]{1,0:T(8,128)(2,1)S(1)} %bitcast.17, bf16[48,2,16,384]{3,2,1,0:T(8,128)(2,1)S(1)} %all-to-all-done.1.received, f32[256,1152]{1,0:T(8,128)} %copy-done.2), custom_call_target="tpu_custom_call" | custom-call | flops 603979776 | bytes 4128768 | tf_op jit(solution)/shard_map/pallas_call | solution.py:225
  173.7 7.4 %all-to-all-done.3 = f32[12,1,128]{2,1,0:T(1,128)S(1)} async-done(((f32[12,1,128]{2,1,0:T(1,128)}), f32[12,1,128]{2,1,0:T(1,128)S(1)}, u32[]{:S(2)}, u32[]{:S(2)}) %all-to-all-start.3) | async-done | bytes 6176 | tf_op jit(solution)/shard_map/all_to_all | solution.py:241
  181.1 0.6 slice_reduce_fusion
  (19 shorter events, 0.1 us)
Async XLA Ops:
  2.8 18.4 %copy-start.10 = (s32[1,1,256]{2,1,0:T(1,128)S(1)}, s32[1,1,256]{2,1,0:T(1,128)}, u32[]{:S(2)}) copy-start(s32[1,1,256]{2,1,0:T(1,128)} %param.8) | copy-start | bytes 3076
  2.8 19.3 %copy-start = (bf16[1,256,1152]{2,1,0:T(8,128)(2,1)S(1)}, bf16[1,256,1152]{2,1,0:T(8,128)(2,1)}, u32[]{:S(2)}) copy-start(bf16[1,256,1152]{2,1,0:T(8,128)(2,1)} %param.6) | copy-start | bytes 1769476
  2.8 19.3 %copy-start.1 = (bf16[1,256,1152]{2,1,0:T(8,128)(2,1)S(1)}, bf16[1,256,1152]{2,1,0:T(8,128)(2,1)}, u32[]{:S(2)}) copy-start(bf16[1,256,1152]{2,1,0:T(8,128)(2,1)} %param.7) | copy-start | bytes 1769476
  2.9 58.2 %all-to-all-start = ((bf16[48,2,16,384]{3,2,1,0:T(8,128)(2,1)}), bf16[48,2,16,384]{3,2,1,0:T(8,128)(2,1)S(1)}, u32[]{:S(2)}, u32[]{:S(2)}) async-start(bf16[48,2,16,384]{3,2,1,0:T(8,128)(2,1)} %shard_map.85), calls=%async_computation | async-start | bytes 2359296 | tf_op jit(solution)/shard_map/all_to_all | solution.py:202
  19.9 41.2 %copy-start.7 = (s32[2,48]{1,0:T(2,128)S(1)}, s32[2,48]{1,0:T(2,128)}, u32[]{:S(2)}) copy-start(s32[2,48]{1,0:T(2,128)} %partners.1) | copy-start | bytes 1156
  22.1 0.9 copy-start.5
  24.3 1.0 copy-start.2
  25.3 0.5 copy-start.8
  25.9 86.1 %copy-start.3 = (f32[256,1152]{1,0:T(8,128)}, f32[256,1152]{1,0:T(8,128)S(1)}, u32[]{:S(2)}) copy-start(f32[256,1152]{1,0:T(8,128)S(1)} %get-tuple-element.22.part) | copy-start | bytes 3538948
  61.8 50.2 %copy-start.4 = (bf16[48,2,16,384]{3,2,1,0:T(8,128)(2,1)}, bf16[48,2,16,384]{3,2,1,0:T(8,128)(2,1)S(1)}, u32[]{:S(2)}) copy-start(bf16[48,2,16,384]{3,2,1,0:T(8,128)(2,1)S(1)} %get-tuple-element.19) | copy-start | bytes 3538948
  112.0 9.4 %copy-start.9 = (f32[1,128]{1,0:T(1,128)S(1)}, f32[1,128]{1,0:T(1,128)}, u32[]{:S(2)}) copy-start(f32[1,128]{1,0:T(1,128)} %copy-done.8) | copy-start | bytes 1540
  112.0 50.5 %all-to-all-start.1 = ((bf16[48,2,16,384]{3,2,1,0:T(8,128)(2,1)}), bf16[48,2,16,384]{3,2,1,0:T(8,128)(2,1)S(1)}, u32[]{:S(2)}, u32[]{:S(2)}) async-start(bf16[48,2,16,384]{3,2,1,0:T(8,128)(2,1)} %copy-done.4), calls=%async_computation.1 | async-start | bytes 2359296 | tf_op jit(solution)/shard_map/all_to_all | solution.py:222
  122.3 0.6 copy-start.6
  162.5 18.6 %all-to-all-start.3 = ((f32[12,1,128]{2,1,0:T(1,128)}), f32[12,1,128]{2,1,0:T(1,128)S(1)}, u32[]{:S(2)}, u32[]{:S(2)}) async-start(f32[12,1,128]{2,1,0:T(1,128)} %psum.31), calls=%async_computation.3 | async-start | bytes 12288 | tf_op jit(solution)/shard_map/all_to_all | solution.py:241

commit v9 on v7

--- a/solution.py
+++ b/solution.py
@@ -122,9 +122,15 @@
 
 def loss_kernel(numbers, own_loss, images, received, loss):
     terms = jnp.zeros((ROWS, ROWS), jnp.float32)
-    for r in range(received.shape[1]):
-        logits = partner_logits(numbers, images, received, r)
-        terms += jnp.maximum(logits, 0.0) + jnp.log1p(jnp.exp(-jnp.abs(logits)))
+    rounds = received.shape[1]
+    for first in range(0, rounds, 2):
+        inner = None
+        for r in range(first, min(first + 2, rounds)):
+            logits = partner_logits(numbers, images, received, r)
+            terms += jnp.maximum(logits, 0.0)
+            e = jnp.exp(-jnp.abs(logits))
+            inner = e if inner is None else inner + e + inner * e
+        terms += jnp.log1p(inner)
     row = own_loss[...] + jnp.sum(terms)
     for place in range(loss.shape[0]):
         loss[place] = row

time: 184 us -> 184 us (level)
  no operation moved by 1% of the time
where the time goes in v9:
time: 184 us; the launch traced here: 181 us
  blocking collectives  98 us (53%)
  waiting for transfers between devices  42.3 us (23%)
  starting transfers between devices  21.6 us (12%)
  Pallas kernels  10.4 us (6%)
  between operations  3.85 us (2%)
  local copies, waits for them, and re-layouts  3.33 us (2%)
    all_to_all x1, blocking collectives, body(): their_texts = exchange(send_texts)  50.3 us
    all_to_all x1, waiting for transfers between devices, body(): exchange(packed)  35.2 us
    psum x4, blocking collectives, body(): loss = lax.psum(loss, axis)  29.4 us
    all_to_all x1, blocking collectives, body(): lax.all_to_all(loss, 'blk_1', split_axis=0, concat_axis=0, tiled=True)  18.4 us
    all_to_all x1, starting transfers between devices, body(): exchange(packed)  17 us
    all_to_all x1, waiting for transfers between devices, body(): their_images = exchange(send_images)  7.18 us
    pallas_call x2, Pallas kernels, gradient(): local_kernel(grad_kernel, grad, [VMEM, VMEM, VMEM, HBM], HBM, scratch, vm...  5.29 us
    all_to_all x1, starting transfers between devices, body(): their_images = exchange(send_images)  4.58 us
  transfers between devices with their start and end apart: 2, of which 2 were waited for; matrix products, arithmetic and copies ran while one was open for 1% of the time, Pallas kernels for 2%

profile of v9, /device:TPU:6, one launch (start us, length us, event | category | flops | bytes accessed | tf_op | source)
XLA Modules:
  0.0 180.9 jit_solution(5712543981135148125)
XLA Ops:
  0.6 2.2 %shard_map.85 = bf16[48,2,16,384]{3,2,1,0:T(8,128)(2,1)} custom-call(bf16[16,16,1152]{2,1,0:T(8,128)(2,1)} %bitcast.15, bf16[16,16,1152]{2,1,0:T(8,128)(2,1)} %bitcast.11), custom_call_target="tpu_custom_call" | custom-call | bytes 2359296 | tf_op jit(solution)/shard_map/pallas_call | solution.py:183
  2.8 0.0 copy-start.9
  2.9 17.0 %all-to-all-start = ((bf16[48,2,16,384]{3,2,1,0:T(8,128)(2,1)}), bf16[48,2,16,384]{3,2,1,0:T(8,128)(2,1)S(1)}, u32[]{:S(2)}, u32[]{:S(2)}) async-start(bf16[48,2,16,384]{3,2,1,0:T(8,128)(2,1)} %shard_map.85), calls=%async_computation | async-start | bytes 2359296 | tf_op jit(solution)/shard_map/all_to_all | solution.py:208
  21.2 0.8 copy.9.labels
  22.0 0.1 pad_maximum_fusion
  22.1 0.1 broadcast_in_dim.12.numbers
  22.1 0.9 copy-done.5
  23.0 1.3 shard_map.86
  24.3 1.0 copy-done.2
  25.3 0.5 copy-done.7
  25.9 35.2 %all-to-all-done.spread = bf16[48,2,16,384]{3,2,1,0:T(8,128)(2,1)S(1)} async-done(((bf16[48,2,16,384]{3,2,1,0:T(8,128)(2,1)}), bf16[48,2,16,384]{3,2,1,0:T(8,128)(2,1)S(1)}, u32[]{:S(2)}, u32[]{:S(2)}) %all-to-all-start) | async-done | bytes 1179680 | tf_op jit(solution)/shard_map/all_to_all | solution.py:208
  61.0 0.8 shard_map.87
  61.8 50.3 %all_to_all.20.received = bf16[48,2,16,384]{3,2,1,0:T(8,128)(2,1)S(1)} all-to-all(bf16[48,2,16,384]{3,2,1,0:T(8,128)(2,1)S(1)} %get-tuple-element.24), channel_id=1, replica_groups=mesh['blk_0'=2,'blk_1'=12,'blk_2'=2,'grp_0'=4,'grp_1'=4] {'blk_0','blk_1..., dimensions={0} | all-to-all | bytes 2359296 | tf_op jit(solution)/shard_map/all_to_all | solution.py:217
  112.1 0.9 shard_map.88
  113.1 18.4 %all_to_all.21 = f32[12,1,128]{2,1,0:T(1,128)} all-to-all(f32[12,1,128]{2,1,0:T(1,128)S(1)} %shard_map.88), channel_id=1, replica_groups=mesh['blk_0'=2,'blk_1'=12,'blk_2'=2,'grp_0'=4,'grp_1'=4] {'blk_1'}, dimensions={0} | all-to-all | bytes 12288 | tf_op jit(solution)/shard_map/all_to_all | solution.py:228
  131.4 4.6 %all-to-all-start.3 = ((bf16[48,2,16,384]{3,2,1,0:T(8,128)(2,1)}), bf16[48,2,16,384]{3,2,1,0:T(8,128)(2,1)S(1)}, u32[]{:S(2)}, u32[]{:S(2)}) async-start(bf16[48,2,16,384]{3,2,1,0:T(8,128)(2,1)} %copy-done.4), calls=%async_computation.3 | async-start | bytes 2359296 | tf_op jit(solution)/shard_map/all_to_all | solution.py:230
  136.0 1.3 slice_reduce_fusion
  137.3 3.1 %psum.28 = f32[]{:T(128)} all-reduce(f32[]{:T(128)} %slice_reduce_fusion), channel_id=1, replica_groups=mesh['blk_0'=2,'blk_1'=12,'blk_2'=2,'grp_0'=4,'grp_1'=4] {'blk_2'}, use_global_device_ids=true, to_apply=%region_1.0 | all-reduce | flops 1 | bytes 8 | tf_op jit(solution)/shard_map/psum | solution.py:248
  140.4 5.6 %psum.29 = f32[]{:T(128)} all-reduce(f32[]{:T(128)} %psum.28), channel_id=1, replica_groups=mesh['blk_0'=2,'blk_1'=12,'blk_2'=2,'grp_0'=4,'grp_1'=4] {'blk_0'}, use_global_device_ids=true, to_apply=%region_2.0 | all-reduce | flops 1 | bytes 8 | tf_op jit(solution)/shard_map/psum | solution.py:248
  146.0 8.1 %psum.30 = f32[]{:T(128)} all-reduce(f32[]{:T(128)} %psum.29), channel_id=1, replica_groups=mesh['blk_0'=2,'blk_1'=12,'blk_2'=2,'grp_0'=4,'grp_1'=4] {'grp_0'}, use_global_device_ids=true, to_apply=%region_3.0 | all-reduce | flops 1 | bytes 8 | tf_op jit(solution)/shard_map/psum | solution.py:248
  154.0 12.6 %psum.31 = f32[]{:T(128)} all-reduce(f32[]{:T(128)} %psum.30), channel_id=1, replica_groups=mesh['blk_0'=2,'blk_1'=12,'blk_2'=2,'grp_0'=4,'grp_1'=4] {'grp_1'}, use_global_device_ids=true, to_apply=%region_4.0 | all-reduce | flops 1 | bytes 8 | tf_op jit(solution)/shard_map/psum | solution.py:248
  167.3 2.6 %shard_map.89 = f32[256,1152]{1,0:T(8,128)} custom-call(f32[2,1152]{1,0:T(2,128)S(1)} %broadcast_in_dim.12.numbers, bf16[256,1152]{1,0:T(8,128)(2,1)S(1)} %bitcast.14, bf16[48,2,16,384]{3,2,1,0:T(8,128)(2,1)S(1)} %all_to_all.20.received, f32[256,1152]{1,0:T(8,128)} %copy-done.3), custom_call_target="tpu_custom_call" | custom-call | flops 603979776 | bytes 4128768 | tf_op jit(solution)/shard_map/pallas_call | solution.py:233
  170.0 7.2 %all-to-all-done.3.received = bf16[48,2,16,384]{3,2,1,0:T(8,128)(2,1)S(1)} async-done(((bf16[48,2,16,384]{3,2,1,0:T(8,128)(2,1)}), bf16[48,2,16,384]{3,2,1,0:T(8,128)(2,1)S(1)}, u32[]{:S(2)}, u32[]{:S(2)}) %all-to-all-start.3) | async-done | bytes 1179680 | tf_op jit(solution)/shard_map/all_to_all | solution.py:230
  177.2 2.6 %shard_map.90 = f32[256,1152]{1,0:T(8,128)} custom-call(f32[2,1152]{1,0:T(2,128)S(1)} %broadcast_in_dim.12.numbers, bf16[256,1152]{1,0:T(8,128)(2,1)S(1)} %bitcast.17, bf16[48,2,16,384]{3,2,1,0:T(8,128)(2,1)S(1)} %all-to-all-done.3.received, f32[256,1152]{1,0:T(8,128)} %copy-done.2), custom_call_target="tpu_custom_call" | custom-call | flops 603979776 | bytes 4128768 | tf_op jit(solution)/shard_map/pallas_call | solution.py:233
  (16 shorter events, 0.0 us)
Async XLA Ops:
  2.8 18.4 %copy-start.9 = (s32[1,1,256]{2,1,0:T(1,128)S(1)}, s32[1,1,256]{2,1,0:T(1,128)}, u32[]{:S(2)}) copy-start(s32[1,1,256]{2,1,0:T(1,128)} %param.8) | copy-start | bytes 3076
  2.8 19.3 %copy-start = (bf16[1,256,1152]{2,1,0:T(8,128)(2,1)S(1)}, bf16[1,256,1152]{2,1,0:T(8,128)(2,1)}, u32[]{:S(2)}) copy-start(bf16[1,256,1152]{2,1,0:T(8,128)(2,1)} %param.6) | copy-start | bytes 1769476
  2.8 19.3 %copy-start.1 = (bf16[1,256,1152]{2,1,0:T(8,128)(2,1)S(1)}, bf16[1,256,1152]{2,1,0:T(8,128)(2,1)}, u32[]{:S(2)}) copy-start(bf16[1,256,1152]{2,1,0:T(8,128)(2,1)} %param.7) | copy-start | bytes 1769476
  2.9 58.2 %all-to-all-start = ((bf16[48,2,16,384]{3,2,1,0:T(8,128)(2,1)}), bf16[48,2,16,384]{3,2,1,0:T(8,128)(2,1)S(1)}, u32[]{:S(2)}, u32[]{:S(2)}) async-start(bf16[48,2,16,384]{3,2,1,0:T(8,128)(2,1)} %shard_map.85), calls=%async_computation | async-start | bytes 2359296 | tf_op jit(solution)/shard_map/all_to_all | solution.py:208
  19.9 41.2 %copy-start.6 = (s32[2,48]{1,0:T(2,128)S(1)}, s32[2,48]{1,0:T(2,128)}, u32[]{:S(2)}) copy-start(s32[2,48]{1,0:T(2,128)} %partners.1) | copy-start | bytes 1156
  22.1 0.9 copy-start.5
  24.3 1.0 copy-start.2
  25.3 0.5 copy-start.7
  25.8 86.3 %copy-start.3 = (f32[256,1152]{1,0:T(8,128)}, f32[256,1152]{1,0:T(8,128)S(1)}, u32[]{:S(2)}) copy-start(f32[256,1152]{1,0:T(8,128)S(1)} %get-tuple-element.28.part) | copy-start | bytes 3538948
  61.8 50.3 %copy-start.4 = (bf16[48,2,16,384]{3,2,1,0:T(8,128)(2,1)}, bf16[48,2,16,384]{3,2,1,0:T(8,128)(2,1)S(1)}, u32[]{:S(2)}) copy-start(bf16[48,2,16,384]{3,2,1,0:T(8,128)(2,1)S(1)} %get-tuple-element.25) | copy-start | bytes 3538948
  61.8 50.3 %copy-start.8 = (f32[1,128]{1,0:T(1,128)S(1)}, f32[1,128]{1,0:T(1,128)}, u32[]{:S(2)}) copy-start(f32[1,128]{1,0:T(1,128)} %copy-done.7) | copy-start | bytes 1540
  131.4 45.7 %all-to-all-start.3 = ((bf16[48,2,16,384]{3,2,1,0:T(8,128)(2,1)}), bf16[48,2,16,384]{3,2,1,0:T(8,128)(2,1)S(1)}, u32[]{:S(2)}, u32[]{:S(2)}) async-start(bf16[48,2,16,384]{3,2,1,0:T(8,128)(2,1)} %copy-done.4), calls=%async_computation.3 | async-start | bytes 2359296 | tf_op jit(solution)/shard_map/all_to_all | solution.py:230
